TPU v7x, 1024 devices: a whole 4x8x16 slice. The times are simulated.
1024 devices in a mesh: gx: 16 (over y, core), gy: 4 (over z_lo), mz: 16 (over z_hi, x).
Axes of the slice: x: 4, y: 8, z: 16 (z_hi: 4, z_lo: 4; z = z_hi * 4 + z_lo), core: 2. Of those that a mesh axis runs over, the one named last changes fastest.
Arguments:
- spectra: bfloat16 [128, 32, 832, 128], P('gx', 'gy', 'mz'), may hold values from 1 to 100
- block_ids: int32 [16, 4, 832], P('gx', 'gy', 'mz'), may hold values from 0 to 97, as said below
- counts: int32 [16, 4, 16], P('gx', 'gy', 'mz'), may hold values from 6 to 52, as said below
- loadings: float32 [128, 32, 64], P('gx', 'gy'), may hold values from 0.15 to 1.5
- components: float32 [64, 200704], P(None, 'mz'), may hold values from 0.15 to 1.5
Outputs:
- w_next: float32 [128, 32, 64], P('gx', 'gy')
- h_next: float32 [64, 200704], P(('gx', 'gy'), 'mz')
Inputs may be any that keep to these rules, and one draw needn't show every extreme that they name: `block_ids`: the 52 numbers of one tile and slab are distinct; the first counts of them are the occupied blocks, the others are unused. `counts`: some tile and slab has exactly 52 occupied slots.
All inputs are finite; a program needn't handle non-finite values.
Results may differ from a plain program's by a relative error of at most 0.0003.
Values may be sent and summed in bfloat16 or wider, within the bound.
No kernel may reach another device: no remote copies, remote signals or barrier semaphores. Data moves between devices by JAX's collectives and lax.ppermute only.
A program may use at most 32 MiB of HBM per device.

v0:
```python
import jax
import jax.numpy as jnp
from jax import lax
from jax.sharding import PartitionSpec as P

tv_edge = 0.1
tv_share = 0.1


def padded_2(cells, sides, width):
    for axis, dim in sides:
        count = lax.axis_size(axis)
        ends = count - 1
        head = lax.slice_in_dim(cells, 0, width, axis=dim)
        tail = lax.slice_in_dim(cells, cells.shape[dim] - width, cells.shape[dim], axis=dim)
        cells = jnp.concatenate(
            [
                lax.ppermute(tail, axis, [(i, (i + 1) % count) for i in range(ends)]),
                cells,
                lax.ppermute(head, axis, [((i + 1) % count, i) for i in range(ends)]),
            ],
            axis=dim,
        )
    return cells


def smoothing(padded):
    centre = padded[1:-1, 1:-1]
    smooth_num = jnp.zeros_like(centre)
    smooth_den = jnp.zeros_like(centre)
    for beside in (padded[2:, 1:-1], padded[:-2, 1:-1], padded[1:-1, 2:], padded[1:-1, :-2]):
        edge_weight = 1.0 / (jnp.abs(centre - beside) + tv_edge)
        smooth_num = smooth_num + edge_weight * beside
        smooth_den = smooth_den + edge_weight * centre
    return (smooth_num, smooth_den)


def local(spectra, block_ids, counts, loadings, components):
    tile_x, tile_y, slot_count, lane_width = spectra.shape
    comps = loadings.shape[2]
    slab_bins = components.shape[1]
    blocks = slab_bins // lane_width
    pixels = spectra.reshape(tile_x * tile_y, slot_count * lane_width)
    w_low = loadings.reshape(tile_x * tile_y, comps).astype(jnp.bfloat16)
    slot_ids = block_ids.reshape(slot_count)
    is_live = jnp.arange(slot_count, dtype=jnp.int32) < counts.reshape(())
    block_range = jnp.arange(blocks, dtype=jnp.int32)
    placing = jnp.logical_and(slot_ids[:, None] == block_range[None, :], is_live[:, None])
    partial_value = lax.dot_general(
        w_low, pixels, (((0,), (0,)), ((), ())), preferred_element_type=jnp.float32
    )
    gram_term = lax.dot_general(
        w_low, w_low, (((0,), (0,)), ((), ())), preferred_element_type=jnp.float32
    )
    groups = lax.axis_size(("gx", "gy"))
    row_count = comps // groups
    first_row = lax.axis_index(("gx", "gy")) * row_count
    gram_full = lax.psum(gram_term, ("gx", "gy"))
    gram_rows = lax.dynamic_slice_in_dim(gram_full, first_row, row_count, 0)
    slot_range = jnp.arange(slot_count, dtype=jnp.int32)
    slot_of_block = jnp.sum(jnp.where(placing, slot_range[:, None], 0), axis=0)
    block_found = jnp.any(placing, axis=0)
    taken = jnp.take(partial_value.reshape(comps, slot_count, lane_width), slot_of_block, axis=1)
    num_term = jnp.where(block_found[None, :, None], taken, 0.0).reshape(comps, slab_bins)
    reduced = lax.psum_scatter(num_term, ("gx", "gy"), scatter_dimension=0, tiled=True)
    own_rows = lax.dynamic_slice_in_dim(components, first_row, row_count, 0)
    denominator = jnp.dot(gram_rows, components, precision=lax.Precision.HIGHEST)
    h_next = own_rows * reduced / denominator
    h_low = h_next.astype(jnp.bfloat16)
    h_whole = lax.all_gather(h_low, ("gx", "gy"), axis=0, tiled=True)
    chosen = jnp.take(h_whole.reshape(comps, blocks, lane_width), slot_ids, axis=1)
    picked = jnp.where(is_live[None, :, None], chosen, jnp.zeros((), jnp.bfloat16))
    cross_term = lax.dot_general(
        pixels,
        picked.reshape(comps, slot_count * lane_width),
        (((1,), (1,)), ((), ())),
        preferred_element_type=jnp.float32,
    )
    spec_term = lax.dot_general(
        h_whole, h_whole, (((1,), (1,)), ((), ())), preferred_element_type=jnp.float32
    )
    cross_sum, spec_gram = lax.psum((cross_term, spec_term), "mz")
    padded = padded_2(loadings, (("gx", 0), ("gy", 1)), 1)
    smooth_num, smooth_den = smoothing(padded)
    tv_strength = tv_share * slab_bins * lax.axis_size("mz")
    fitted = jnp.dot(
        loadings.reshape(tile_x * tile_y, comps), spec_gram, precision=lax.Precision.HIGHEST
    ).reshape(tile_x, tile_y, comps)
    w_next = (
        loadings
        * (cross_sum.reshape(tile_x, tile_y, comps) + tv_strength * smooth_num)
        / (fitted + tv_strength * smooth_den)
    )
    return (w_next, h_next)


def solution(mesh):
    in_specs = (
        P("gx", "gy", "mz", None),
        P("gx", "gy", "mz"),
        P("gx", "gy", "mz"),
        P("gx", "gy", None),
        P(None, "mz"),
    )
    out_specs = (P("gx", "gy", None), P(("gx", "gy"), "mz"))
    return jax.shard_map(local, mesh=mesh, in_specs=in_specs, out_specs=out_specs, check_vma=False)
```

profile of v0, /device:TPU:24, one launch (start us, length us, event | category | flops | bytes accessed | tf_op | source)
XLA Modules:
  0.0 918.5 jit_solution(16534480873528003570)
XLA Ops:
  7.2 0.0 copy-start
  7.2 0.0 all-reduce.4.cloned.1.call-start
  8.0 0.8 select_reduce_fusion
  8.7 0.8 fusion.29
  9.5 0.7 fusion.34
  10.1 0.1 broadcast_bitcast_fusion
  10.3 0.0 copy-done
  10.3 1.2 fusion.6
  11.4 2.5 gather_fusion
  13.9 3.9 fusion
  17.8 0.0 copy-start.1
  17.8 0.0 copy-start.3
  17.8 0.0 all-reduce.4.cloned.1.call-update
  17.8 0.0 all-gather.3.cloned.1.call-start
  17.9 1.3 dynamic-slice
  19.2 0.0 copy-done.1
  19.2 0.2 convolution_bitcast_fusion.2
  19.4 260.9 %psum.21 = f32[64,64]{1,0:T(8,128)S(1)} all-reduce(f32[64,64]{1,0:T(8,128)S(1)} %convolution_bitcast_fusion.2), channel_id=1, replica_groups=mesh['gx'=16,'gy'=4,'mz'=16] {'gx','gy'}, use_global_device_ids=true, to_apply=%region_3.4 | all-reduce | flops 4096 | bytes 32768 | tf_op jit(solution)/shard_map/psum | solution.py:58
  280.3 299.4 %all-reduce.4.cloned.1.call-done = f32[64,12544]{1,0:T(8,128)} async-done(((f32[64,12544]{1,0:T(8,128)}), f32[64,12544]{1,0:T(8,128)}) %all-reduce.4.cloned.1.call-update) | async-done | bytes 3211280
  579.7 4.3 convolution_divide_fusion
  584.0 0.0 copy-start.2
  584.0 0.6 convert_bitcast_fusion
  584.7 0.0 all-gather.3.cloned.1.call-update
  584.7 7.3 collective-permute-start.1
  592.0 1.9 collective-permute-start
  593.9 0.0 copy-done.3
  594.0 0.0 collective-permute-done.1
  594.0 7.5 collective-permute-done
  601.5 1.3 collective-permute-start.2
  602.8 4.7 collective-permute-start.3
  607.5 183.8 %all-gather.3.cloned.1.call-done = bf16[64,1,12544]{2,1,0:T(2,128)(2,1)} async-done(((bf16[1,1,12544]{2,1,0:T(2,128)(2,1)}), bf16[64,1,12544]{2,1,0:T(2,128)(2,1)}) %all-gather.3.cloned.1.call-update) | async-done | bytes 1605648 | tf_op jit(solution)/shard_map/all_gather | solution.py:70
  791.3 10.8 %reduce = bf16[64,12544]{1,0:T(8,128)(2,1)S(1)} reduce(bf16[64,1,12544]{2,1,0:T(2,128)(2,1)} %all-gather.3.cloned.1.call-done, bf16[]{:T(256)} %constant.67), dimensions={1}, to_apply=%all-gather.reduce_sub_computation | reduce | bytes 3211266 | tf_op jit(solution)/shard_map/all_gather | solution.py:70
  802.1 1.6 copy_bitcast_fusion
  803.7 0.0 copy-done.2
  803.7 2.1 gather_fusion.1
  805.9 0.4 convolution_bitcast_fusion.1
  806.3 0.1 copy.29
  806.4 3.5 fusion.1
  809.9 100.8 %all-reduce.1 = (f32[8,8,64]{2,1,0:T(8,128)S(1)}, f32[64,64]{1,0:T(8,128)S(1)}) all-reduce(f32[8,8,64]{2,1,0:T(8,128)S(1)} %bitcast.80, f32[64,64]{1,0:T(8,128)S(1)} %fusion.1), channel_id=1, replica_groups=mesh['gx'=16,'gy'=4,'mz'=16] {'mz'}, use_global_device_ids=true, to_apply=%region_4.5 | all-reduce | flops 8192 | bytes 65536 | tf_op jit(solution)/shard_map/psum | solution.py:82
  910.6 0.2 convolution_bitcast_fusion
  910.9 0.1 copy.30
  910.9 0.0 collective-permute-done.2
  911.0 0.0 collective-permute-done.3
  911.0 0.7 fusion.18
  (10 shorter events, 0.1 us)
Async XLA Ops:
  7.2 3.1 copy-start
  7.2 572.5 %all-reduce.4.cloned.1.call-start = ((), (), s32[]{:S(2)}) async-start(), calls=%async_computation.1 | async-start | bytes 6422528
  17.8 1.4 copy-start.1
  17.8 576.1 %copy-start.3 = (s32[1,1,52]{2,1,0:T(1,128)S(1)}, s32[1,1,52]{2,1,0:T(1,128)}, u32[]{:S(2)}) copy-start(s32[1,1,52]{2,1,0:T(1,128)} %param.6) | copy-start | bytes 628
  17.8 773.5 %all-gather.3.cloned.1.call-start = ((), (), s32[]{:S(2)}) async-start(), calls=%async_computation | async-start | bytes 3261440 | tf_op jit(solution)/shard_map/all_gather | solution.py:70
  584.0 219.7 %copy-start.2 = (f32[1,12544]{1,0:T(1,128)}, f32[1,12544]{1,0:T(1,128)S(1)}, u32[]{:S(2)}) copy-start(f32[1,12544]{1,0:T(1,128)S(1)} %convolution_divide_fusion) | copy-start | bytes 150532
  584.7 9.2 %collective-permute-start.1 = (f32[1,8,64]{2,1,0:T(8,128)S(1)}, f32[1,8,64]{2,1,0:T(8,128)S(1)}, u32[]{:S(2)}, u32[]{:S(2)}) collective-permute-start(f32[1,8,64]{2,1,0:T(8,128)S(1)} %get-tuple-element.7), channel_id=1, source_target_pairs={{0,64},{64,128},{128,192},{192,256},{256,320},{320,384},{384,448},... | collective-permute-start | bytes 6152 | tf_op jit(solution)/shard_map/ppermute | solution.py:18
  592.0 9.4 %collective-permute-start = (f32[1,8,64]{2,1,0:T(8,128)S(1)}, f32[1,8,64]{2,1,0:T(8,128)S(1)}, u32[]{:S(2)}, u32[]{:S(2)}) collective-permute-start(f32[1,8,64]{2,1,0:T(8,128)S(1)} %get-tuple-element.6), channel_id=1, source_target_pairs={{64,0},{128,64},{192,128},{256,192},{320,256},{384,320},{448,384},... | collective-permute-start | bytes 6152 | tf_op jit(solution)/shard_map/ppermute | solution.py:20
  601.5 309.5 %collective-permute-start.2 = (f32[10,1,64]{2,1,0:T(1,128)S(1)}, f32[10,1,64]{2,1,0:T(1,128)S(1)}, u32[]{:S(2)}, u32[]{:S(2)}) collective-permute-start(f32[10,1,64]{2,1,0:T(1,128)S(1)} %get-tuple-element.4), channel_id=1, source_target_pairs={{16,0},{32,16},{48,32},{17,1},{33,17},{49,33},{18,2},{34,18},{50,3... | collective-permute-start | bytes 7688 | tf_op jit(solution)/shard_map/ppermute | solution.py:20
  602.8 308.2 %collective-permute-start.3 = (f32[10,1,64]{2,1,0:T(1,128)S(1)}, f32[10,1,64]{2,1,0:T(1,128)S(1)}, u32[]{:S(2)}, u32[]{:S(2)}) collective-permute-start(f32[10,1,64]{2,1,0:T(1,128)S(1)} %get-tuple-element.5), channel_id=1, source_target_pairs={{0,16},{16,32},{32,48},{1,17},{17,33},{33,49},{2,18},{18,34},{34,5... | collective-permute-start | bytes 7688 | tf_op jit(solution)/shard_map/ppermute | solution.py:18
Sparse Core Ops, SparseCore 0:
  18.0 561.6 all-reduce.3
  584.8 206.4 all-gather.2
where the time goes:
time: 919 us; the launch traced here: 918 us
  waiting for transfers between devices  491 us (53%)
  blocking collectives  362 us (39%)
  other arithmetic  18.2 us (2%)
  starting transfers between devices  15.3 us (2%)
  between operations  15 us (2%)
  matrix products  9.83 us (1%)
    unnamed x3, waiting for transfers between devices  299 us
    psum x1, blocking collectives, local(): gram_full = lax.psum(gram_term, ('gx', 'gy'))  261 us
    all_gather x1, waiting for transfers between devices, local(): h_whole = lax.all_gather(h_low, ('gx', 'gy'), axis=0, tiled=True)  184 us
    psum x1, blocking collectives, local(): cross_sum, spec_gram = lax.psum((cross_term, spec_term), 'mz')  101 us
  transfers between devices with their start and end apart: 6, of which 3 were waited for; matrix products, arithmetic and copies ran while one was open for 2% of the time, Pallas kernels for 0%

commit v1 on v0

v1 whole, which is shorter than its diff:
```python
import functools
import jax
import jax.numpy as jnp
from jax import lax
from jax.experimental import pallas as pl
from jax.experimental.pallas import tpu as pltpu
from jax.sharding import Mesh, PartitionSpec as P

tv_edge = 0.1
tv_share = 0.1
LANE = 128
VMEM_LIMIT = 48 * 1024 * 1024
F32 = jnp.float32
BF16 = jnp.bfloat16


def params():
    return pltpu.CompilerParams(vmem_limit_bytes=VMEM_LIMIT)


def vmem():
    return pl.BlockSpec(memory_space=pltpu.VMEM)


def smem():
    return pl.BlockSpec(memory_space=pltpu.SMEM)


def iota(shape, dim):
    return lax.broadcasted_iota(jnp.int32, shape, dim)


def nt(a, b):
    return lax.dot_general(a, b, (((1,), (1,)), ((), ())), preferred_element_type=F32)


def numer_kernel(where_ref, ids_ref, count_ref, x_ref, w_ref, out_ref, dense_ref, wide_ref):
    tile, slots, lane = x_ref.shape
    pitch = wide_ref.shape[0] // tile
    half_blocks = dense_ref.shape[0]
    comps = w_ref.shape[1]
    rows = out_ref.shape[0]
    me = where_ref[0]
    last = rows // 8 - 1

    w = w_ref[...]
    w_low = w.astype(BF16)
    w_two = jnp.concatenate([w_low, w_low], axis=0)
    row = iota((rows, comps), 0)
    pick = jnp.where(iota((rows, comps), 1) == 4 * (row // 8) + row % 4, 1.0, 0.0).astype(BF16)
    spread = nt(pick, w_two)
    row = iota((rows, 2 * tile), 0)
    same_half = (row // 4) % 2 == iota((rows, 2 * tile), 1) // tile
    left = jnp.where(same_half, spread, 0.0).astype(BF16)

    dense_ref[...] = jnp.zeros_like(dense_ref)
    for p in range(tile):
        wide_ref[p * pitch : p * pitch + slots, :] = x_ref[p].astype(F32)

    def place(s, carry):
        block = ids_ref[s]
        high = block // half_blocks
        rows_of_slot = wide_ref[pl.ds(s, tile, stride=pitch), :].astype(BF16)
        dense_ref[block - high * half_blocks, pl.ds(pl.multiple_of(high * tile, tile), tile), :] = rows_of_slot
        return carry

    lax.fori_loop(0, count_ref[0], place, 0)

    for j in range(half_blocks):
        out_ref[:, j * lane : (j + 1) * lane] = jnp.dot(left, dense_ref[j], preferred_element_type=F32)

    base = half_blocks * lane
    out_ref[:, base : base + 3 * lane] = jnp.zeros((rows, 3 * lane), F32)
    out_ref[:, base : base + comps] = jnp.dot(left, w_two, preferred_element_type=F32)

    pair = jnp.concatenate([w, w], axis=1)
    first = iota((8, lane), 1) < comps

    @pl.when(me < last)
    def _():
        at = pl.ds(pl.multiple_of(8 * (me + 1), 8), 8)
        out_ref[at, base + lane : base + 2 * lane] += jnp.where(first, pair[tile - 8 :], 0.0)

    @pl.when(me > 0)
    def _():
        at = pl.ds(pl.multiple_of(8 * (me - 1), 8), 8)
        out_ref[at, base + lane : base + 2 * lane] += jnp.where(first, 0.0, pair[:8])

    heads = jnp.concatenate([pair[8 * i : 8 * i + 1] for i in range(8)], axis=0)
    tails = jnp.concatenate([pair[8 * i + 7 : 8 * i + 8] for i in range(8)], axis=0)
    out_ref[pl.ds(pl.multiple_of(8 * me, 8), 8), base + 2 * lane :] = jnp.where(first, heads, tails)


def spectra_kernel(tv_strength, where_ref, parts_ref, comps_ref, w_ref, h_low_ref, h_ref, tv_num_ref, tv_den_ref):
    lane = LANE
    half_blocks = h_low_ref.shape[1] // lane
    base = half_blocks * lane
    comps = comps_ref.shape[0]
    me, side = where_ref[0], where_ref[1]
    sides = parts_ref.shape[0]

    def total(start):
        block = parts_ref[0, :, pl.ds(start, lane)]
        for i in range(1, sides):
            block = block + parts_ref[i, :, pl.ds(start, lane)]
        return block

    gram = jnp.transpose(total(base))[:comps, :]
    weights = [jnp.broadcast_to(gram[:, i : i + 1], (comps, lane)) for i in range(4)]
    odd = me % 2
    own_at = pl.ds(pl.multiple_of(8 * (me // 2), 8), 8)
    top = iota((8, lane), 0) < 4

    def block_step(j, carry):
        numer = total(pl.multiple_of(j * lane, lane))
        denominators = []
        own = []
        for half in range(2):
            at = pl.ds(pl.multiple_of((half * half_blocks + j) * lane, lane), lane)
            block = comps_ref[:, at]
            for i in range(4):
                denominators.append(jnp.sum(block * weights[i], axis=0, keepdims=True))
            own.append(comps_ref[own_at, at])
        denominator = jnp.concatenate(denominators, axis=0)
        own_rows = jnp.where(top, pltpu.roll(own[0], 4 * odd, 0), pltpu.roll(own[1], 4 * (1 - odd), 0))
        h = own_rows * numer / denominator
        h_low_ref[:, pl.ds(pl.multiple_of(j * lane, lane), lane)] = h.astype(BF16)
        turned = pltpu.roll(h, lax.rem(8 - side, 8), 0)
        h_ref[:, pl.ds(pl.multiple_of(j * lane, lane), lane)] = turned[0:1]
        h_ref[:, pl.ds(pl.multiple_of((half_blocks + j) * lane, lane), lane)] = turned[4:5]
        return carry

    lax.fori_loop(0, half_blocks, block_step, 0)

    rim = parts_ref[side, :, base + lane : base + 2 * lane]
    above, below = rim[:, :comps], rim[:, comps:]
    before = parts_ref[jnp.maximum(side - 1, 0), :, base + 2 * lane :][:, comps:]
    before = jnp.where(side > 0, before, 0.0)
    after = parts_ref[jnp.minimum(side + 1, sides - 1), :, base + 2 * lane :][:, :comps]
    after = jnp.where(side < sides - 1, after, 0.0)
    spot = iota((8, comps), 0)
    rows = [w_ref[8 * i : 8 * i + 8, :] for i in range(8)]
    for i in range(8):
        centre = rows[i]
        beside = (
            rows[i + 1] if i < 7 else below,
            rows[i - 1] if i > 0 else above,
            jnp.where(spot == 7, after[i : i + 1], pltpu.roll(centre, 7, 0)),
            jnp.where(spot == 0, before[i : i + 1], pltpu.roll(centre, 1, 0)),
        )
        num = jnp.zeros_like(centre)
        den = jnp.zeros_like(centre)
        for q in beside:
            edge_weight = 1.0 / (jnp.abs(centre - q) + tv_edge)
            num = num + edge_weight * q
            den = den + edge_weight * centre
        tv_num_ref[8 * i : 8 * i + 8, :] = tv_strength * num
        tv_den_ref[8 * i : 8 * i + 8, :] = tv_strength * den


def project_kernel(h_ref, dense_ref, out_ref):
    half_blocks, two_tiles, lane = dense_ref.shape
    rows = h_ref.shape[0]
    copies, tile, _ = out_ref.shape
    comps = rows // 2
    cross = jnp.zeros((two_tiles, rows), F32)
    spec = jnp.zeros((rows, rows), F32)
    for j in range(half_blocks):
        block = h_ref[:, j * lane : (j + 1) * lane]
        cross = cross + nt(dense_ref[j], block)
        spec = spec + nt(block, block)
    row, col = iota((two_tiles, rows), 0), iota((two_tiles, rows), 1)
    cross = jnp.where(row // tile == (col // 4) % 2, cross, 0.0)
    cross = cross[:tile] + cross[tile:]
    row, col = iota((rows, rows), 0), iota((rows, rows), 1)
    spec = jnp.where((row // 4) % 2 == (col // 4) % 2, spec, 0.0)
    name = 4 * (row // 8) + row % 4
    to_low = jnp.where(col == name, 1.0, 0.0)
    to_high = jnp.where(col == name + comps, 1.0, 0.0)
    spec = lax.dot_general(
        to_low, spec, (((0,), (0,)), ((), ())), preferred_element_type=F32, precision=lax.Precision.HIGHEST
    )[:comps]
    both = jnp.dot(cross, to_low, preferred_element_type=F32, precision=lax.Precision.HIGHEST) + jnp.dot(
        spec, to_high, preferred_element_type=F32, precision=lax.Precision.HIGHEST
    )
    for i in range(copies):
        out_ref[i] = both


def sum_kernel(parts_ref, out_ref):
    block = parts_ref[0]
    for i in range(1, parts_ref.shape[0]):
        block = block + parts_ref[i]
    out_ref[...] = block


def loadings_kernel(parts_ref, w_ref, tv_num_ref, tv_den_ref, out_ref):
    comps = w_ref.shape[1]
    block = parts_ref[0]
    for i in range(1, parts_ref.shape[0]):
        block = block + parts_ref[i]
    w = w_ref[...]
    fitted = jnp.dot(w, block, preferred_element_type=F32, precision=lax.Precision.HIGHEST)
    fitted = pltpu.roll(fitted, comps, 1)[:, :comps]
    out_ref[...] = w * (block[:, :comps] + tv_num_ref[...]) / (fitted + tv_den_ref[...])


def local(spectra, block_ids, counts, loadings, components):
    tile_x, tile_y, slot_count, lane = spectra.shape
    tile = tile_x * tile_y
    comps = loadings.shape[2]
    slab_bins = components.shape[1]
    half_blocks = slab_bins // lane // 2
    half_bins = half_blocks * lane
    rows = 2 * comps
    width = half_bins + 3 * lane
    here = jnp.stack([lax.axis_index("gx"), lax.axis_index("gy")]).astype(jnp.int32)
    pixels = spectra.reshape(tile, slot_count, lane)
    w = loadings.reshape(tile, comps)
    pitch = -(-slot_count // 8) * 8

    num_term, dense = pl.pallas_call(
        numer_kernel,
        out_shape=(
            jax.ShapeDtypeStruct((rows, width), F32),
            jax.ShapeDtypeStruct((half_blocks, 2 * tile, lane), BF16),
        ),
        in_specs=[smem(), smem(), smem(), vmem(), vmem()],
        out_specs=(vmem(), vmem()),
        scratch_shapes=[pltpu.VMEM((tile * pitch, lane), F32)],
        compiler_params=params(),
        name="numer",
    )(here, block_ids.reshape(slot_count), counts.reshape(1), pixels, w)

    reduced = lax.psum_scatter(num_term, "gx", scatter_dimension=0, tiled=True)
    parts = lax.all_gather(reduced, "gy", axis=0)

    tv_strength = tv_share * slab_bins * lax.axis_size(("w", "x"))
    h_low, h_next, tv_num, tv_den = pl.pallas_call(
        functools.partial(spectra_kernel, tv_strength),
        out_shape=(
            jax.ShapeDtypeStruct((8, half_bins), BF16),
            jax.ShapeDtypeStruct((1, slab_bins), F32),
            jax.ShapeDtypeStruct((tile, comps), F32),
            jax.ShapeDtypeStruct((tile, comps), F32),
        ),
        in_specs=[smem(), vmem(), vmem(), vmem()],
        out_specs=(vmem(),) * 4,
        compiler_params=params(),
        name="spectra",
    )(here, parts, components, w)

    h_whole = lax.all_gather(h_low, "gx", axis=0, tiled=True)

    copies = lax.axis_size("x")
    both = pl.pallas_call(
        project_kernel,
        out_shape=jax.ShapeDtypeStruct((copies, tile, 2 * comps), F32),
        in_specs=[vmem(), vmem()],
        out_specs=vmem(),
        compiler_params=params(),
        name="project",
    )(h_whole, dense)

    both = lax.all_to_all(both, "x", 0, 0, tiled=True)
    both = pl.pallas_call(
        sum_kernel,
        out_shape=jax.ShapeDtypeStruct((tile, 2 * comps), F32),
        in_specs=[vmem()],
        out_specs=vmem(),
        compiler_params=params(),
        name="sum",
    )(both)
    both = lax.all_gather(both, "w", axis=0)
    w_next = pl.pallas_call(
        loadings_kernel,
        out_shape=jax.ShapeDtypeStruct((tile, comps), F32),
        in_specs=[vmem()] * 4,
        out_specs=vmem(),
        compiler_params=params(),
        name="loadings",
    )(both, w, tv_num, tv_den)
    return (w_next.reshape(tile_x, tile_y, comps), h_next)


def solution(mesh):
    gx, gy, mz = mesh.devices.shape
    fine = Mesh(mesh.devices.reshape(gx, gy, 4, mz // 4), ("gx", "gy", "w", "x"))
    slabs = ("w", "x")
    in_specs = (
        P("gx", "gy", slabs, None),
        P("gx", "gy", slabs),
        P("gx", "gy", slabs),
        P("gx", "gy", None),
        P(None, slabs),
    )
    out_specs = (P("gx", "gy", None), P(("gx", "gy"), slabs))
    return jax.shard_map(local, mesh=fine, in_specs=in_specs, out_specs=out_specs, check_vma=False)
```

time: 919 us -> 210 us (0.23)
  waiting for transfers between devices: 491 us -> 123 us
  blocking collectives: 362 us -> 53.6 us
  other arithmetic: 18.2 us -> 0.08 us
  starting transfers between devices: 15.3 us -> 0.08 us
  Pallas kernels: 0 us -> 10.5 us
  matrix products: 9.83 us -> 0 us
    psum x2 -> x0, blocking collectives: 362 us -> none  [the longest x1 261 us: local(): gram_full = lax.psum(gram_term, ('gx', 'gy'))]
    unnamed x3 -> x2, waiting for transfers between devices: 299 us -> 0.03 us
    all_gather x1, waiting for transfers between devices: 184 us -> 49.1 us  [local(): h_whole = lax.all_gather(h_low, 'gx', axis=0, tiled=True)]
    reduce_scatter x0 -> x1, waiting for transfers between devices: none -> 74.3 us  [local(): reduced = lax.psum_scatter(num_term, 'gx', scatter_dimension=0, tiled=True)]
    all_gather x0 -> x2, blocking collectives: none -> 43.6 us  [the longest x1 24.6 us: local(): both = lax.all_gather(both, 'w', axis=0)]
    ppermute x4 -> x0, starting transfers between devices: 15.2 us -> none  [the longest x2 12 us: padded_2(): lax.ppermute(tail, axis, [(i, (i + 1) % count) for i in range(ends)])]
    all_gather x1 -> x0, other arithmetic: 10.8 us -> none  [local(): h_whole = lax.all_gather(h_low, ('gx', 'gy'), axis=0, tiled=True)]
    pallas_call x0 -> x5, Pallas kernels: none -> 10.5 us  [the longest x1 3.54 us: local(): pl.pallas_call(functools.partial(spectra_kernel, tv_strength), out_shape=...]
  transfers between devices with their start and end apart: 6 -> 2, of which waited for: 3 -> 2; matrix products, arithmetic and copies ran while one was open for 2% -> 0% of each run, Pallas kernels for 0% -> 0%
where the time goes in v1:
time: 210 us; the launch traced here: 209 us
  waiting for transfers between devices  123 us (59%)
  blocking collectives  53.6 us (26%)
  between operations  14.7 us (7%)
  Pallas kernels  10.5 us (5%)
  local copies, waits for them, and re-layouts  6.91 us (3%)
    reduce_scatter x1, waiting for transfers between devices, local(): reduced = lax.psum_scatter(num_term, 'gx', scatter_dimension=0, tiled=True)  74.3 us
    all_gather x1, waiting for transfers between devices, local(): h_whole = lax.all_gather(h_low, 'gx', axis=0, tiled=True)  49.1 us
    all_gather x1, blocking collectives, local(): both = lax.all_gather(both, 'w', axis=0)  24.6 us
    all_gather x1, blocking collectives, local(): parts = lax.all_gather(reduced, 'gy', axis=0)  19 us
    all_to_all x1, blocking collectives, local(): both = lax.all_to_all(both, 'x', 0, 0, tiled=True)  10 us
    unnamed x15, local copies, waits for them, and re-layouts  6.91 us
  transfers between devices with their start and end apart: 2, of which 2 were waited for; matrix products, arithmetic and copies ran while one was open for 0% of the time, Pallas kernels for 0%

profile of v1, /device:TPU:24, one launch (start us, length us, event | category | flops | bytes accessed | tf_op | source)
XLA Modules:
  0.0 209.4 jit_solution(12812812897413171159)
XLA Ops:
  7.2 0.0 reduce-scatter.2.cloned.1.call-start
  7.9 0.0 copy-start
  7.9 1.5 copy.7
  9.3 0.1 pad_add_fusion.where_ref
  9.4 0.0 copy-start.4
  9.4 0.8 copy-done.4
  10.2 0.0 copy-start.6
  10.2 0.7 copy-done.6
  10.8 0.0 copy-start.5
  10.8 3.3 %numer.1 = (f32[128,6656]{1,0:T(8,128)}, bf16[49,128,128]{2,1,0:T(8,128)(2,1)S(1)}) custom-call(s32[2]{0:T(128)S(1)} %pad_add_fusion.where_ref, s32[52]{0:T(128)S(1)} %bitcast.16, s32[1]{0:T(128)} %bitcast.9.count_ref, bf16[64,52,128]{2,1,0:T(8,128)(2,1)S(1)} %bitcast.10, f32[64,64]{1,0:T(8,128)S(1)} %bitcast.13), custom_call_target="tpu_custom_call" | custom-call | tf_op jit(solution)/shard_map/numer/pallas_call | solution.py:222
  14.2 0.0 copy-start.1
  14.2 1.2 copy-done.1
  15.3 0.0 reduce-scatter.2.cloned.1.call-update
  15.4 0.0 all-gather.4.cloned.1.call-start
  15.4 74.3 %reduce-scatter.2.cloned.1.call-done = f32[8,6656]{1,0:T(8,128)} async-done(((f32[128,6656]{1,0:T(8,128)}), f32[8,6656]{1,0:T(8,128)}) %reduce-scatter.2.cloned.1.call-update) | async-done | bytes 213008 | tf_op jit(solution)/shard_map/reduce_scatter | solution.py:235
  89.7 19.0 %all-gather = f32[32,6656]{1,0:T(8,128)S(1)} all-gather(f32[8,6656]{1,0:T(8,128)} %reduce-scatter.2.cloned.1.call-done), channel_id=2, replica_groups=mesh['gx'=16,'gy'=4,'w'=4,'x'=4] {'gy'}, dimensions={0}, use_global_device_ids=true | all-gather | bytes 1064960 | tf_op jit(solution)/shard_map/all_gather | solution.py:236
  108.8 0.0 copy-done
  108.8 0.0 copy-done.5
  108.8 3.5 %spectra.1 = (bf16[8,6272]{1,0:T(8,128)(2,1)}, f32[1,12544]{1,0:T(1,128)}, f32[64,64]{1,0:T(8,128)S(1)}, f32[64,64]{1,0:T(8,128)S(1)}) custom-call(s32[2]{0:T(128)S(1)} %pad_add_fusion.where_ref, f32[4,8,6656]{2,1,0:T(8,128)S(1)} %bitcast.11, f32[64,12544]{1,0:T(8,128)S(1)} %copy-done, f32[64,64]{1,0:T(8,128)S(1)} %bitcast.14), custom_call_target="tpu_custom_call" | custom-call | tf_op jit(solution)/shard_map/spectra/pallas_call | solution.py:239
  112.3 0.0 all-gather.4.cloned.1.call-update
  112.3 49.1 %all-gather.4.cloned.1.call-done.h_ref = bf16[128,6272]{1,0:T(8,128)(2,1)} async-done(((bf16[8,6272]{1,0:T(8,128)(2,1)}), bf16[128,6272]{1,0:T(8,128)(2,1)}) %all-gather.4.cloned.1.call-update) | async-done | bytes 1605648 | tf_op jit(solution)/shard_map/all_gather | solution.py:253
  161.5 0.0 copy-start.2
  161.5 1.4 copy-done.2
  162.9 0.0 copy-start.3
  162.9 1.4 copy-done.3
  164.3 2.7 %project.1 = f32[4,64,128]{2,1,0:T(8,128)S(1)} custom-call(bf16[128,6272]{1,0:T(8,128)(2,1)S(1)} %copy-done.3, bf16[49,128,128]{2,1,0:T(8,128)(2,1)S(1)} %copy-done.2), custom_call_target="tpu_custom_call" | custom-call | tf_op jit(solution)/shard_map/project/pallas_call | solution.py:256
  167.0 10.0 %all_to_all.5.parts_ref = f32[4,64,128]{2,1,0:T(8,128)S(1)} all-to-all(f32[4,64,128]{2,1,0:T(8,128)S(1)} %project.1), channel_id=1, replica_groups=mesh['gx'=16,'gy'=4,'w'=4,'x'=4] {'x'}, dimensions={0} | all-to-all | bytes 262144 | tf_op jit(solution)/shard_map/all_to_all | solution.py:265
  177.1 24.6 %all-gather.1 = f32[256,128]{1,0:T(8,128)S(1)} all-gather(f32[64,128]{1,0:T(8,128)S(1)} %sum.1), channel_id=3, replica_groups=mesh['gx'=16,'gy'=4,'w'=4,'x'=4] {'w'}, dimensions={0}, use_global_device_ids=true | all-gather | bytes 163840 | tf_op jit(solution)/shard_map/all_gather | solution.py:274
  201.7 0.9 loadings.1
  (1 shorter events, 0.0 us)
Async XLA Ops:
  7.2 82.6 %reduce-scatter.2.cloned.1.call-start = ((), (), s32[]{:S(2)}) async-start(), calls=%async_computation.2 | async-start | bytes 3620864 | tf_op jit(solution)/shard_map/reduce_scatter | solution.py:235
  7.9 100.9 %copy-start = (f32[64,12544]{1,0:T(8,128)S(1)}, f32[64,12544]{1,0:T(8,128)}, u32[]{:S(2)}) copy-start(f32[64,12544]{1,0:T(8,128)} %comps_ref.1) | copy-start | bytes 9633796
  9.4 0.8 copy-start.4
  10.2 0.7 copy-start.6
  10.8 97.9 %copy-start.5 = (f32[8,8,64]{2,1,0:T(8,128)S(1)}, f32[8,8,64]{2,1,0:T(8,128)}, u32[]{:S(2)}) copy-start(f32[8,8,64]{2,1,0:T(8,128)} %param.8) | copy-start | bytes 49156
  14.2 1.2 copy-start.1
  15.4 146.1 %all-gather.4.cloned.1.call-start = ((), (), s32[]{:S(2)}) async-start(), calls=%async_computation.3 | async-start | bytes 1705984 | tf_op jit(solution)/shard_map/all_gather | solution.py:253
  161.5 1.4 copy-start.2
  162.9 1.4 copy-start.3
Sparse Core Ops, SparseCore 0:
  15.5 74.1 reduce-scatter.1
  112.5 48.9 all-gather.3

commit v2 on v1

--- a/solution.py
+++ b/solution.py
@@ -34,64 +34,132 @@
     return lax.dot_general(a, b, (((1,), (1,)), ((), ())), preferred_element_type=F32)
 
 
-def numer_kernel(where_ref, ids_ref, count_ref, x_ref, w_ref, out_ref, dense_ref, wide_ref):
-    tile, slots, lane = x_ref.shape
-    pitch = wide_ref.shape[0] // tile
+LOG_LOW = 3.25
+LOG_STEPS = 5950.0
+GRAM_SCALE = 64.0
+OFFSET = 32768
+
+
+def encode(value):
+    steps = (jnp.log2(jnp.maximum(value, 1.0)) - LOG_LOW) * LOG_STEPS
+    code = jnp.where(value > 0.0, jnp.maximum(steps, 0.0) + 1.5, 0.0).astype(jnp.int32)
+    return (jnp.minimum(code, 65535) - OFFSET).astype(jnp.int16)
+
+
+def decode(code):
+    steps = code.astype(jnp.int32).astype(F32) + float(OFFSET)
+    return jnp.where(steps > 0.0, jnp.exp2((steps - 1.0) * (1.0 / LOG_STEPS) + LOG_LOW), 0.0)
+
+
+def numer_kernel(where_ref, ids_ref, count_ref, x_ref, w_ref, send_ref, keep_ref, dense_ref):
+    tile_x, slots, tile_y, lane = x_ref.shape
+    tile = tile_x * tile_y
     half_blocks = dense_ref.shape[0]
     comps = w_ref.shape[1]
-    rows = out_ref.shape[0]
-    me = where_ref[0]
-    last = rows // 8 - 1
+    rows = send_ref.shape[0]
+    core = where_ref[2]
 
     w = w_ref[...]
     w_low = w.astype(BF16)
     w_two = jnp.concatenate([w_low, w_low], axis=0)
-    row = iota((rows, comps), 0)
-    pick = jnp.where(iota((rows, comps), 1) == 4 * (row // 8) + row % 4, 1.0, 0.0).astype(BF16)
+    row = iota((2 * rows, comps), 0)
+    row_core = jnp.where(row < rows, 1 - core, core)
+    row = row % rows
+    name = 8 * (row // 8) + 4 * row_core + row % 4
+    pick = jnp.where(iota((2 * rows, comps), 1) == name, 1.0, 0.0).astype(BF16)
     spread = nt(pick, w_two)
-    row = iota((rows, 2 * tile), 0)
-    same_half = (row // 4) % 2 == iota((rows, 2 * tile), 1) // tile
+    row = iota((2 * rows, 2 * tile), 0)
+    same_half = (row // 4) % 2 == iota((2 * rows, 2 * tile), 1) // tile
     left = jnp.where(same_half, spread, 0.0).astype(BF16)
 
     dense_ref[...] = jnp.zeros_like(dense_ref)
-    for p in range(tile):
-        wide_ref[p * pitch : p * pitch + slots, :] = x_ref[p].astype(F32)
 
     def place(s, carry):
         block = ids_ref[s]
         high = block // half_blocks
-        rows_of_slot = wide_ref[pl.ds(s, tile, stride=pitch), :].astype(BF16)
+        rows_of_slot = x_ref[:, s].astype(F32).reshape(tile, lane).astype(BF16)
         dense_ref[block - high * half_blocks, pl.ds(pl.multiple_of(high * tile, tile), tile), :] = rows_of_slot
         return carry
 
     lax.fori_loop(0, count_ref[0], place, 0)
 
     for j in range(half_blocks):
-        out_ref[:, j * lane : (j + 1) * lane] = jnp.dot(left, dense_ref[j], preferred_element_type=F32)
+        product = jnp.dot(left, dense_ref[j], preferred_element_type=F32)
+        send_ref[:, j * lane : (j + 1) * lane] = product[:rows]
+        keep_ref[:, j * lane : (j + 1) * lane] = product[rows:]
 
     base = half_blocks * lane
-    out_ref[:, base : base + 3 * lane] = jnp.zeros((rows, 3 * lane), F32)
-    out_ref[:, base : base + comps] = jnp.dot(left, w_two, preferred_element_type=F32)
-
-    pair = jnp.concatenate([w, w], axis=1)
+    product = jnp.dot(left, w_two, preferred_element_type=F32)
+    for ref, part in ((send_ref, product[:rows]), (keep_ref, product[rows:])):
+        ref[:, base:] = jnp.zeros((rows, 2 * lane), F32)
+        ref[:, base : base + comps] = part
+        ref[:, base + lane : base + lane + comps] = w
+
+
+def encode_kernel(where_ref, keep_ref, got_ref, out_ref, partner_ref):
+    lane = LANE
+    chunks, rows, width = out_ref.shape
+    base = width - 2 * lane
+    comps = partner_ref.shape[1]
+    tile = keep_ref.shape[0]
+    y, core = where_ref[3], where_ref[2]
+    at_first = core == 0
+    mine = keep_ref[:, base + lane :]
+    other = got_ref[:, base + lane :]
+    bottom = jnp.where(at_first, other[tile - 8 :], mine[tile - 8 :])
+    top = jnp.where(at_first, mine[:8], other[:8])
+    partner_ref[...] = jnp.where(at_first, other[:8], other[tile - 8 :])[:, :comps]
+    for i in range(chunks):
+        at = slice(i * rows, (i + 1) * rows)
+        for j in range(base // lane):
+            block = slice(j * lane, (j + 1) * lane)
+            out_ref[i, :, block] = encode(keep_ref[at, block] + got_ref[at, block])
+        block = slice(base, base + lane)
+        out_ref[i, :, block] = encode((keep_ref[at, block] + got_ref[at, block]) * GRAM_SCALE)
+        rim = jnp.where(i == y + 1, bottom, jnp.where(i == y - 1, top, 0.0))
+        scaled = rim * 32768.0
+        coarse = scaled.astype(jnp.int32)
+        fine = ((scaled - coarse.astype(F32)) * 65536.0).astype(jnp.int32)
+        both = jnp.where(iota((rows, lane), 1) < comps, coarse, pltpu.roll(fine, comps, 1))
+        out_ref[i, :, base + lane :] = (both - OFFSET).astype(jnp.int16)
+
+
+def merge_kernel(where_ref, codes_ref, partner_ref, w_ref, out_ref, rim_ref):
+    lane = LANE
+    chunks, rows, width = codes_ref.shape
+    base = width - 2 * lane
+    tile, comps = w_ref.shape
+    y, core = where_ref[3], where_ref[2]
+
+    def total(block):
+        out = decode(codes_ref[0, :, block])
+        for i in range(1, chunks):
+            out = out + decode(codes_ref[i, :, block])
+        return out
+
+    for j in range(base // lane):
+        block = slice(j * lane, (j + 1) * lane)
+        out_ref[:, block] = total(block)
+    out_ref[:, base : base + lane] = total(slice(base, base + lane)) * (1.0 / GRAM_SCALE)
+
+    pair = jnp.concatenate([w_ref[...], w_ref[...]], axis=1)
     first = iota((8, lane), 1) < comps
-
-    @pl.when(me < last)
-    def _():
-        at = pl.ds(pl.multiple_of(8 * (me + 1), 8), 8)
-        out_ref[at, base + lane : base + 2 * lane] += jnp.where(first, pair[tile - 8 :], 0.0)
-
-    @pl.when(me > 0)
-    def _():
-        at = pl.ds(pl.multiple_of(8 * (me - 1), 8), 8)
-        out_ref[at, base + lane : base + 2 * lane] += jnp.where(first, 0.0, pair[:8])
-
     heads = jnp.concatenate([pair[8 * i : 8 * i + 1] for i in range(8)], axis=0)
     tails = jnp.concatenate([pair[8 * i + 7 : 8 * i + 8] for i in range(8)], axis=0)
-    out_ref[pl.ds(pl.multiple_of(8 * me, 8), 8), base + 2 * lane :] = jnp.where(first, heads, tails)
-
-
-def spectra_kernel(tv_strength, where_ref, parts_ref, comps_ref, w_ref, h_low_ref, h_ref, tv_num_ref, tv_den_ref):
+    out_ref[:, base + lane :] = jnp.where(first, heads, tails)
+
+    source = jnp.where(core == 0, y - 1, y + 1)
+    inside = jnp.logical_and(source >= 0, source < chunks)
+    both = codes_ref[jnp.clip(source, 0, chunks - 1), :, base + lane :].astype(jnp.int32) + OFFSET
+    both = both.astype(F32)
+    outer = both * (1.0 / 32768.0) + pltpu.roll(both, comps, 1) * (1.0 / 2147483648.0)
+    outer = jnp.where(inside, outer, 0.0)[:, :comps]
+    partner = partner_ref[...]
+    rim_ref[0] = jnp.where(core == 0, outer, partner)
+    rim_ref[1] = jnp.where(core == 0, partner, outer)
+
+
+def spectra_kernel(tv_strength, where_ref, parts_ref, rim_ref, comps_ref, w_ref, h_low_ref, h_ref, tv_num_ref, tv_den_ref):
     lane = LANE
     half_blocks = h_low_ref.shape[1] // lane
     base = half_blocks * lane
@@ -132,11 +200,10 @@
 
     lax.fori_loop(0, half_blocks, block_step, 0)
 
-    rim = parts_ref[side, :, base + lane : base + 2 * lane]
-    above, below = rim[:, :comps], rim[:, comps:]
-    before = parts_ref[jnp.maximum(side - 1, 0), :, base + 2 * lane :][:, comps:]
+    above, below = rim_ref[0], rim_ref[1]
+    before = parts_ref[jnp.maximum(side - 1, 0), :, base + lane :][:, comps:]
     before = jnp.where(side > 0, before, 0.0)
-    after = parts_ref[jnp.minimum(side + 1, sides - 1), :, base + 2 * lane :][:, :comps]
+    after = parts_ref[jnp.minimum(side + 1, sides - 1), :, base + lane :][:, :comps]
     after = jnp.where(side < sides - 1, after, 0.0)
     spot = iota((8, comps), 0)
     rows = [w_ref[8 * i : 8 * i + 8, :] for i in range(8)]
@@ -158,15 +225,17 @@
         tv_den_ref[8 * i : 8 * i + 8, :] = tv_strength * den
 
 
-def project_kernel(h_ref, dense_ref, out_ref):
+def project_kernel(where_ref, mine_ref, other_ref, dense_ref, out_ref):
     half_blocks, two_tiles, lane = dense_ref.shape
-    rows = h_ref.shape[0]
+    comps = mine_ref.shape[0]
+    rows = 2 * comps
     copies, tile, _ = out_ref.shape
-    comps = rows // 2
+    core = where_ref[2]
     cross = jnp.zeros((two_tiles, rows), F32)
     spec = jnp.zeros((rows, rows), F32)
     for j in range(half_blocks):
-        block = h_ref[:, j * lane : (j + 1) * lane]
+        at = slice(j * lane, (j + 1) * lane)
+        block = jnp.concatenate([mine_ref[:, at], other_ref[:, at]], axis=0)
         cross = cross + nt(dense_ref[j], block)
         spec = spec + nt(block, block)
     row, col = iota((two_tiles, rows), 0), iota((two_tiles, rows), 1)
@@ -174,15 +243,14 @@
     cross = cross[:tile] + cross[tile:]
     row, col = iota((rows, rows), 0), iota((rows, rows), 1)
     spec = jnp.where((row // 4) % 2 == (col // 4) % 2, spec, 0.0)
-    name = 4 * (row // 8) + row % 4
+    row_core = jnp.where(row < comps, core, 1 - core)
+    name = 8 * (row % comps // 8) + 4 * row_core + row % 4
     to_low = jnp.where(col == name, 1.0, 0.0)
-    to_high = jnp.where(col == name + comps, 1.0, 0.0)
-    spec = lax.dot_general(
-        to_low, spec, (((0,), (0,)), ((), ())), preferred_element_type=F32, precision=lax.Precision.HIGHEST
-    )[:comps]
-    both = jnp.dot(cross, to_low, preferred_element_type=F32, precision=lax.Precision.HIGHEST) + jnp.dot(
-        spec, to_high, preferred_element_type=F32, precision=lax.Precision.HIGHEST
-    )
+    to_high = jnp.where(iota((comps, rows), 1) == iota((comps, rows), 0) + comps, 1.0, 0.0)
+    exact = dict(preferred_element_type=F32, precision=lax.Precision.HIGHEST)
+    spec = lax.dot_general(to_low, spec, (((0,), (0,)), ((), ())), **exact)[:comps]
+    spec = jnp.dot(spec, to_low, **exact)[:, :comps]
+    both = jnp.dot(cross, to_low, **exact) + jnp.dot(spec, to_high, **exact)
     for i in range(copies):
         out_ref[i] = both
 
@@ -212,28 +280,51 @@
     slab_bins = components.shape[1]
     half_blocks = slab_bins // lane // 2
     half_bins = half_blocks * lane
-    rows = 2 * comps
-    width = half_bins + 3 * lane
-    here = jnp.stack([lax.axis_index("gx"), lax.axis_index("gy")]).astype(jnp.int32)
-    pixels = spectra.reshape(tile, slot_count, lane)
+    width = half_bins + 2 * lane
+    spots = [lax.axis_index(axis) for axis in (("y", "core"), "gy", "core", "y")]
+    here = jnp.stack(spots).astype(jnp.int32)
+    chunks = lax.axis_size("y")
+    pixels = spectra.transpose(0, 2, 1, 3)
     w = loadings.reshape(tile, comps)
-    pitch = -(-slot_count // 8) * 8
-
-    num_term, dense = pl.pallas_call(
+    swap = [(0, 1), (1, 0)]
+
+    send, keep, dense = pl.pallas_call(
         numer_kernel,
         out_shape=(
-            jax.ShapeDtypeStruct((rows, width), F32),
+            jax.ShapeDtypeStruct((comps, width), F32),
+            jax.ShapeDtypeStruct((comps, width), F32),
             jax.ShapeDtypeStruct((half_blocks, 2 * tile, lane), BF16),
         ),
         in_specs=[smem(), smem(), smem(), vmem(), vmem()],
-        out_specs=(vmem(), vmem()),
-        scratch_shapes=[pltpu.VMEM((tile * pitch, lane), F32)],
+        out_specs=(vmem(),) * 3,
         compiler_params=params(),
         name="numer",
     )(here, block_ids.reshape(slot_count), counts.reshape(1), pixels, w)
-
-    reduced = lax.psum_scatter(num_term, "gx", scatter_dimension=0, tiled=True)
-    parts = lax.all_gather(reduced, "gy", axis=0)
+    got = lax.ppermute(send, "core", swap)
+    codes, partner = pl.pallas_call(
+        encode_kernel,
+        out_shape=(
+            jax.ShapeDtypeStruct((chunks, 8, width), jnp.int16),
+            jax.ShapeDtypeStruct((8, comps), F32),
+        ),
+        in_specs=[smem(), vmem(), vmem()],
+        out_specs=(vmem(),) * 2,
+        compiler_params=params(),
+        name="encode",
+    )(here, keep, got)
+    codes = lax.all_to_all(codes, "y", 0, 0, tiled=True)
+    merged, rims = pl.pallas_call(
+        merge_kernel,
+        out_shape=(
+            jax.ShapeDtypeStruct((8, width), F32),
+            jax.ShapeDtypeStruct((2, 8, comps), F32),
+        ),
+        in_specs=[smem(), vmem(), vmem(), vmem()],
+        out_specs=(vmem(),) * 2,
+        compiler_params=params(),
+        name="merge",
+    )(here, codes, partner, w)
+    parts = lax.all_gather(merged, "gy", axis=0)
 
     tv_strength = tv_share * slab_bins * lax.axis_size(("w", "x"))
     h_low, h_next, tv_num, tv_den = pl.pallas_call(
@@ -244,23 +335,24 @@
             jax.ShapeDtypeStruct((tile, comps), F32),
             jax.ShapeDtypeStruct((tile, comps), F32),
         ),
-        in_specs=[smem(), vmem(), vmem(), vmem()],
+        in_specs=[smem(), vmem(), vmem(), vmem(), vmem()],
         out_specs=(vmem(),) * 4,
         compiler_params=params(),
         name="spectra",
-    )(here, parts, components, w)
-
-    h_whole = lax.all_gather(h_low, "gx", axis=0, tiled=True)
+    )(here, parts, rims, components, w)
+
+    h_mine = lax.all_gather(h_low, "y", axis=0, tiled=True)
+    h_other = lax.ppermute(h_mine, "core", swap)
 
     copies = lax.axis_size("x")
     both = pl.pallas_call(
         project_kernel,
         out_shape=jax.ShapeDtypeStruct((copies, tile, 2 * comps), F32),
-        in_specs=[vmem(), vmem()],
+        in_specs=[smem(), vmem(), vmem(), vmem()],
         out_specs=vmem(),
         compiler_params=params(),
         name="project",
-    )(h_whole, dense)
+    )(here, h_mine, h_other, dense)
 
     both = lax.all_to_all(both, "x", 0, 0, tiled=True)
     both = pl.pallas_call(
@@ -285,14 +377,14 @@
 
 def solution(mesh):
     gx, gy, mz = mesh.devices.shape
-    fine = Mesh(mesh.devices.reshape(gx, gy, 4, mz // 4), ("gx", "gy", "w", "x"))
-    slabs = ("w", "x")
+    fine = Mesh(mesh.devices.reshape(gx // 2, 2, gy, 4, mz // 4), ("y", "core", "gy", "w", "x"))
+    rows, slabs = ("y", "core"), ("w", "x")
     in_specs = (
-        P("gx", "gy", slabs, None),
-        P("gx", "gy", slabs),
-        P("gx", "gy", slabs),
-        P("gx", "gy", None),
+        P(rows, "gy", slabs, None),
+        P(rows, "gy", slabs),
+        P(rows, "gy", slabs),
+        P(rows, "gy", None),
         P(None, slabs),
     )
-    out_specs = (P("gx", "gy", None), P(("gx", "gy"), slabs))
+    out_specs = (P(rows, "gy", None), P(("y", "core", "gy"), slabs))
     return jax.shard_map(local, mesh=fine, in_specs=in_specs, out_specs=out_specs, check_vma=False)

time: 210 us -> 143 us (0.68)
  the two profiles are of different devices: /device:TPU:24 before, /device:TPU:2 now
where the time goes in v2:
time: 143 us
  blocking collectives  117 us (82%)
  Pallas kernels  12.1 us (8%)
  waiting for transfers between devices  5.79 us (4%)
  starting transfers between devices  3.83 us (3%)
  local copies, waits for them, and re-layouts  2.58 us (2%)
    all_to_all x1, blocking collectives, local(): codes = lax.all_to_all(codes, 'y', 0, 0, tiled=True)  32.1 us
    all_gather x1, blocking collectives, local(): h_mine = lax.all_gather(h_low, 'y', axis=0, tiled=True)  26.3 us
    all_gather x1, blocking collectives, local(): both = lax.all_gather(both, 'w', axis=0)  26.1 us
    all_gather x1, blocking collectives, local(): parts = lax.all_gather(merged, 'gy', axis=0)  22 us
    all_to_all x1, blocking collectives, local(): both = lax.all_to_all(both, 'x', 0, 0, tiled=True)  10.8 us
    ppermute x1, waiting for transfers between devices, local(): got = lax.ppermute(send, 'core', swap)  3.52 us
    pallas_call x1, Pallas kernels, local(): pl.pallas_call(functools.partial(spectra_kernel, tv_strength), out_shape=...  3.51 us
    pallas_call x1, Pallas kernels, local(): pl.pallas_call(project_kernel, out_shape=jax.ShapeDtypeStruct((copies, ti...  3.43 us
  transfers between devices with their start and end apart: 2, of which 2 were waited for; matrix products, arithmetic and copies ran while one was open for 0% of the time, Pallas kernels for 0%

profile of v2, /device:TPU:2, one launch (start us, length us, event | category | flops | bytes accessed | tf_op | source)
XLA Modules:
  0.0 143.1 jit_solution(12307974903307483211)
XLA Ops:
  1.3 0.1 pad_add_fusion.where_ref
  1.4 0.0 copy-start.1
  1.4 1.2 copy-done.1
  2.5 0.0 copy-start.2
  2.5 0.8 copy-done.2
  3.3 0.0 copy-start.4
  3.3 0.7 copy-done.4
  3.9 1.9 %numer.1 = (f32[64,6528]{1,0:T(8,128)S(1)}, f32[64,6528]{1,0:T(8,128)S(1)}, bf16[49,128,128]{2,1,0:T(8,128)(2,1)S(1)}) custom-call(s32[4]{0:T(128)S(1)} %pad_add_fusion.where_ref, s32[52]{0:T(128)S(1)} %bitcast.19, s32[1]{0:T(128)} %bitcast.11.count_ref, bf16[8,52,8,128]{3,2,1,0:T(8,128)(2,1)S(1)} %bitcast.13, f32[64,64]{1,0:T(8,128)S(1)} %bitcast.14), custom_call_target="tpu_custom_call" | custom-call | tf_op jit(solution)/shard_map/numer/pallas_call | solution.py:291
  5.8 1.9 %collective-permute-start = (f32[64,6528]{1,0:T(8,128)S(1)}, f32[64,6528]{1,0:T(8,128)S(1)}, u32[]{:S(2)}, u32[]{:S(2)}) collective-permute-start(f32[64,6528]{1,0:T(8,128)S(1)} %get-tuple-element.14), channel_id=1, source_target_pairs={{0,64},{64,0},{1,65},{65,1},{2,66},{66,2},{3,67},{67,3},{4,68},{68... | collective-permute-start | bytes 5013512 | tf_op jit(solution)/shard_map/ppermute | solution.py:303
  7.7 3.5 %collective-permute-done.got_ref = f32[64,6528]{1,0:T(8,128)S(1)} collective-permute-done((f32[64,6528]{1,0:T(8,128)S(1)}, f32[64,6528]{1,0:T(8,128)S(1)}, u32[]{:S(2)}, u32[]{:S(2)}) %collective-permute-start) | collective-permute-done | bytes 1671200 | tf_op jit(solution)/shard_map/ppermute | solution.py:303
  11.3 1.4 encode.1
  12.6 0.0 copy-start.3
  12.7 0.0 copy-start
  12.7 32.1 %all_to_all.10.codes_ref = s16[8,8,6528]{2,1,0:T(8,128)(2,1)S(1)} all-to-all(s16[8,8,6528]{2,1,0:T(8,128)(2,1)S(1)} %get-tuple-element.15), channel_id=1, replica_groups=mesh['y'=8,'core'=2,'gy'=4,'w'=4,'x'=4] {'y'}, dimensions={0} | all-to-all | bytes 1671168 | tf_op jit(solution)/shard_map/all_to_all | solution.py:315
  44.8 0.0 copy-done.3
  44.8 1.1 merge.1
  45.9 22.0 %all-gather = f32[32,6528]{1,0:T(8,128)S(1)} all-gather(f32[8,6528]{1,0:T(8,128)S(1)} %get-tuple-element.17), channel_id=2, replica_groups=mesh['y'=8,'core'=2,'gy'=4,'w'=4,'x'=4] {'gy'}, dimensions={0}, use_global_device_ids=true | all-gather | bytes 1044480 | tf_op jit(solution)/shard_map/all_gather | solution.py:327
  67.8 0.0 copy-done
  67.8 3.5 %spectra.1 = (bf16[8,6272]{1,0:T(8,128)(2,1)S(1)}, f32[1,12544]{1,0:T(1,128)}, f32[64,64]{1,0:T(8,128)S(1)}, f32[64,64]{1,0:T(8,128)S(1)}) custom-call(s32[4]{0:T(128)S(1)} %pad_add_fusion.where_ref, f32[4,8,6528]{2,1,0:T(8,128)S(1)} %bitcast.12, f32[2,8,64]{2,1,0:T(8,128)S(1)} %get-tuple-element.18.rim_ref, f32[64,12544]{1,0:T(8,128)S(1)} %copy-done, ...), custom_call_target="tpu_custom_call" | custom-call | tf_op jit(solution)/shard_map/spectra/pallas_call | solution.py:330
  71.3 26.3 %all_gather.17.mine_ref = bf16[64,6272]{1,0:T(8,128)(2,1)S(1)} all-gather(bf16[8,6272]{1,0:T(8,128)(2,1)S(1)} %get-tuple-element.19), channel_id=1, replica_groups=mesh['y'=8,'core'=2,'gy'=4,'w'=4,'x'=4] {'y'}, dimensions={0}, use_global_device_ids=true | all-gather | bytes 903168 | tf_op jit(solution)/shard_map/all_gather | solution.py:344
  97.6 1.9 %collective-permute-start.1 = (bf16[64,6272]{1,0:T(8,128)(2,1)S(1)}, bf16[64,6272]{1,0:T(8,128)(2,1)S(1)}, u32[]{:S(2)}, u32[]{:S(2)}) collective-permute-start(bf16[64,6272]{1,0:T(8,128)(2,1)S(1)} %all_gather.17.mine_ref), channel_id=1, source_target_pairs={{0,64},{64,0},{1,65},{65,1},{2,66},{66,2},{3,67},{67,3},{4,68},{68... | collective-permute-start | bytes 2408456 | tf_op jit(solution)/shard_map/ppermute | solution.py:345
  99.5 2.3 %collective-permute-done.1.other_ref = bf16[64,6272]{1,0:T(8,128)(2,1)S(1)} collective-permute-done((bf16[64,6272]{1,0:T(8,128)(2,1)S(1)}, bf16[64,6272]{1,0:T(8,128)(2,1)S(1)}, u32[]{:S(2)}, u32[]{:S(2)}) %collective-permute-start.1) | collective-permute-done | bytes 802848 | tf_op jit(solution)/shard_map/ppermute | solution.py:345
  101.8 3.4 %project.1 = f32[4,64,128]{2,1,0:T(8,128)S(1)} custom-call(s32[4]{0:T(128)S(1)} %pad_add_fusion.where_ref, bf16[64,6272]{1,0:T(8,128)(2,1)S(1)} %all_gather.17.mine_ref, bf16[64,6272]{1,0:T(8,128)(2,1)S(1)} %collective-permute-done.1.other_ref, bf16[49,128,128]{2,1,0:T(8,128)(2,1)S(1)} %get-tuple-element.20.dense_ref), custom_call_target="tpu_custom_call" | custom-call | tf_op jit(solution)/shard_map/project/pallas_call | solution.py:348
  105.2 10.8 %all_to_all.11.parts_ref = f32[4,64,128]{2,1,0:T(8,128)S(1)} all-to-all(f32[4,64,128]{2,1,0:T(8,128)S(1)} %project.1), channel_id=1, replica_groups=mesh['y'=8,'core'=2,'gy'=4,'w'=4,'x'=4] {'x'}, dimensions={0} | all-to-all | bytes 262144 | tf_op jit(solution)/shard_map/all_to_all | solution.py:357
  116.1 26.1 %all-gather.1 = f32[256,128]{1,0:T(8,128)S(1)} all-gather(f32[64,128]{1,0:T(8,128)S(1)} %sum.1), channel_id=3, replica_groups=mesh['y'=8,'core'=2,'gy'=4,'w'=4,'x'=4] {'w'}, dimensions={0}, use_global_device_ids=true | all-gather | bytes 163840 | tf_op jit(solution)/shard_map/all_gather | solution.py:366
  142.2 0.9 loadings.1
  (1 shorter events, 0.0 us)
Async XLA Ops:
  1.4 1.2 copy-start.1
  2.5 0.8 copy-start.2
  3.3 0.7 copy-start.4
  5.8 5.4 %collective-permute-start = (f32[64,6528]{1,0:T(8,128)S(1)}, f32[64,6528]{1,0:T(8,128)S(1)}, u32[]{:S(2)}, u32[]{:S(2)}) collective-permute-start(f32[64,6528]{1,0:T(8,128)S(1)} %get-tuple-element.14), channel_id=1, source_target_pairs={{0,64},{64,0},{1,65},{65,1},{2,66},{66,2},{3,67},{67,3},{4,68},{68... | collective-permute-start | bytes 5013512 | tf_op jit(solution)/shard_map/ppermute | solution.py:303
  12.6 32.1 %copy-start.3 = (f32[8,8,64]{2,1,0:T(8,128)S(1)}, f32[8,8,64]{2,1,0:T(8,128)}, u32[]{:S(2)}) copy-start(f32[8,8,64]{2,1,0:T(8,128)} %param.8) | copy-start | bytes 49156
  12.7 55.2 %copy-start = (f32[64,12544]{1,0:T(8,128)S(1)}, f32[64,12544]{1,0:T(8,128)}, u32[]{:S(2)}) copy-start(f32[64,12544]{1,0:T(8,128)} %comps_ref.1) | copy-start | bytes 9633796
  97.6 4.2 %collective-permute-start.1 = (bf16[64,6272]{1,0:T(8,128)(2,1)S(1)}, bf16[64,6272]{1,0:T(8,128)(2,1)S(1)}, u32[]{:S(2)}, u32[]{:S(2)}) collective-permute-start(bf16[64,6272]{1,0:T(8,128)(2,1)S(1)} %all_gather.17.mine_ref), channel_id=1, source_target_pairs={{0,64},{64,0},{1,65},{65,1},{2,66},{66,2},{3,67},{67,3},{4,68},{68... | collective-permute-start | bytes 2408456 | tf_op jit(solution)/shard_map/ppermute | solution.py:345

commit v3 on v2

v3 whole, which is shorter than its diff:
```python
import functools
import jax
import jax.numpy as jnp
from jax import lax
from jax.experimental import pallas as pl
from jax.experimental.pallas import tpu as pltpu
from jax.sharding import Mesh, PartitionSpec as P

tv_edge = 0.1
tv_share = 0.1
LANE = 128
VMEM_LIMIT = 48 * 1024 * 1024
F32 = jnp.float32
BF16 = jnp.bfloat16


def params():
    return pltpu.CompilerParams(vmem_limit_bytes=VMEM_LIMIT)


def vmem():
    return pl.BlockSpec(memory_space=pltpu.VMEM)


def smem():
    return pl.BlockSpec(memory_space=pltpu.SMEM)


def iota(shape, dim):
    return lax.broadcasted_iota(jnp.int32, shape, dim)


def nt(a, b):
    return lax.dot_general(a, b, (((1,), (1,)), ((), ())), preferred_element_type=F32)


LOG_LOW = 3.25
LOG_STEPS = 5950.0
GRAM_SCALE = 64.0
OFFSET = 32768


def encode(value):
    steps = (jnp.log2(jnp.maximum(value, 1.0)) - LOG_LOW) * LOG_STEPS
    code = jnp.where(value > 0.0, jnp.maximum(steps, 0.0) + 1.5, 0.0).astype(jnp.int32)
    return jnp.minimum(code, 65535)


def decode(code):
    steps = code.astype(jnp.int32).astype(F32) + float(OFFSET)
    return jnp.where(steps > 0.0, jnp.exp2((steps - 1.0) * (1.0 / LOG_STEPS) + LOG_LOW), 0.0)


GRAM_ROW = 14
HALO_ROW = 15


def numer_kernel(where_ref, ids_ref, count_ref, x_ref, w_ref, send_ref, keep_ref, dense_ref):
    tile_x, slots, tile_y, lane = x_ref.shape
    tile = tile_x * tile_y
    blocks = dense_ref.shape[0]
    comps = w_ref.shape[1]
    half = comps // 2
    across = keep_ref.shape[0]
    depth = keep_ref.shape[1] // half
    core = where_ref[2]

    w = w_ref[...]
    w_low = w.astype(BF16)
    row = iota((comps, comps), 0)
    name = 8 * (row % half // 4) + 4 * jnp.where(row < half, 1 - core, core) + row % 4
    pick = jnp.where(iota((comps, comps), 1) == name, 1.0, 0.0).astype(BF16)
    left = nt(pick, w_low).astype(BF16)

    dense_ref[...] = jnp.zeros_like(dense_ref)

    def place(s, carry):
        dense_ref[ids_ref[s]] = x_ref[:, s].astype(F32).reshape(tile, lane).astype(BF16)
        return carry

    lax.fori_loop(0, count_ref[0], place, 0)

    def put(ref, r, j, value):
        ref[j, pl.ds(r, half, stride=depth), :] = value

    for b in range(0, blocks, 2):
        right = jnp.concatenate([dense_ref[b], dense_ref[b + 1]], axis=1)
        product = jnp.dot(left, right, preferred_element_type=F32)
        for i in range(2):
            r, j = divmod(b + i, across)
            put(send_ref, r, j, product[:half, i * lane : (i + 1) * lane])
            put(keep_ref, r, j, product[half:, i * lane : (i + 1) * lane])

    product = jnp.dot(left, jnp.concatenate([w_low, w_low], axis=1), preferred_element_type=F32)
    wide = jnp.concatenate([w[:half], w[half:]], axis=1)
    empty = jnp.zeros((half, lane), F32)
    for ref, part in ((send_ref, product[:half]), (keep_ref, product[half:])):
        for j in range(across):
            put(ref, GRAM_ROW, j, part if j == 0 else wide if j == 1 else empty)
            put(ref, HALO_ROW, j, empty)


def rim_codes(rim):
    scaled = jnp.concatenate([rim, rim], axis=1) * 32768.0
    coarse = scaled.astype(jnp.int32)
    fine = ((scaled - coarse.astype(F32)) * 65536.0).astype(jnp.int32)
    return jnp.where(iota(scaled.shape, 1) < rim.shape[1], coarse, fine)


def encode_kernel(where_ref, keep_ref, got_ref, w_ref, out_ref, partner_ref):
    lane = LANE
    chunks, depth, width = out_ref.shape
    sides = 4
    tile, comps = w_ref.shape
    half = comps // 2
    side, core, y = where_ref[1], where_ref[2], where_ref[3]
    at_first = core == 0
    w = w_ref[...]
    wide = got_ref[1, pl.ds(GRAM_ROW, half, stride=depth), :]
    partner_top, partner_bottom = wide[:8, :comps], wide[half - 8 :, comps:]
    partner_ref[...] = jnp.where(at_first, partner_top, partner_bottom)
    bottom = rim_codes(jnp.where(at_first, partner_bottom, w[tile - 8 :]))
    top = rim_codes(jnp.where(at_first, w[:8], partner_top))
    first = rim_codes(jnp.concatenate([w[8 * i : 8 * i + 1] for i in range(8)], axis=0))
    last = rim_codes(jnp.concatenate([w[8 * i + 7 : 8 * i + 8] for i in range(8)], axis=0))
    row = iota((depth, lane), 0)
    scale = jnp.where(row == GRAM_ROW, GRAM_SCALE, 1.0)
    for i in range(chunks):
        to_y, to_side = divmod(i, sides)
        same_side, same_y = side == to_side, y == to_y
        halo = jnp.where(jnp.logical_and(same_side, y + 1 == to_y), bottom, 0)
        halo = jnp.where(jnp.logical_and(same_side, y - 1 == to_y), top, halo)
        halo = jnp.where(jnp.logical_and(same_y, side + 1 == to_side), last, halo)
        halo = jnp.where(jnp.logical_and(same_y, side - 1 == to_side), first, halo)
        at = slice(i * depth, (i + 1) * depth)
        for j in range(width // lane):
            block = slice(j * lane, (j + 1) * lane)
            value = keep_ref[j, at, :] + got_ref[j, at, :]
            code = encode(value * scale if j == 0 else value)
            code = jnp.where(row == HALO_ROW, halo[j : j + 1], code)
            if j == 1:
                code = jnp.where(row == GRAM_ROW, halo[7:8], code)
            out_ref[i, :, block] = (code - OFFSET).astype(jnp.int16)


def spectra_kernel(tv_strength, where_ref, codes_ref, partner_ref, comps_ref, w_ref, h_all_ref, h_ref, tv_num_ref, tv_den_ref):
    lane = LANE
    chunks, depth, width = codes_ref.shape
    across = width // lane
    sides = 4
    tile, comps = w_ref.shape
    side, core, y = where_ref[1], where_ref[2], where_ref[3]
    turn = lax.rem(8 - 4 * core - side, 8)

    def total(j):
        block = slice(j * lane, (j + 1) * lane)
        out = decode(codes_ref[0, :, block])
        for i in range(1, chunks):
            out = out + decode(codes_ref[i, :, block])
        return out

    sums = [total(j) for j in range(across)]
    gram = jnp.transpose(sums[0])[:comps, GRAM_ROW : GRAM_ROW + 1] * (1.0 / GRAM_SCALE)
    gram = jnp.broadcast_to(gram, (comps, lane))
    for j in range(across):
        denominators, own_rows = [], []
        for r in range(GRAM_ROW):
            block = slice((r * across + j) * lane, (r * across + j + 1) * lane)
            denominators.append(jnp.sum(comps_ref[:, block] * gram, axis=0, keepdims=True))
            group = comps_ref[pl.ds(pl.multiple_of(8 * y, 8), 8), block]
            own_rows.append(pltpu.roll(group, turn, 0)[:1])
        denominators.append(jnp.ones((depth - GRAM_ROW, lane), F32))
        own_rows.append(jnp.zeros((depth - GRAM_ROW, lane), F32))
        h = jnp.concatenate(own_rows, axis=0) * sums[j] / jnp.concatenate(denominators, axis=0)
        for r in range(GRAM_ROW):
            h_ref[:, (r * across + j) * lane : (r * across + j + 1) * lane] = h[r : r + 1]
        h_low = h.astype(BF16)
        for i in range(chunks):
            h_all_ref[i, :, j * lane : (j + 1) * lane] = h_low

    def halo(from_y, from_side):
        inside = jnp.logical_and(
            jnp.logical_and(from_y >= 0, from_y < chunks // sides), jnp.logical_and(from_side >= 0, from_side < sides)
        )
        source = jnp.where(inside, from_y * sides + from_side, 0)
        rows = [
            codes_ref[source, :, j * lane : (j + 1) * lane].astype(jnp.int32)[HALO_ROW : HALO_ROW + 1]
            for j in range(across)
        ]
        rows.append(codes_ref[source, :, lane : 2 * lane].astype(jnp.int32)[GRAM_ROW : GRAM_ROW + 1])
        both = (jnp.concatenate(rows, axis=0) + OFFSET).astype(F32)
        value = both * (1.0 / 32768.0) + pltpu.roll(both, comps, 1) * (1.0 / 2147483648.0)
        return jnp.where(inside, value, 0.0)[:, :comps]

    outer = halo(jnp.where(core == 0, y - 1, y + 1), side)
    before, after = halo(y, side - 1), halo(y, side + 1)
    partner = partner_ref[...]
    above = jnp.where(core == 0, outer, partner)
    below = jnp.where(core == 0, partner, outer)
    spot = iota((8, comps), 0)
    rows = [w_ref[8 * i : 8 * i + 8, :] for i in range(8)]
    for i in range(8):
        centre = rows[i]
        beside = (
            rows[i + 1] if i < 7 else below,
            rows[i - 1] if i > 0 else above,
            jnp.where(spot == 7, after[i : i + 1], pltpu.roll(centre, 7, 0)),
            jnp.where(spot == 0, before[i : i + 1], pltpu.roll(centre, 1, 0)),
        )
        num = jnp.zeros_like(centre)
        den = jnp.zeros_like(centre)
        for q in beside:
            edge_weight = 1.0 / (jnp.abs(centre - q) + tv_edge)
            num = num + edge_weight * q
            den = den + edge_weight * centre
        tv_num_ref[8 * i : 8 * i + 8, :] = tv_strength * num
        tv_den_ref[8 * i : 8 * i + 8, :] = tv_strength * den


def project_kernel(where_ref, mine_ref, other_ref, dense_ref, out_ref, wide_ref):
    blocks, tile, lane = dense_ref.shape
    half, depth, width = mine_ref.shape
    across = width // lane
    comps = 2 * half
    copies = out_ref.shape[0]
    core = where_ref[2]
    for i, ref in enumerate((mine_ref, other_ref)):
        for j in range(across):
            block = ref[:, :, j * lane : (j + 1) * lane]
            wide_ref[i, j] = block.astype(F32).reshape(half * depth, lane)

    def spectrum(b):
        r, j = divmod(b, across)
        parts = [wide_ref[i, j, pl.ds(r, half, stride=depth), :] for i in range(2)]
        return jnp.concatenate(parts, axis=0).astype(BF16)

    total = jnp.zeros((tile + comps, comps), F32)
    for b in range(0, blocks, 2):
        h = jnp.concatenate([spectrum(b), spectrum(b + 1)], axis=1)
        x = jnp.concatenate([dense_ref[b], dense_ref[b + 1]], axis=1)
        total = total + nt(jnp.concatenate([x, h], axis=0), h)
    row = iota((comps, lane), 0)
    name = 8 * (row % half // 4) + 4 * jnp.where(row < half, core, 1 - core) + row % 4
    to_low = jnp.where(iota((comps, lane), 1) == name, 1.0, 0.0)
    to_high = jnp.where(iota((comps, lane), 1) == name + comps, 1.0, 0.0)
    exact = dict(preferred_element_type=F32, precision=lax.Precision.HIGHEST)
    spec = lax.dot_general(to_low, total[tile:], (((0,), (0,)), ((), ())), **exact)[:comps]
    both = jnp.dot(total[:tile], to_low, **exact) + jnp.dot(spec, to_high, **exact)
    for i in range(copies):
        out_ref[i] = both


def sum_kernel(parts_ref, out_ref):
    block = parts_ref[0]
    for i in range(1, parts_ref.shape[0]):
        block = block + parts_ref[i]
    out_ref[...] = block


def loadings_kernel(parts_ref, w_ref, tv_num_ref, tv_den_ref, out_ref):
    comps = w_ref.shape[1]
    block = parts_ref[0]
    for i in range(1, parts_ref.shape[0]):
        block = block + parts_ref[i]
    w = w_ref[...]
    fitted = jnp.dot(w, block, preferred_element_type=F32, precision=lax.Precision.HIGHEST)
    fitted = pltpu.roll(fitted, comps, 1)[:, :comps]
    out_ref[...] = w * (block[:, :comps] + tv_num_ref[...]) / (fitted + tv_den_ref[...])


def local(spectra, block_ids, counts, loadings, components):
    tile_x, tile_y, slot_count, lane = spectra.shape
    tile = tile_x * tile_y
    comps = loadings.shape[2]
    slab_bins = components.shape[1]
    blocks = slab_bins // lane
    half = comps // 2
    depth = 16
    width = slab_bins // GRAM_ROW
    spots = [lax.axis_index(axis) for axis in (("y", "core"), "gy", "core", "y")]
    here = jnp.stack(spots).astype(jnp.int32)
    peers = ("y", "gy")
    chunks = lax.axis_size(peers)
    pixels = spectra.transpose(0, 2, 1, 3)
    w = loadings.reshape(tile, comps)
    swap = [(0, 1), (1, 0)]

    send, keep, dense = pl.pallas_call(
        numer_kernel,
        out_shape=(
            jax.ShapeDtypeStruct((width // lane, half * depth, lane), F32),
            jax.ShapeDtypeStruct((width // lane, half * depth, lane), F32),
            jax.ShapeDtypeStruct((blocks, tile, lane), BF16),
        ),
        in_specs=[smem(), smem(), smem(), vmem(), vmem()],
        out_specs=(vmem(),) * 3,
        compiler_params=params(),
        name="numer",
    )(here, block_ids.reshape(slot_count), counts.reshape(1), pixels, w)
    got = lax.ppermute(send, "core", swap)
    codes, partner = pl.pallas_call(
        encode_kernel,
        out_shape=(
            jax.ShapeDtypeStruct((chunks, depth, width), jnp.int16),
            jax.ShapeDtypeStruct((8, comps), F32),
        ),
        in_specs=[smem(), vmem(), vmem(), vmem()],
        out_specs=(vmem(),) * 2,
        compiler_params=params(),
        name="encode",
    )(here, keep, got, w)
    codes = lax.all_to_all(codes, peers, 0, 0, tiled=True)
    tv_strength = tv_share * slab_bins * lax.axis_size(("w", "x"))
    h_all, h_next, tv_num, tv_den = pl.pallas_call(
        functools.partial(spectra_kernel, tv_strength),
        out_shape=(
            jax.ShapeDtypeStruct((chunks, depth, width), BF16),
            jax.ShapeDtypeStruct((1, slab_bins), F32),
            jax.ShapeDtypeStruct((tile, comps), F32),
            jax.ShapeDtypeStruct((tile, comps), F32),
        ),
        in_specs=[smem(), vmem(), vmem(), vmem(), vmem()],
        out_specs=(vmem(),) * 4,
        compiler_params=params(),
        name="spectra",
    )(here, codes, partner, components, w)

    h_mine = lax.all_to_all(h_all, peers, 0, 0, tiled=True)
    h_other = lax.ppermute(h_mine, "core", swap)

    copies = lax.axis_size("x")
    both = pl.pallas_call(
        project_kernel,
        out_shape=jax.ShapeDtypeStruct((copies, tile, 2 * comps), F32),
        in_specs=[smem(), vmem(), vmem(), vmem()],
        out_specs=vmem(),
        scratch_shapes=[pltpu.VMEM((2, width // lane, half * depth, lane), F32)],
        compiler_params=params(),
        name="project",
    )(here, h_mine, h_other, dense)

    both = lax.all_to_all(both, "x", 0, 0, tiled=True)
    both = pl.pallas_call(
        sum_kernel,
        out_shape=jax.ShapeDtypeStruct((tile, 2 * comps), F32),
        in_specs=[vmem()],
        out_specs=vmem(),
        compiler_params=params(),
        name="sum",
    )(both)
    both = lax.all_gather(both, "w", axis=0)
    w_next = pl.pallas_call(
        loadings_kernel,
        out_shape=jax.ShapeDtypeStruct((tile, comps), F32),
        in_specs=[vmem()] * 4,
        out_specs=vmem(),
        compiler_params=params(),
        name="loadings",
    )(both, w, tv_num, tv_den)
    return (w_next.reshape(tile_x, tile_y, comps), h_next)


def solution(mesh):
    gx, gy, mz = mesh.devices.shape
    fine = Mesh(mesh.devices.reshape(gx // 2, 2, gy, 4, mz // 4), ("y", "core", "gy", "w", "x"))
    rows, slabs = ("y", "core"), ("w", "x")
    in_specs = (
        P(rows, "gy", slabs, None),
        P(rows, "gy", slabs),
        P(rows, "gy", slabs),
        P(rows, "gy", None),
        P(None, slabs),
    )
    out_specs = (P(rows, "gy", None), P(("y", "core", "gy"), slabs))
    return jax.shard_map(local, mesh=fine, in_specs=in_specs, out_specs=out_specs, check_vma=False)
```

time: 143 us -> 131 us (0.916)
  the two profiles are of different devices: /device:TPU:2 before, /device:TPU:8 now
where the time goes in v3:
time: 131 us
  blocking collectives  106 us (81%)
  Pallas kernels  9.8 us (7%)
  waiting for transfers between devices  6.19 us (5%)
  starting transfers between devices  3.83 us (3%)
  local copies, waits for them, and re-layouts  3.33 us (3%)
  between operations  1.33 us (1%)
    all_to_all x1, blocking collectives, local(): codes = lax.all_to_all(codes, peers, 0, 0, tiled=True)  41.8 us
    all_to_all x1, blocking collectives, local(): h_mine = lax.all_to_all(h_all, peers, 0, 0, tiled=True)  30 us
    all_gather x1, blocking collectives, local(): both = lax.all_gather(both, 'w', axis=0)  25.9 us
    all_to_all x1, blocking collectives, local(): both = lax.all_to_all(both, 'x', 0, 0, tiled=True)  8.36 us
    ppermute x1, waiting for transfers between devices, local(): got = lax.ppermute(send, 'core', swap)  3.75 us
    unnamed x12, local copies, waits for them, and re-layouts  3.33 us
  transfers between devices with their start and end apart: 2, of which 2 were waited for; matrix products, arithmetic and copies ran while one was open for 0% of the time, Pallas kernels for 0%

profile of v3, /device:TPU:8, one launch (start us, length us, event | category | flops | bytes accessed | tf_op | source)
XLA Modules:
  0.0 130.7 jit_solution(18177770828816783401)
XLA Ops:
  1.3 0.1 pad_add_fusion.where_ref
  1.4 0.0 copy-start.1
  1.4 1.2 copy-done.1
  2.5 0.0 copy-start.2
  2.5 0.8 copy-done.2
  3.3 0.0 copy-start.5
  3.3 0.7 copy-done.5
  3.9 2.5 %numer.1 = (f32[7,512,128]{2,1,0:T(8,128)S(1)}, f32[7,512,128]{2,1,0:T(8,128)S(1)}, bf16[98,64,128]{2,1,0:T(8,128)(2,1)S(1)}) custom-call(s32[4]{0:T(128)S(1)} %pad_add_fusion.where_ref, s32[52]{0:T(128)S(1)} %bitcast.17, s32[1]{0:T(128)} %bitcast.10.count_ref, bf16[8,52,8,128]{3,2,1,0:T(8,128)(2,1)S(1)} %bitcast.11, f32[64,64]{1,0:T(8,128)S(1)} %bitcast.12), custom_call_target="tpu_custom_call" | custom-call | tf_op jit(solution)/shard_map/numer/pallas_call | solution.py:288
  6.4 1.9 %collective-permute-start = (f32[7,512,128]{2,1,0:T(8,128)S(1)}, f32[7,512,128]{2,1,0:T(8,128)S(1)}, u32[]{:S(2)}, u32[]{:S(2)}) collective-permute-start(f32[7,512,128]{2,1,0:T(8,128)S(1)} %get-tuple-element.12), channel_id=1, source_target_pairs={{0,64},{64,0},{1,65},{65,1},{2,66},{66,2},{3,67},{67,3},{4,68},{68... | collective-permute-start | bytes 5505032 | tf_op jit(solution)/shard_map/ppermute | solution.py:300
  8.4 3.8 %collective-permute-done.got_ref = f32[7,512,128]{2,1,0:T(8,128)S(1)} collective-permute-done((f32[7,512,128]{2,1,0:T(8,128)S(1)}, f32[7,512,128]{2,1,0:T(8,128)S(1)}, u32[]{:S(2)}, u32[]{:S(2)}) %collective-permute-start) | collective-permute-done | bytes 1835040 | tf_op jit(solution)/shard_map/ppermute | solution.py:300
  12.1 0.0 copy-start.3
  12.1 0.8 copy-done.3
  12.9 0.0 copy-start
  12.9 1.7 %encode.1 = (s16[32,16,896]{2,1,0:T(8,128)(2,1)S(1)}, f32[8,64]{1,0:T(8,128)S(1)}) custom-call(s32[4]{0:T(128)S(1)} %pad_add_fusion.where_ref, f32[7,512,128]{2,1,0:T(8,128)S(1)} %get-tuple-element.11.keep_ref, f32[7,512,128]{2,1,0:T(8,128)S(1)} %collective-permute-done.got_ref, f32[64,64]{1,0:T(8,128)S(1)} %bitcast.13), custom_call_target="tpu_custom_call" | custom-call | tf_op jit(solution)/shard_map/encode/pallas_call | solution.py:301
  14.5 41.8 %all_to_all.15.codes_ref = s16[32,16,896]{2,1,0:T(8,128)(2,1)S(1)} all-to-all(s16[32,16,896]{2,1,0:T(8,128)(2,1)S(1)} %get-tuple-element.13), channel_id=1, replica_groups=mesh['y'=8,'core'=2,'gy'=4,'w'=4,'x'=4] {'y','gy'}, dimensions={0} | all-to-all | bytes 1835008 | tf_op jit(solution)/shard_map/all_to_all | solution.py:312
  56.4 0.0 copy-done
  56.4 2.3 %spectra.1 = (bf16[32,16,896]{2,1,0:T(8,128)(2,1)S(1)}, f32[1,12544]{1,0:T(1,128)}, f32[64,64]{1,0:T(8,128)S(1)}, f32[64,64]{1,0:T(8,128)S(1)}) custom-call(s32[4]{0:T(128)S(1)} %pad_add_fusion.where_ref, s16[32,16,896]{2,1,0:T(8,128)(2,1)S(1)} %all_to_all.15.codes_ref, f32[8,64]{1,0:T(8,128)S(1)} %get-tuple-element.14.partner_ref, f32[64,12544]{1,0:T(8,128)S(1)} %copy-done, ...), custom_call_target="tpu_custom_call" | custom-call | tf_op jit(solution)/shard_map/spectra/pallas_call | solution.py:314
  58.7 30.0 %all_to_all.16.mine_ref = bf16[32,16,896]{2,1,0:T(8,128)(2,1)S(1)} all-to-all(bf16[32,16,896]{2,1,0:T(8,128)(2,1)S(1)} %get-tuple-element.15), channel_id=1, replica_groups=mesh['y'=8,'core'=2,'gy'=4,'w'=4,'x'=4] {'y','gy'}, dimensions={0} | all-to-all | bytes 1835008 | tf_op jit(solution)/shard_map/all_to_all | solution.py:328
  88.7 1.9 %collective-permute-start.1 = (bf16[32,16,896]{2,1,0:T(8,128)(2,1)S(1)}, bf16[32,16,896]{2,1,0:T(8,128)(2,1)S(1)}, u32[]{:S(2)}, u32[]{:S(2)}) collective-permute-start(bf16[32,16,896]{2,1,0:T(8,128)(2,1)S(1)} %all_to_all.16.mine_ref), channel_id=1, source_target_pairs={{0,64},{64,0},{1,65},{65,1},{2,66},{66,2},{3,67},{67,3},{4,68},{68... | collective-permute-start | bytes 2752520 | tf_op jit(solution)/shard_map/ppermute | solution.py:329
  90.6 2.4 %collective-permute-done.1.other_ref = bf16[32,16,896]{2,1,0:T(8,128)(2,1)S(1)} collective-permute-done((bf16[32,16,896]{2,1,0:T(8,128)(2,1)S(1)}, bf16[32,16,896]{2,1,0:T(8,128)(2,1)S(1)}, u32[]{:S(2)}, u32[]{:S(2)}) %collective-permute-start.1) | collective-permute-done | bytes 917536 | tf_op jit(solution)/shard_map/ppermute | solution.py:329
  93.1 0.0 copy-start.4
  93.1 2.5 %project.1 = f32[4,64,128]{2,1,0:T(8,128)S(1)} custom-call(s32[4]{0:T(128)S(1)} %pad_add_fusion.where_ref, bf16[32,16,896]{2,1,0:T(8,128)(2,1)S(1)} %all_to_all.16.mine_ref, bf16[32,16,896]{2,1,0:T(8,128)(2,1)S(1)} %collective-permute-done.1.other_ref, bf16[98,64,128]{2,1,0:T(8,128)(2,1)S(1)} %get-tuple-element.16.dense_ref), custom_call_target="tpu_custom_call" | custom-call | tf_op jit(solution)/shard_map/project/pallas_call | solution.py:332
  95.6 8.4 %all_to_all.17.parts_ref = f32[4,64,128]{2,1,0:T(8,128)S(1)} all-to-all(f32[4,64,128]{2,1,0:T(8,128)S(1)} %project.1), channel_id=1, replica_groups=mesh['y'=8,'core'=2,'gy'=4,'w'=4,'x'=4] {'x'}, dimensions={0} | all-to-all | bytes 262144 | tf_op jit(solution)/shard_map/all_to_all | solution.py:342
  104.0 25.9 %all-gather = f32[256,128]{1,0:T(8,128)S(1)} all-gather(f32[64,128]{1,0:T(8,128)S(1)} %sum.1), channel_id=2, replica_groups=mesh['y'=8,'core'=2,'gy'=4,'w'=4,'x'=4] {'w'}, dimensions={0}, use_global_device_ids=true | all-gather | bytes 163840 | tf_op jit(solution)/shard_map/all_gather | solution.py:351
  129.8 0.0 copy-done.4
  129.8 0.9 loadings.1
  (1 shorter events, 0.0 us)
Async XLA Ops:
  1.4 1.2 copy-start.1
  2.5 0.8 copy-start.2
  3.3 0.7 copy-start.5
  6.4 5.7 %collective-permute-start = (f32[7,512,128]{2,1,0:T(8,128)S(1)}, f32[7,512,128]{2,1,0:T(8,128)S(1)}, u32[]{:S(2)}, u32[]{:S(2)}) collective-permute-start(f32[7,512,128]{2,1,0:T(8,128)S(1)} %get-tuple-element.12), channel_id=1, source_target_pairs={{0,64},{64,0},{1,65},{65,1},{2,66},{66,2},{3,67},{67,3},{4,68},{68... | collective-permute-start | bytes 5505032 | tf_op jit(solution)/shard_map/ppermute | solution.py:300
  12.1 0.8 copy-start.3
  12.9 43.5 %copy-start = (f32[64,12544]{1,0:T(8,128)S(1)}, f32[64,12544]{1,0:T(8,128)}, u32[]{:S(2)}) copy-start(f32[64,12544]{1,0:T(8,128)} %comps_ref.1) | copy-start | bytes 9633796
  88.7 4.4 %collective-permute-start.1 = (bf16[32,16,896]{2,1,0:T(8,128)(2,1)S(1)}, bf16[32,16,896]{2,1,0:T(8,128)(2,1)S(1)}, u32[]{:S(2)}, u32[]{:S(2)}) collective-permute-start(bf16[32,16,896]{2,1,0:T(8,128)(2,1)S(1)} %all_to_all.16.mine_ref), channel_id=1, source_target_pairs={{0,64},{64,0},{1,65},{65,1},{2,66},{66,2},{3,67},{67,3},{4,68},{68... | collective-permute-start | bytes 2752520 | tf_op jit(solution)/shard_map/ppermute | solution.py:329
  93.1 36.8 %copy-start.4 = (f32[8,8,64]{2,1,0:T(8,128)S(1)}, f32[8,8,64]{2,1,0:T(8,128)}, u32[]{:S(2)}) copy-start(f32[8,8,64]{2,1,0:T(8,128)} %param.8) | copy-start | bytes 49156

commit v4 on v3

v4 whole, which is shorter than its diff:
```python
import functools
import jax
import jax.numpy as jnp
from jax import lax
from jax.experimental import pallas as pl
from jax.experimental.pallas import tpu as pltpu
from jax.sharding import Mesh, PartitionSpec as P

tv_edge = 0.1
tv_share = 0.1
LANE = 128
VMEM_LIMIT = 48 * 1024 * 1024
F32 = jnp.float32
BF16 = jnp.bfloat16


def params():
    return pltpu.CompilerParams(vmem_limit_bytes=VMEM_LIMIT)


def vmem():
    return pl.BlockSpec(memory_space=pltpu.VMEM)


def smem():
    return pl.BlockSpec(memory_space=pltpu.SMEM)


def iota(shape, dim):
    return lax.broadcasted_iota(jnp.int32, shape, dim)


def nt(a, b):
    return lax.dot_general(a, b, (((1,), (1,)), ((), ())), preferred_element_type=F32)


LOG_LOW = 3.25
LOG_STEPS = 5950.0
GRAM_SCALE = 64.0
OFFSET = 32768


def encode(value):
    steps = (jnp.log2(jnp.maximum(value, 1.0)) - LOG_LOW) * LOG_STEPS
    code = jnp.where(value > 0.0, jnp.maximum(steps, 0.0) + 1.5, 0.0).astype(jnp.int32)
    return jnp.minimum(code, 65535)


def decode(code):
    steps = code.astype(jnp.int32).astype(F32) + float(OFFSET)
    return jnp.where(steps > 0.0, jnp.exp2((steps - 1.0) * (1.0 / LOG_STEPS) + LOG_LOW), 0.0)


ACROSS = 13
DEPTH = 8
HALO = 4


def place_of(q):
    return divmod(q, ACROSS)


def component_of(row):
    return 8 * (row % 32 // 4) + 4 * (row // 32) + row % 4


def anywhere():
    return pl.BlockSpec(memory_space=pl.ANY)


def scatter_kernel(where_ref, ids_hbm, count_hbm, x_ref, w_ref, keep_ref, send_ref, ids_ref, count_ref, sems):
    copies = [
        pltpu.make_async_copy(ids_hbm, ids_ref, sems.at[0]),
        pltpu.make_async_copy(count_hbm, count_ref, sems.at[1]),
    ]
    for copy in copies:
        copy.start()
    tile_x, slots, tile_y, lane = x_ref.shape
    tile, comps = w_ref.shape
    half_blocks = keep_ref.shape[0]
    core = where_ref[2]
    keep_ref[...] = jnp.zeros_like(keep_ref)
    send_ref[...] = jnp.zeros_like(send_ref)
    w = w_ref[...]
    edges = jnp.concatenate([w[:8], w[tile - 8 :]], axis=0)
    high = edges.astype(BF16).astype(F32)
    mid = (edges - high).astype(BF16).astype(F32)
    pieces = jnp.concatenate([high, mid, edges - high - mid, jnp.zeros_like(edges)], axis=0)
    send_ref[half_blocks] = jnp.concatenate([w, pieces], axis=1).astype(BF16)
    for copy in copies:
        copy.wait()

    def place(s, carry):
        block = ids_ref[s]
        high = block // half_blocks
        at = block - high * half_blocks
        rows_of_slot = x_ref[:, s].astype(F32).reshape(tile, lane).astype(BF16)

        @pl.when(high == core)
        def _():
            keep_ref[at] = rows_of_slot

        @pl.when(high != core)
        def _():
            send_ref[at] = rows_of_slot

        return carry

    lax.fori_loop(0, count_ref[0], place, 0)


def rims(where_ref, w, edges):
    at_first = where_ref[2] == 0
    tile = w.shape[0]
    bottom = jnp.where(at_first, edges[8:], w[tile - 8 :])
    top = jnp.where(at_first, w[:8], edges[:8])
    first = jnp.concatenate([w[8 * i : 8 * i + 1] for i in range(8)], axis=0)
    last = jnp.concatenate([w[8 * i + 7 : 8 * i + 8] for i in range(8)], axis=0)
    return [jnp.concatenate([rim[:4], rim[4:]], axis=1) for rim in (bottom, top, last, first)]


def coarse_part(value):
    return (value * 32768.0 + 0.5).astype(jnp.int32)


def rim_for(i, where_ref, values):
    side, y = where_ref[1], where_ref[3]
    to_y, to_side = divmod(i, 4)
    same_side, same_y = side == to_side, y == to_y
    out = jnp.where(jnp.logical_and(same_side, y + 1 == to_y), values[0], jnp.zeros_like(values[0]))
    out = jnp.where(jnp.logical_and(same_side, y - 1 == to_y), values[1], out)
    out = jnp.where(jnp.logical_and(same_y, side + 1 == to_side), values[2], out)
    return jnp.where(jnp.logical_and(same_y, side - 1 == to_side), values[3], out)


def rim_sources(where_ref, chunks):
    side, core, y = where_ref[1], where_ref[2], where_ref[3]
    out = []
    for from_y, from_side in ((jnp.where(core == 0, y - 1, y + 1), side), (y, side - 1), (y, side + 1)):
        inside = jnp.logical_and(
            jnp.logical_and(from_y >= 0, from_y < chunks // 4), jnp.logical_and(from_side >= 0, from_side < 4)
        )
        out.append((jnp.where(inside, from_y * 4 + from_side, 0), inside))
    return out


def unfold(rows):
    half = rows.shape[1] // 2
    return jnp.concatenate([rows[:, :half], rows[:, half:]], axis=0)


def numer_kernel(where_ref, keep_ref, got_ref, w_ref, codes_ref, edges_ref, wide_ref):
    half_blocks, tile, lane = keep_ref.shape
    comps = w_ref.shape[1]
    chunks = codes_ref.shape[0]
    w = w_ref[...]
    apart = got_ref[half_blocks]
    pieces = apart[:, comps:].astype(F32)
    edges = pieces[:16] + pieces[16:32] + pieces[32:48]
    edges_ref[...] = edges
    w_two = jnp.concatenate([w.astype(BF16), apart[:, :comps]], axis=0)
    pick = jnp.where(iota((comps, comps), 1) == component_of(iota((comps, comps), 0)), 1.0, 0.0).astype(BF16)
    left = nt(pick, w_two).astype(BF16)

    def put(q, value):
        r, j = place_of(q)
        wide_ref[j, pl.ds(r, chunks, stride=DEPTH), :] = value

    def both_tiles(b):
        return jnp.concatenate([keep_ref[b], got_ref[b]], axis=0)

    for b in range(0, half_blocks, 2):
        group = range(b, min(b + 2, half_blocks))
        right = jnp.concatenate([both_tiles(i) for i in group], axis=1)
        product = jnp.dot(left, right, preferred_element_type=F32)
        for i in group:
            for m in range(2):
                put(m * half_blocks + i, product[m * chunks : (m + 1) * chunks, (i - b) * lane : (i - b + 1) * lane])
    gram = jnp.dot(left, w_two, preferred_element_type=F32) * GRAM_SCALE
    put(2 * half_blocks, jnp.concatenate([gram[:chunks], gram[chunks:]], axis=1))
    for q in range(2 * half_blocks + 1, ACROSS * DEPTH):
        put(q, jnp.zeros((chunks, lane), F32))

    rim_values = [coarse_part(rim) for rim in rims(where_ref, w, edges)]
    row = iota((DEPTH, lane), 0)
    halo_row, halo_at = place_of(2 * half_blocks + 1)
    for i in range(chunks):
        rim = rim_for(i, where_ref, rim_values)
        for j in range(ACROSS):
            code = encode(wide_ref[j, i * DEPTH : (i + 1) * DEPTH, :])
            if halo_at <= j < halo_at + HALO:
                code = jnp.where(row == halo_row, rim[j - halo_at : j - halo_at + 1], code)
            codes_ref[i, :, j * lane : (j + 1) * lane] = (code - OFFSET).astype(jnp.int16)


def spectra_kernel(
    where_ref, codes_ref, edges_ref, comps_ref, w_ref, h_all_ref, mine_ref, send_ref, coarse_ref, first_ref, second_ref
):
    lane = LANE
    chunks = codes_ref.shape[0]
    tile, comps = w_ref.shape
    half_blocks = mine_ref.shape[1] // lane
    side, core, y = where_ref[1], where_ref[2], where_ref[3]
    turn = lax.rem(8 - side, 8)
    parts = (first_ref, second_ref)

    def total(j):
        block = slice(j * lane, (j + 1) * lane)
        out = decode(codes_ref[0, :, block])
        for i in range(1, chunks):
            out = out + decode(codes_ref[i, :, block])
        return out

    sums = [total(j) for j in range(ACROSS)]
    gram_row, gram_at = place_of(2 * half_blocks)
    gram = jnp.transpose(sums[gram_at])[:, gram_row : gram_row + 1] * (1.0 / GRAM_SCALE)
    grams = [jnp.broadcast_to(gram[m * comps : (m + 1) * comps], (comps, lane)) for m in range(2)]
    halo_row, halo_at = place_of(2 * half_blocks + 1)
    w = w_ref[...]
    rim_values = [rim - coarse_part(rim).astype(F32) * (1.0 / 32768.0) for rim in rims(where_ref, w, edges_ref[...])]
    rim_low = [rim_for(i, where_ref, rim_values) for i in range(chunks)]
    row = iota((DEPTH, lane), 0)
    for j in range(ACROSS):
        denominators, own_rows = [], []
        for r in range(DEPTH):
            q = r * ACROSS + j
            if q < 2 * half_blocks:
                m, b = divmod(q, half_blocks)
                at = pl.ds(pl.multiple_of((core * half_blocks + b) * lane, lane), lane)
                denominators.append(jnp.sum(comps_ref[:, at] * grams[m], axis=0, keepdims=True))
                group = comps_ref[pl.ds(pl.multiple_of(8 * y, 8), 8), at]
                own_rows.append(pltpu.roll(group, turn, 0)[4 * m : 4 * m + 1])
            else:
                denominators.append(jnp.ones((1, lane), F32))
                own_rows.append(jnp.zeros((1, lane), F32))
        h = jnp.concatenate(own_rows, axis=0) * sums[j] / jnp.concatenate(denominators, axis=0)
        for r in range(DEPTH):
            q = r * ACROSS + j
            if q < 2 * half_blocks:
                m, b = divmod(q, half_blocks)
                parts[m][:, b * lane : (b + 1) * lane] = h[r : r + 1]
        h_low = h.astype(BF16)
        for i in range(chunks):
            if halo_at <= j < halo_at + HALO:
                rim = rim_low[i][j - halo_at : j - halo_at + 1]
                h_low = jnp.where(row == halo_row, rim, h).astype(BF16)
            h_all_ref[i, :, j * lane : (j + 1) * lane] = h_low
    mine_ref[...] = jnp.where(core == 0, first_ref[...], second_ref[...])
    send_ref[...] = jnp.where(core == 0, second_ref[...], first_ref[...])

    for n, (source, inside) in enumerate(rim_sources(where_ref, chunks)):
        rows = [
            codes_ref[source, :, j * lane : (j + 1) * lane].astype(jnp.int32)[halo_row : halo_row + 1]
            for j in range(halo_at, halo_at + HALO)
        ]
        value = (jnp.concatenate(rows, axis=0) + OFFSET).astype(F32) * (1.0 / 32768.0)
        coarse_ref[8 * n : 8 * n + 8, :] = jnp.where(inside, unfold(value), 0.0)


def smooth(tv_strength, where_ref, outer, before, after, edges, w_ref, tv_num_ref, tv_den_ref):
    comps = w_ref.shape[1]
    at_first = where_ref[2] == 0
    above = jnp.where(at_first, outer, edges[8:])
    below = jnp.where(at_first, edges[:8], outer)
    spot = iota((8, comps), 0)
    rows = [w_ref[8 * i : 8 * i + 8, :] for i in range(8)]
    for i in range(8):
        centre = rows[i]
        beside = (
            rows[i + 1] if i < 7 else below,
            rows[i - 1] if i > 0 else above,
            jnp.where(spot == 7, after[i : i + 1], pltpu.roll(centre, 7, 0)),
            jnp.where(spot == 0, before[i : i + 1], pltpu.roll(centre, 1, 0)),
        )
        num = jnp.zeros_like(centre)
        den = jnp.zeros_like(centre)
        for q in beside:
            edge_weight = 1.0 / (jnp.abs(centre - q) + tv_edge)
            num = num + edge_weight * q
            den = den + edge_weight * centre
        tv_num_ref[8 * i : 8 * i + 8, :] = tv_strength * num
        tv_den_ref[8 * i : 8 * i + 8, :] = tv_strength * den


def project_kernel(
    tv_strength, where_ref, h_ref, keep_ref, got_ref, coarse_ref, edges_ref, w_ref, out_ref, tv_num_ref, tv_den_ref, wide_ref
):
    half_blocks, tile, lane = keep_ref.shape
    chunks = h_ref.shape[0]
    comps = w_ref.shape[1]
    copies = out_ref.shape[0]
    core = where_ref[2]
    for j in range(ACROSS):
        block = h_ref[:, :, j * lane : (j + 1) * lane]
        wide_ref[j] = block.astype(F32).reshape(chunks * DEPTH, lane)

    def spectrum(b):
        parts = []
        for m in range(2):
            r, j = place_of(m * half_blocks + b)
            parts.append(wide_ref[j, pl.ds(r, chunks, stride=DEPTH), :])
        return jnp.concatenate(parts, axis=0).astype(BF16)

    total = jnp.zeros((2 * tile + comps, comps), F32)
    for b in range(0, half_blocks, 2):
        group = range(b, min(b + 2, half_blocks))
        h = jnp.concatenate([spectrum(i) for i in group], axis=1)
        own = jnp.concatenate([keep_ref[i] for i in group], axis=1)
        partner = jnp.concatenate([got_ref[i] for i in group], axis=1)
        total = total + nt(jnp.concatenate([own, partner, h], axis=0), h)
    name = component_of(iota((comps, lane), 0))
    to_low = jnp.where(iota((comps, lane), 1) == name, 1.0, 0.0)
    to_high = jnp.where(iota((comps, lane), 1) == name + comps, 1.0, 0.0)
    exact = dict(preferred_element_type=F32, precision=lax.Precision.HIGHEST)
    spec = lax.dot_general(to_low, total[2 * tile :], (((0,), (0,)), ((), ())), **exact)[:comps]
    spec = jnp.dot(spec, to_high, **exact)
    cross = jnp.dot(total[: 2 * tile], to_low, **exact)
    for to_core in range(2):
        both = spec + jnp.where(core == to_core, cross[:tile], cross[tile:])
        for i in range(copies // 2):
            out_ref[to_core * (copies // 2) + i] = both

    halo_row, halo_at = place_of(2 * half_blocks + 1)
    halos = []
    for n, (source, inside) in enumerate(rim_sources(where_ref, chunks)):
        rows = [
            h_ref[source, :, j * lane : (j + 1) * lane].astype(F32)[halo_row : halo_row + 1]
            for j in range(halo_at, halo_at + HALO)
        ]
        fine = unfold(jnp.concatenate(rows, axis=0))
        halos.append(jnp.where(inside, coarse_ref[8 * n : 8 * n + 8, :] + fine, 0.0))
    smooth(tv_strength, where_ref, *halos, edges_ref[...], w_ref, tv_num_ref, tv_den_ref)


def sum_kernel(parts_ref, out_ref):
    block = parts_ref[0]
    for i in range(1, parts_ref.shape[0]):
        block = block + parts_ref[i]
    out_ref[...] = block


def loadings_kernel(where_ref, parts_ref, w_ref, tv_num_ref, tv_den_ref, mine_ref, got_ref, out_ref, h_ref):
    comps = w_ref.shape[1]
    half_bins = mine_ref.shape[1]
    at_first = where_ref[2] == 0
    mine, got = mine_ref[...], got_ref[...]
    h_ref[:, :half_bins] = jnp.where(at_first, mine, got)
    h_ref[:, half_bins:] = jnp.where(at_first, got, mine)
    block = parts_ref[0]
    for i in range(1, parts_ref.shape[0]):
        block = block + parts_ref[i]
    w = w_ref[...]
    fitted = jnp.dot(w, block, preferred_element_type=F32, precision=lax.Precision.HIGHEST)
    fitted = pltpu.roll(fitted, comps, 1)[:, :comps]
    out_ref[...] = w * (block[:, :comps] + tv_num_ref[...]) / (fitted + tv_den_ref[...])


def call(kernel, name, outs, in_specs, scratch=()):
    return pl.pallas_call(
        kernel,
        out_shape=tuple(jax.ShapeDtypeStruct(shape, dtype) for shape, dtype in outs),
        in_specs=in_specs,
        out_specs=(vmem(),) * len(outs),
        scratch_shapes=scratch,
        compiler_params=params(),
        name=name,
    )


def local(spectra, block_ids, counts, loadings, components):
    tile_x, tile_y, slot_count, lane = spectra.shape
    tile = tile_x * tile_y
    comps = loadings.shape[2]
    slab_bins = components.shape[1]
    half_blocks = slab_bins // lane // 2
    half_bins = half_blocks * lane
    width = ACROSS * lane
    spots = [lax.axis_index(axis) for axis in (("y", "core"), "gy", "core", "y")]
    here = jnp.stack(spots).astype(jnp.int32)
    peers = ("y", "gy")
    chunks = lax.axis_size(peers)
    pixels = spectra.transpose(0, 2, 1, 3)
    w = loadings.reshape(tile, comps)
    swap = [(0, 1), (1, 0)]
    tv_strength = tv_share * slab_bins * lax.axis_size(("w", "x"))

    keep, send = call(
        scatter_kernel,
        "scatter",
        [((half_blocks, tile, lane), BF16), ((half_blocks + 1, tile, lane), BF16)],
        [smem(), anywhere(), anywhere(), vmem(), vmem()],
        [pltpu.SMEM((slot_count,), jnp.int32), pltpu.SMEM((1,), jnp.int32), pltpu.SemaphoreType.DMA((2,))],
    )(here, block_ids.reshape(slot_count), counts.reshape(1), pixels, w)
    got = lax.ppermute(send, "core", swap)
    codes, edges = call(
        numer_kernel,
        "numer",
        [((chunks, DEPTH, width), jnp.int16), ((16, comps), F32)],
        [smem(), vmem(), vmem(), vmem()],
        [pltpu.VMEM((ACROSS, chunks * DEPTH, lane), F32)],
    )(here, keep, got, w)
    codes = lax.all_to_all(codes, peers, 0, 0, tiled=True)
    h_all, h_mine, h_send, coarse = call(
        spectra_kernel,
        "spectra",
        [((chunks, DEPTH, width), BF16), ((1, half_bins), F32), ((1, half_bins), F32), ((24, comps), F32)],
        [smem(), vmem(), vmem(), vmem(), vmem()],
        [pltpu.VMEM((1, half_bins), F32)] * 2,
    )(here, codes, edges, components, w)
    h_got = lax.ppermute(h_send, "core", swap)
    h_all = lax.all_to_all(h_all, peers, 0, 0, tiled=True)
    copies = lax.axis_size(("core", "x"))
    both, tv_num, tv_den = call(
        functools.partial(project_kernel, tv_strength),
        "project",
        [((copies, tile, 2 * comps), F32), ((tile, comps), F32), ((tile, comps), F32)],
        [smem()] + [vmem()] * 6,
        [pltpu.VMEM((ACROSS, chunks * DEPTH, lane), F32)],
    )(here, h_all, keep, got, coarse, edges, w)
    both = lax.all_to_all(both, ("core", "x"), 0, 0, tiled=True)
    (both,) = call(sum_kernel, "sum", [((tile, 2 * comps), F32)], [vmem()])(both)
    both = lax.all_gather(both, "w", axis=0)
    w_next, h_next = call(
        loadings_kernel,
        "loadings",
        [((tile, comps), F32), ((1, slab_bins), F32)],
        [smem()] + [vmem()] * 6,
    )(here, both, w, tv_num, tv_den, h_mine, h_got)
    return (w_next.reshape(tile_x, tile_y, comps), h_next)


def solution(mesh):
    gx, gy, mz = mesh.devices.shape
    fine = Mesh(mesh.devices.reshape(gx // 2, 2, gy, 4, mz // 4), ("y", "core", "gy", "w", "x"))
    rows, slabs = ("y", "core"), ("w", "x")
    in_specs = (
        P(rows, "gy", slabs, None),
        P(rows, "gy", slabs),
        P(rows, "gy", slabs),
        P(rows, "gy", None),
        P(None, slabs),
    )
    out_specs = (P(rows, "gy", None), P(("y", "core", "gy"), slabs))
    return jax.shard_map(local, mesh=fine, in_specs=in_specs, out_specs=out_specs, check_vma=False)
```

time: 131 us -> 124 us (0.947)
  blocking collectives: 106 us -> 94 us
  starting transfers between devices: 3.83 us -> 8.77 us
    all_to_all x2 -> x1, blocking collectives: 38.4 us -> 28.7 us  [local(): h_all = lax.all_to_all(h_all, peers, 0, 0, tiled=True)]
    all_to_all x0 -> x1, waiting for transfers between devices: none -> 4.51 us  [local(): both = lax.all_to_all(both, ('core', 'x'), 0, 0, tiled=True)]
    all_to_all x0 -> x1, starting transfers between devices: none -> 3.41 us  [local(): both = lax.all_to_all(both, ('core', 'x'), 0, 0, tiled=True)]
    ppermute x1, waiting for transfers between devices: 2.44 us -> 0.01 us  [local(): h_got = lax.ppermute(h_send, 'core', swap)]
    ppermute x1, waiting for transfers between devices: 3.75 us -> 1.94 us  [local(): got = lax.ppermute(send, 'core', swap)]
    all_gather x1, blocking collectives: 25.9 us -> 24.3 us  [local(): both = lax.all_gather(both, 'w', axis=0)]
  transfers between devices with their start and end apart: 2 -> 3, of which waited for: 2 -> 2; matrix products, arithmetic and copies ran while one was open for 0% -> 0% of each run, Pallas kernels for 0% -> 0%
where the time goes in v4:
time: 124 us
  blocking collectives  94 us (76%)
  Pallas kernels  9.45 us (8%)
  starting transfers between devices  8.77 us (7%)
  waiting for transfers between devices  6.45 us (5%)
  local copies, waits for them, and re-layouts  3.42 us (3%)
  between operations  1.5 us (1%)
    all_to_all x1, blocking collectives, local(): codes = lax.all_to_all(codes, peers, 0, 0, tiled=True)  41 us
    all_to_all x1, blocking collectives, local(): h_all = lax.all_to_all(h_all, peers, 0, 0, tiled=True)  28.7 us
    all_gather x1, blocking collectives, local(): both = lax.all_gather(both, 'w', axis=0)  24.3 us
    all_to_all x1, waiting for transfers between devices, local(): both = lax.all_to_all(both, ('core', 'x'), 0, 0, tiled=True)  4.51 us
    unnamed x12, local copies, waits for them, and re-layouts  3.42 us
    all_to_all x1, starting transfers between devices, local(): both = lax.all_to_all(both, ('core', 'x'), 0, 0, tiled=True)  3.41 us
    ppermute x1, starting transfers between devices, local(): got = lax.ppermute(send, 'core', swap)  3.04 us
    pallas_call x1, Pallas kernels, local(): call(functools.partial(project_kernel, tv_strength), 'project', [((copies...  2.73 us
  transfers between devices with their start and end apart: 3, of which 2 were waited for; matrix products, arithmetic and copies ran while one was open for 0% of the time, Pallas kernels for 0%

profile of v4, /device:TPU:8, one launch (start us, length us, event | category | flops | bytes accessed | tf_op | source)
XLA Modules:
  0.0 123.7 jit_solution(16919490347748395653)
XLA Ops:
  0.6 0.0 copy-start
  1.4 0.1 pad_add_fusion.where_ref
  1.5 0.0 copy-start.1
  1.5 1.2 %copy-done.1 = bf16[8,8,52,128]{3,1,2,0:T(8,128)(2,1)S(1)} copy-done((bf16[8,8,52,128]{3,1,2,0:T(8,128)(2,1)S(1)}, bf16[8,8,52,128]{3,1,2,0:T(8,128)(2,1)}, u32[]{:S(2)}) %copy-start.1) | copy-done | bytes 851992
  2.8 0.0 copy-start.2
  2.8 0.8 copy-done.2
  3.5 0.0 copy-start.5
  3.5 0.7 copy-done.5
  4.2 1.3 %scatter.1 = (bf16[49,64,128]{2,1,0:T(8,128)(2,1)S(1)}, bf16[50,64,128]{2,1,0:T(8,128)(2,1)S(1)}) custom-call(s32[4]{0:T(128)S(1)} %pad_add_fusion.where_ref, s32[52]{0:T(128)S(1)} %bitcast.18, s32[1]{0:T(128)} %bitcast.10.count_hbm, bf16[8,52,8,128]{3,2,1,0:T(8,128)(2,1)S(1)} %bitcast.11, f32[64,64]{1,0:T(8,128)S(1)} %bitcast.12), custom_call_target="tpu_custom_call" | custom-call | tf_op jit(solution)/shard_map/scatter/pallas_call | solution.py:387
  5.5 3.0 %collective-permute-start = (bf16[50,64,128]{2,1,0:T(8,128)(2,1)S(1)}, bf16[50,64,128]{2,1,0:T(8,128)(2,1)S(1)}, u32[]{:S(2)}, u32[]{:S(2)}) collective-permute-start(bf16[50,64,128]{2,1,0:T(8,128)(2,1)S(1)} %get-tuple-element.16), channel_id=1, source_target_pairs={{0,64},{64,0},{1,65},{65,1},{2,66},{66,2},{3,67},{67,3},{4,68},{68... | collective-permute-start | bytes 2457608 | tf_op jit(solution)/shard_map/ppermute | solution.py:394
  8.5 1.9 %collective-permute-done.got_ref = bf16[50,64,128]{2,1,0:T(8,128)(2,1)S(1)} collective-permute-done((bf16[50,64,128]{2,1,0:T(8,128)(2,1)S(1)}, bf16[50,64,128]{2,1,0:T(8,128)(2,1)S(1)}, u32[]{:S(2)}, u32[]{:S(2)}) %collective-permute-start) | collective-permute-done | bytes 819232 | tf_op jit(solution)/shard_map/ppermute | solution.py:394
  10.5 0.0 copy-start.3
  10.5 0.8 copy-done.3
  11.2 2.1 %numer.1 = (s16[32,8,1664]{2,1,0:T(8,128)(2,1)S(1)}, f32[16,64]{1,0:T(8,128)S(1)}) custom-call(s32[4]{0:T(128)S(1)} %pad_add_fusion.where_ref, bf16[49,64,128]{2,1,0:T(8,128)(2,1)S(1)} %get-tuple-element.15.keep_ref, bf16[50,64,128]{2,1,0:T(8,128)(2,1)S(1)} %collective-permute-done.got_ref, f32[64,64]{1,0:T(8,128)S(1)} %bitcast.13), custom_call_target="tpu_custom_call" | custom-call | tf_op jit(solution)/shard_map/numer/pallas_call | solution.py:395
  13.4 41.0 %all_to_all.15.codes_ref = s16[32,8,1664]{2,1,0:T(8,128)(2,1)S(1)} all-to-all(s16[32,8,1664]{2,1,0:T(8,128)(2,1)S(1)} %get-tuple-element.17), channel_id=1, replica_groups=mesh['y'=8,'core'=2,'gy'=4,'w'=4,'x'=4] {'y','gy'}, dimensions={0} | all-to-all | bytes 1703936 | tf_op jit(solution)/shard_map/all_to_all | solution.py:402
  54.4 0.0 copy-start.4
  54.4 0.0 copy-done
  54.4 1.9 %spectra.1 = (bf16[32,8,1664]{2,1,0:T(8,128)(2,1)S(1)}, f32[1,6272]{1,0:T(1,128)S(1)}, f32[1,6272]{1,0:T(1,128)S(1)}, f32[24,64]{1,0:T(8,128)S(1)}) custom-call(s32[4]{0:T(128)S(1)} %pad_add_fusion.where_ref, s16[32,8,1664]{2,1,0:T(8,128)(2,1)S(1)} %all_to_all.15.codes_ref, f32[16,64]{1,0:T(8,128)S(1)} %get-tuple-element.18.edges_ref, ...), custom_call_target="tpu_custom_call" | custom-call | tf_op jit(solution)/shard_map/spectra/pallas_call | solution.py:403
  56.3 28.7 %all_to_all.16.h_ref = bf16[32,8,1664]{2,1,0:T(8,128)(2,1)S(1)} all-to-all(bf16[32,8,1664]{2,1,0:T(8,128)(2,1)S(1)} %get-tuple-element.19), channel_id=1, replica_groups=mesh['y'=8,'core'=2,'gy'=4,'w'=4,'x'=4] {'y','gy'}, dimensions={0} | all-to-all | bytes 1703936 | tf_op jit(solution)/shard_map/all_to_all | solution.py:411
  85.0 0.0 copy-done.4
  85.0 2.7 %project.1 = (f32[8,64,128]{2,1,0:T(8,128)}, f32[64,64]{1,0:T(8,128)S(1)}, f32[64,64]{1,0:T(8,128)S(1)}) custom-call(s32[4]{0:T(128)S(1)} %pad_add_fusion.where_ref, bf16[32,8,1664]{2,1,0:T(8,128)(2,1)S(1)} %all_to_all.16.h_ref, bf16[49,64,128]{2,1,0:T(8,128)(2,1)S(1)} %get-tuple-element.15.keep_ref, bf16[50,64,128]{2,1,0:T(8,128)(2,1)S(1)} %collective-permute-done.got_ref, ...), custom_call_target="tpu_custom_call" | custom-call | tf_op jit(solution)/shard_map/project/pallas_call | solution.py:413
  87.7 3.4 %all-to-all-start.2 = ((f32[8,64,128]{2,1,0:T(8,128)}), f32[8,64,128]{2,1,0:T(8,128)S(1)}, u32[]{:S(2)}, u32[]{:S(2)}) async-start(f32[8,64,128]{2,1,0:T(8,128)} %get-tuple-element.21), calls=%async_computation.2 | async-start | bytes 524288 | tf_op jit(solution)/shard_map/all_to_all | solution.py:420
  91.1 2.3 %collective-permute-start.1 = (f32[1,6272]{1,0:T(1,128)S(1)}, f32[1,6272]{1,0:T(1,128)S(1)}, u32[]{:S(2)}, u32[]{:S(2)}) collective-permute-start(f32[1,6272]{1,0:T(1,128)S(1)} %get-tuple-element.25), channel_id=1, source_target_pairs={{0,64},{64,0},{1,65},{65,1},{2,66},{66,2},{3,67},{67,3},{4,68},{68... | collective-permute-start | bytes 75272 | tf_op jit(solution)/shard_map/ppermute | solution.py:410
  93.4 4.5 %all-to-all-done.2.parts_ref = f32[8,64,128]{2,1,0:T(8,128)S(1)} async-done(((f32[8,64,128]{2,1,0:T(8,128)}), f32[8,64,128]{2,1,0:T(8,128)S(1)}, u32[]{:S(2)}, u32[]{:S(2)}) %all-to-all-start.2) | async-done | bytes 262176 | tf_op jit(solution)/shard_map/all_to_all | solution.py:420
  98.0 24.3 %all-gather = f32[256,128]{1,0:T(8,128)S(1)} all-gather(f32[64,128]{1,0:T(8,128)S(1)} %sum.1), channel_id=2, replica_groups=mesh['y'=8,'core'=2,'gy'=4,'w'=4,'x'=4] {'w'}, dimensions={0}, use_global_device_ids=true | all-gather | bytes 163840 | tf_op jit(solution)/shard_map/all_gather | solution.py:422
  122.3 0.0 collective-permute-done.1.got_ref
  122.3 1.4 %loadings.1 = (f32[64,64]{1,0:T(8,128)}, f32[1,12544]{1,0:T(1,128)}) custom-call(s32[4]{0:T(128)S(1)} %pad_add_fusion.where_ref, f32[4,64,128]{2,1,0:T(8,128)S(1)} %bitcast.17, f32[64,64]{1,0:T(8,128)S(1)} %bitcast.16, f32[64,64]{1,0:T(8,128)S(1)} %get-tuple-element.22.tv_num_ref, f32[64,64]{1,0:T(8,128)S(1)} %get-tuple-element.23.tv_den_ref, ...), custom_call_target="tpu_custom_call" | custom-call | tf_op jit(solution)/shard_map/loadings/pallas_call | solution.py:423
  (1 shorter events, 0.0 us)
Async XLA Ops:
  0.6 53.8 %copy-start = (f32[64,12544]{1,0:T(8,128)S(1)}, f32[64,12544]{1,0:T(8,128)}, u32[]{:S(2)}) copy-start(f32[64,12544]{1,0:T(8,128)} %comps_ref.1) | copy-start | bytes 9633796
  1.5 1.2 %copy-start.1 = (bf16[8,8,52,128]{3,1,2,0:T(8,128)(2,1)S(1)}, bf16[8,8,52,128]{3,1,2,0:T(8,128)(2,1)}, u32[]{:S(2)}) copy-start(bf16[8,8,52,128]{3,1,2,0:T(8,128)(2,1)} %param.5) | copy-start | bytes 2555908
  2.8 0.8 copy-start.2
  3.5 0.7 copy-start.5
  5.5 5.0 %collective-permute-start = (bf16[50,64,128]{2,1,0:T(8,128)(2,1)S(1)}, bf16[50,64,128]{2,1,0:T(8,128)(2,1)S(1)}, u32[]{:S(2)}, u32[]{:S(2)}) collective-permute-start(bf16[50,64,128]{2,1,0:T(8,128)(2,1)S(1)} %get-tuple-element.16), channel_id=1, source_target_pairs={{0,64},{64,0},{1,65},{65,1},{2,66},{66,2},{3,67},{67,3},{4,68},{68... | collective-permute-start | bytes 2457608 | tf_op jit(solution)/shard_map/ppermute | solution.py:394
  10.5 0.8 copy-start.3
  54.4 30.6 %copy-start.4 = (f32[8,8,64]{2,1,0:T(8,128)S(1)}, f32[8,8,64]{2,1,0:T(8,128)}, u32[]{:S(2)}) copy-start(f32[8,8,64]{2,1,0:T(8,128)} %param.8) | copy-start | bytes 49156
  87.7 10.3 %all-to-all-start.2 = ((f32[8,64,128]{2,1,0:T(8,128)}), f32[8,64,128]{2,1,0:T(8,128)S(1)}, u32[]{:S(2)}, u32[]{:S(2)}) async-start(f32[8,64,128]{2,1,0:T(8,128)} %get-tuple-element.21), calls=%async_computation.2 | async-start | bytes 524288 | tf_op jit(solution)/shard_map/all_to_all | solution.py:420
  91.1 31.2 %collective-permute-start.1 = (f32[1,6272]{1,0:T(1,128)S(1)}, f32[1,6272]{1,0:T(1,128)S(1)}, u32[]{:S(2)}, u32[]{:S(2)}) collective-permute-start(f32[1,6272]{1,0:T(1,128)S(1)} %get-tuple-element.25), channel_id=1, source_target_pairs={{0,64},{64,0},{1,65},{65,1},{2,66},{66,2},{3,67},{67,3},{4,68},{68... | collective-permute-start | bytes 75272 | tf_op jit(solution)/shard_map/ppermute | solution.py:410

commit v5 on v4

--- a/solution.py
+++ b/solution.py
@@ -41,14 +41,13 @@
 
 
 def encode(value):
-    steps = (jnp.log2(jnp.maximum(value, 1.0)) - LOG_LOW) * LOG_STEPS
-    code = jnp.where(value > 0.0, jnp.maximum(steps, 0.0) + 1.5, 0.0).astype(jnp.int32)
-    return jnp.minimum(code, 65535)
+    steps = jnp.log2(jnp.maximum(value, 1.0)) * LOG_STEPS + (1.5 - LOG_LOW * LOG_STEPS)
+    return jnp.maximum(steps, 0.0).astype(jnp.int32)
 
 
 def decode(code):
     steps = code.astype(jnp.int32).astype(F32) + float(OFFSET)
-    return jnp.where(steps > 0.0, jnp.exp2((steps - 1.0) * (1.0 / LOG_STEPS) + LOG_LOW), 0.0)
+    return jnp.where(steps > 0.0, jnp.exp2(steps * (1.0 / LOG_STEPS) + (LOG_LOW - 1.0 / LOG_STEPS)), 0.0)
 
 
 ACROSS = 13
@@ -68,45 +67,76 @@
     return pl.BlockSpec(memory_space=pl.ANY)
 
 
-def scatter_kernel(where_ref, ids_hbm, count_hbm, x_ref, w_ref, keep_ref, send_ref, ids_ref, count_ref, sems):
-    copies = [
-        pltpu.make_async_copy(ids_hbm, ids_ref, sems.at[0]),
-        pltpu.make_async_copy(count_hbm, count_ref, sems.at[1]),
-    ]
+def fetch(pairs, sems):
+    copies = [pltpu.make_async_copy(source, target, sems.at[i]) for i, (source, target) in enumerate(pairs)]
     for copy in copies:
         copy.start()
-    tile_x, slots, tile_y, lane = x_ref.shape
-    tile, comps = w_ref.shape
+    return copies
+
+
+def scatter_kernel(where_ref, count_ref, ids_hbm, w_hbm, x_hbm, keep_ref, send_ref, w_ref, ids_ref, x_ref, sems):
+    copies = fetch([(x_hbm, x_ref), (ids_hbm, ids_ref), (w_hbm, w_ref)], sems)
+    tile_x, _, tile_y, lane = x_ref.shape
+    tile = tile_x * tile_y
     half_blocks = keep_ref.shape[0]
     core = where_ref[2]
     keep_ref[...] = jnp.zeros_like(keep_ref)
     send_ref[...] = jnp.zeros_like(send_ref)
+    for copy in copies:
+        copy.wait()
     w = w_ref[...]
     edges = jnp.concatenate([w[:8], w[tile - 8 :]], axis=0)
     high = edges.astype(BF16).astype(F32)
     mid = (edges - high).astype(BF16).astype(F32)
     pieces = jnp.concatenate([high, mid, edges - high - mid, jnp.zeros_like(edges)], axis=0)
     send_ref[half_blocks] = jnp.concatenate([w, pieces], axis=1).astype(BF16)
-    for copy in copies:
-        copy.wait()
 
     def place(s, carry):
         block = ids_ref[s]
-        high = block // half_blocks
-        at = block - high * half_blocks
+        half = block // half_blocks
+        at = block - half * half_blocks
         rows_of_slot = x_ref[:, s].astype(F32).reshape(tile, lane).astype(BF16)
 
-        @pl.when(high == core)
+        @pl.when(half == core)
         def _():
             keep_ref[at] = rows_of_slot
 
-        @pl.when(high != core)
+        @pl.when(half != core)
         def _():
             send_ref[at] = rows_of_slot
 
         return carry
 
     lax.fori_loop(0, count_ref[0], place, 0)
+
+
+def put(wide_ref, q, value):
+    r, j = place_of(q)
+    wide_ref[j, pl.ds(r, value.shape[0], stride=DEPTH), :] = value
+
+
+def numerators(w_low, dense_ref, half_blocks, wide_ref):
+    comps = w_low.shape[1]
+    chunks = wide_ref.shape[1] // DEPTH
+    lane = LANE
+    pick = jnp.where(iota((comps, comps), 1) == component_of(iota((comps, comps), 0)), 1.0, 0.0).astype(BF16)
+    left = nt(pick, w_low).astype(BF16)
+    for b in range(0, half_blocks, 2):
+        group = range(b, min(b + 2, half_blocks))
+        right = jnp.concatenate([dense_ref[i] for i in group], axis=1)
+        product = jnp.dot(left, right, preferred_element_type=F32)
+        for i in group:
+            for m in range(2):
+                part = product[m * chunks : (m + 1) * chunks, (i - b) * lane : (i - b + 1) * lane]
+                put(wide_ref, m * half_blocks + i, part)
+    gram = jnp.dot(left, w_low, preferred_element_type=F32) * GRAM_SCALE
+    put(wide_ref, 2 * half_blocks, jnp.concatenate([gram[:chunks], gram[chunks:]], axis=1))
+    for q in range(2 * half_blocks + 1, ACROSS * DEPTH):
+        put(wide_ref, q, jnp.zeros((chunks, lane), F32))
+
+
+def own_kernel(keep_ref, w_ref, own_ref):
+    numerators(w_ref[...].astype(BF16), keep_ref, keep_ref.shape[0], own_ref)
 
 
 def rims(where_ref, w, edges):
@@ -149,45 +179,25 @@
     return jnp.concatenate([rows[:, :half], rows[:, half:]], axis=0)
 
 
-def numer_kernel(where_ref, keep_ref, got_ref, w_ref, codes_ref, edges_ref, wide_ref):
-    half_blocks, tile, lane = keep_ref.shape
+def numer_kernel(where_ref, own_ref, got_ref, w_ref, codes_ref, edges_ref, wide_ref):
+    half_blocks = got_ref.shape[0] - 1
+    lane = LANE
     comps = w_ref.shape[1]
     chunks = codes_ref.shape[0]
-    w = w_ref[...]
     apart = got_ref[half_blocks]
     pieces = apart[:, comps:].astype(F32)
     edges = pieces[:16] + pieces[16:32] + pieces[32:48]
     edges_ref[...] = edges
-    w_two = jnp.concatenate([w.astype(BF16), apart[:, :comps]], axis=0)
-    pick = jnp.where(iota((comps, comps), 1) == component_of(iota((comps, comps), 0)), 1.0, 0.0).astype(BF16)
-    left = nt(pick, w_two).astype(BF16)
-
-    def put(q, value):
-        r, j = place_of(q)
-        wide_ref[j, pl.ds(r, chunks, stride=DEPTH), :] = value
-
-    def both_tiles(b):
-        return jnp.concatenate([keep_ref[b], got_ref[b]], axis=0)
-
-    for b in range(0, half_blocks, 2):
-        group = range(b, min(b + 2, half_blocks))
-        right = jnp.concatenate([both_tiles(i) for i in group], axis=1)
-        product = jnp.dot(left, right, preferred_element_type=F32)
-        for i in group:
-            for m in range(2):
-                put(m * half_blocks + i, product[m * chunks : (m + 1) * chunks, (i - b) * lane : (i - b + 1) * lane])
-    gram = jnp.dot(left, w_two, preferred_element_type=F32) * GRAM_SCALE
-    put(2 * half_blocks, jnp.concatenate([gram[:chunks], gram[chunks:]], axis=1))
-    for q in range(2 * half_blocks + 1, ACROSS * DEPTH):
-        put(q, jnp.zeros((chunks, lane), F32))
-
-    rim_values = [coarse_part(rim) for rim in rims(where_ref, w, edges)]
+    numerators(apart[:, :comps], got_ref, half_blocks, wide_ref)
+
+    rim_values = [coarse_part(rim) for rim in rims(where_ref, w_ref[...], edges)]
     row = iota((DEPTH, lane), 0)
     halo_row, halo_at = place_of(2 * half_blocks + 1)
     for i in range(chunks):
         rim = rim_for(i, where_ref, rim_values)
+        at = slice(i * DEPTH, (i + 1) * DEPTH)
         for j in range(ACROSS):
-            code = encode(wide_ref[j, i * DEPTH : (i + 1) * DEPTH, :])
+            code = encode(own_ref[j, at, :] + wide_ref[j, at, :])
             if halo_at <= j < halo_at + HALO:
                 code = jnp.where(row == halo_row, rim[j - halo_at : j - halo_at + 1], code)
             codes_ref[i, :, j * lane : (j + 1) * lane] = (code - OFFSET).astype(jnp.int16)
@@ -282,12 +292,10 @@
         tv_den_ref[8 * i : 8 * i + 8, :] = tv_strength * den
 
 
-def project_kernel(
-    tv_strength, where_ref, h_ref, keep_ref, got_ref, coarse_ref, edges_ref, w_ref, out_ref, tv_num_ref, tv_den_ref, wide_ref
-):
+def project_kernel(where_ref, h_ref, keep_ref, got_ref, out_ref, wide_ref):
     half_blocks, tile, lane = keep_ref.shape
     chunks = h_ref.shape[0]
-    comps = w_ref.shape[1]
+    comps = 2 * chunks
     copies = out_ref.shape[0]
     core = where_ref[2]
     for j in range(ACROSS):
@@ -320,6 +328,10 @@
         for i in range(copies // 2):
             out_ref[to_core * (copies // 2) + i] = both
 
+
+def smooth_kernel(tv_strength, half_blocks, where_ref, h_ref, coarse_ref, edges_ref, w_ref, tv_num_ref, tv_den_ref):
+    lane = LANE
+    chunks = h_ref.shape[0]
     halo_row, halo_at = place_of(2 * half_blocks + 1)
     halos = []
     for n, (source, inside) in enumerate(rim_sources(where_ref, chunks)):
@@ -339,13 +351,8 @@
     out_ref[...] = block
 
 
-def loadings_kernel(where_ref, parts_ref, w_ref, tv_num_ref, tv_den_ref, mine_ref, got_ref, out_ref, h_ref):
+def loadings_kernel(parts_ref, w_ref, tv_num_ref, tv_den_ref, out_ref):
     comps = w_ref.shape[1]
-    half_bins = mine_ref.shape[1]
-    at_first = where_ref[2] == 0
-    mine, got = mine_ref[...], got_ref[...]
-    h_ref[:, :half_bins] = jnp.where(at_first, mine, got)
-    h_ref[:, half_bins:] = jnp.where(at_first, got, mine)
     block = parts_ref[0]
     for i in range(1, parts_ref.shape[0]):
         block = block + parts_ref[i]
@@ -355,13 +362,14 @@
     out_ref[...] = w * (block[:, :comps] + tv_num_ref[...]) / (fitted + tv_den_ref[...])
 
 
-def call(kernel, name, outs, in_specs, scratch=()):
+def call(kernel, name, outs, in_specs, scratch=(), out_specs=None, cost=None):
     return pl.pallas_call(
         kernel,
         out_shape=tuple(jax.ShapeDtypeStruct(shape, dtype) for shape, dtype in outs),
         in_specs=in_specs,
-        out_specs=(vmem(),) * len(outs),
+        out_specs=out_specs or (vmem(),) * len(outs),
         scratch_shapes=scratch,
+        cost_estimate=cost,
         compiler_params=params(),
         name=name,
     )
@@ -379,26 +387,41 @@
     here = jnp.stack(spots).astype(jnp.int32)
     peers = ("y", "gy")
     chunks = lax.axis_size(peers)
-    pixels = spectra.transpose(0, 2, 1, 3)
     w = loadings.reshape(tile, comps)
     swap = [(0, 1), (1, 0)]
     tv_strength = tv_share * slab_bins * lax.axis_size(("w", "x"))
 
-    keep, send = call(
+    in_hbm = [
+        pltpu.with_memory_space_constraint(array, pltpu.HBM)
+        for array in (block_ids.reshape(slot_count), w, spectra.transpose(0, 2, 1, 3))
+    ]
+    wide = ((ACROSS, chunks * DEPTH, lane), F32)
+    keep, send, w = call(
         scatter_kernel,
         "scatter",
-        [((half_blocks, tile, lane), BF16), ((half_blocks + 1, tile, lane), BF16)],
-        [smem(), anywhere(), anywhere(), vmem(), vmem()],
-        [pltpu.SMEM((slot_count,), jnp.int32), pltpu.SMEM((1,), jnp.int32), pltpu.SemaphoreType.DMA((2,))],
-    )(here, block_ids.reshape(slot_count), counts.reshape(1), pixels, w)
+        [((half_blocks, tile, lane), BF16), ((half_blocks + 1, tile, lane), BF16), ((tile, comps), F32)],
+        [smem(), smem(), anywhere(), anywhere(), anywhere()],
+        [
+            pltpu.SMEM((slot_count,), jnp.int32),
+            pltpu.VMEM((tile_x, slot_count, tile_y, lane), BF16),
+            pltpu.SemaphoreType.DMA((3,)),
+        ],
+    )(here, counts.reshape(1), *in_hbm)
     got = lax.ppermute(send, "core", swap)
+    (own,) = call(
+        own_kernel,
+        "own",
+        [wide],
+        [vmem(), vmem()],
+        cost=pl.CostEstimate(flops=2 * tile * comps * half_bins, bytes_accessed=4 * comps * half_bins, transcendentals=0),
+    )(keep, w)
     codes, edges = call(
         numer_kernel,
         "numer",
         [((chunks, DEPTH, width), jnp.int16), ((16, comps), F32)],
         [smem(), vmem(), vmem(), vmem()],
-        [pltpu.VMEM((ACROSS, chunks * DEPTH, lane), F32)],
-    )(here, keep, got, w)
+        [pltpu.VMEM(*wide)],
+    )(here, own, got, w)
     codes = lax.all_to_all(codes, peers, 0, 0, tiled=True)
     h_all, h_mine, h_send, coarse = call(
         spectra_kernel,
@@ -410,22 +433,26 @@
     h_got = lax.ppermute(h_send, "core", swap)
     h_all = lax.all_to_all(h_all, peers, 0, 0, tiled=True)
     copies = lax.axis_size(("core", "x"))
-    both, tv_num, tv_den = call(
-        functools.partial(project_kernel, tv_strength),
+    (both,) = call(
+        project_kernel,
         "project",
-        [((copies, tile, 2 * comps), F32), ((tile, comps), F32), ((tile, comps), F32)],
-        [smem()] + [vmem()] * 6,
-        [pltpu.VMEM((ACROSS, chunks * DEPTH, lane), F32)],
-    )(here, h_all, keep, got, coarse, edges, w)
+        [((copies, tile, 2 * comps), F32)],
+        [smem(), vmem(), vmem(), vmem()],
+        [pltpu.VMEM(*wide)],
+    )(here, h_all, keep, got)
+    tv_num, tv_den = call(
+        functools.partial(smooth_kernel, tv_strength, half_blocks),
+        "smooth",
+        [((tile, comps), F32)] * 2,
+        [smem()] + [vmem()] * 4,
+        cost=pl.CostEstimate(flops=80 * tile * comps, bytes_accessed=64 * tile * comps, transcendentals=8 * tile * comps),
+    )(here, h_all, coarse, edges, w)
     both = lax.all_to_all(both, ("core", "x"), 0, 0, tiled=True)
     (both,) = call(sum_kernel, "sum", [((tile, 2 * comps), F32)], [vmem()])(both)
     both = lax.all_gather(both, "w", axis=0)
-    w_next, h_next = call(
-        loadings_kernel,
-        "loadings",
-        [((tile, comps), F32), ((1, slab_bins), F32)],
-        [smem()] + [vmem()] * 6,
-    )(here, both, w, tv_num, tv_den, h_mine, h_got)
+    (w_next,) = call(loadings_kernel, "loadings", [((tile, comps), F32)], [vmem()] * 4)(both, w, tv_num, tv_den)
+    h_pair = jnp.concatenate([h_got, h_mine, h_got], axis=1)
+    h_next = lax.dynamic_slice_in_dim(h_pair, (1 - lax.axis_index("core")) * half_bins, slab_bins, 1)
     return (w_next.reshape(tile_x, tile_y, comps), h_next)
 
 

time: 124 us -> 122 us (0.984)
  blocking collectives: 94 us -> 64.7 us
  waiting for transfers between devices: 6.45 us -> 28.4 us
  starting transfers between devices: 8.77 us -> 12.5 us
  Pallas kernels: 9.45 us -> 13 us
  local copies, waits for them, and re-layouts: 3.42 us -> 0.01 us
    all_to_all x1 -> x0, blocking collectives: 28.7 us -> none  [local(): h_all = lax.all_to_all(h_all, peers, 0, 0, tiled=True)]
    all_to_all x0 -> x1, waiting for transfers between devices: none -> 21.7 us  [local(): h_all = lax.all_to_all(h_all, peers, 0, 0, tiled=True)]
    all_to_all x0 -> x1, starting transfers between devices: none -> 5.24 us  [local(): h_all = lax.all_to_all(h_all, peers, 0, 0, tiled=True)]
    unnamed x12 -> x2, local copies, waits for them, and re-layouts: 3.42 us -> 0.01 us
    pallas_call x1, Pallas kernels: 1.28 us -> 3.25 us  [local(): call(scatter_kernel, 'scatter', [((half_blocks, tile, lane), BF16), ((hal...]
    pallas_call x2 -> x4, Pallas kernels: 4.13 us -> 4.98 us  [the longest x1 2.73 us: local(): call(project_kernel, 'project', [((copies, tile, 2 * comps), F32)], [smem...]
  transfers between devices with their start and end apart: 3 -> 4, of which waited for: 2 -> 3; matrix products, arithmetic and copies ran while one was open for 0% -> 1% of each run, Pallas kernels for 0% -> 3%
where the time goes in v5:
time: 122 us; the launch traced here: 121 us
  blocking collectives  64.7 us (53%)
  waiting for transfers between devices  28.4 us (23%)
  Pallas kernels  13 us (11%)
  starting transfers between devices  12.5 us (10%)
  between operations  1.37 us (1%)
    all_to_all x1, blocking collectives, local(): codes = lax.all_to_all(codes, peers, 0, 0, tiled=True)  40.5 us
    all_gather x1, blocking collectives, local(): both = lax.all_gather(both, 'w', axis=0)  24.2 us
    all_to_all x1, waiting for transfers between devices, local(): h_all = lax.all_to_all(h_all, peers, 0, 0, tiled=True)  21.7 us
    all_to_all x1, starting transfers between devices, local(): h_all = lax.all_to_all(h_all, peers, 0, 0, tiled=True)  5.24 us
    all_to_all x1, waiting for transfers between devices, local(): both = lax.all_to_all(both, ('core', 'x'), 0, 0, tiled=True)  5.13 us
    all_to_all x1, starting transfers between devices, local(): both = lax.all_to_all(both, ('core', 'x'), 0, 0, tiled=True)  3.41 us
    pallas_call x1, Pallas kernels, local(): call(scatter_kernel, 'scatter', [((half_blocks, tile, lane), BF16), ((hal...  3.25 us
    pallas_call x1, Pallas kernels, local(): call(spectra_kernel, 'spectra', [((chunks, DEPTH, width), BF16), ((1, hal...  2.75 us
  transfers between devices with their start and end apart: 4, of which 3 were waited for; matrix products, arithmetic and copies ran while one was open for 1% of the time, Pallas kernels for 3%

profile of v5, /device:TPU:8, one launch (start us, length us, event | category | flops | bytes accessed | tf_op | source)
XLA Modules:
  0.0 121.1 jit_solution(17771218727507869547)
XLA Ops:
  1.3 0.1 pad_add_fusion.where_ref
  1.4 3.3 %scatter.1 = (bf16[49,64,128]{2,1,0:T(8,128)(2,1)S(1)}, bf16[50,64,128]{2,1,0:T(8,128)(2,1)S(1)}, f32[64,64]{1,0:T(8,128)S(1)}) custom-call(s32[4]{0:T(128)S(1)} %pad_add_fusion.where_ref, s32[1]{0:T(128)} %bitcast.10.count_ref, s32[52]{0:T(128)} %bitcast.15, f32[64,64]{1,0:T(8,128)} %bitcast.14, bf16[8,52,8,128]{3,2,1,0:T(8,128)(2,1)} %bitcast.12), custom_call_target="tpu_custom_call" | custom-call | tf_op jit(solution)/shard_map/scatter/pallas_call | solution.py:399
  4.6 1.9 %collective-permute-start = (bf16[50,64,128]{2,1,0:T(8,128)(2,1)S(1)}, bf16[50,64,128]{2,1,0:T(8,128)(2,1)S(1)}, u32[]{:S(2)}, u32[]{:S(2)}) collective-permute-start(bf16[50,64,128]{2,1,0:T(8,128)(2,1)S(1)} %get-tuple-element.15), channel_id=1, source_target_pairs={{0,64},{64,0},{1,65},{65,1},{2,66},{66,2},{3,67},{67,3},{4,68},{68... | collective-permute-start | bytes 2457608 | tf_op jit(solution)/shard_map/ppermute | solution.py:410
  6.6 0.0 copy-start
  6.6 0.7 own.1.own_ref
  7.3 1.6 %collective-permute-done.got_ref = bf16[50,64,128]{2,1,0:T(8,128)(2,1)S(1)} collective-permute-done((bf16[50,64,128]{2,1,0:T(8,128)(2,1)S(1)}, bf16[50,64,128]{2,1,0:T(8,128)(2,1)S(1)}, u32[]{:S(2)}, u32[]{:S(2)}) %collective-permute-start) | collective-permute-done | bytes 819232 | tf_op jit(solution)/shard_map/ppermute | solution.py:410
  8.8 2.0 %numer.1 = (s16[32,8,1664]{2,1,0:T(8,128)(2,1)S(1)}, f32[16,64]{1,0:T(8,128)S(1)}) custom-call(s32[4]{0:T(128)S(1)} %pad_add_fusion.where_ref, f32[13,256,128]{2,1,0:T(8,128)S(1)} %own.1.own_ref, bf16[50,64,128]{2,1,0:T(8,128)(2,1)S(1)} %collective-permute-done.got_ref, f32[64,64]{1,0:T(8,128)S(1)} %get-tuple-element.14.w_ref), custom_call_target="tpu_custom_call" | custom-call | tf_op jit(solution)/shard_map/numer/pallas_call | solution.py:418
  10.8 40.5 %all_to_all.15.codes_ref = s16[32,8,1664]{2,1,0:T(8,128)(2,1)S(1)} all-to-all(s16[32,8,1664]{2,1,0:T(8,128)(2,1)S(1)} %get-tuple-element.16), channel_id=1, replica_groups=mesh['y'=8,'core'=2,'gy'=4,'w'=4,'x'=4] {'y','gy'}, dimensions={0} | all-to-all | bytes 1703936 | tf_op jit(solution)/shard_map/all_to_all | solution.py:425
  51.3 0.0 copy-done
  51.3 2.8 %spectra.1 = (bf16[32,8,1664]{2,1,0:T(8,128)(2,1)}, f32[1,6272]{1,0:T(1,128)S(1)}, f32[1,6272]{1,0:T(1,128)S(1)}, f32[24,64]{1,0:T(8,128)S(1)}) custom-call(s32[4]{0:T(128)S(1)} %pad_add_fusion.where_ref, s16[32,8,1664]{2,1,0:T(8,128)(2,1)S(1)} %all_to_all.15.codes_ref, f32[16,64]{1,0:T(8,128)S(1)} %get-tuple-element.17.edges_ref, f32[64,12544]{1,0:T(8,128)S(1)} %copy-done, ...), custom_call_target="tpu_custom_call" | custom-call | tf_op jit(solution)/shard_map/spectra/pallas_call | solution.py:426
  54.1 5.2 %all-to-all-start.1 = ((bf16[32,8,1664]{2,1,0:T(8,128)(2,1)}), bf16[32,8,1664]{2,1,0:T(8,128)(2,1)S(1)}, u32[]{:S(2)}, u32[]{:S(2)}) async-start(bf16[32,8,1664]{2,1,0:T(8,128)(2,1)} %get-tuple-element.18), calls=%async_computation.1 | async-start | bytes 1703936 | tf_op jit(solution)/shard_map/all_to_all | solution.py:434
  59.3 1.9 %collective-permute-start.1 = (f32[1,6272]{1,0:T(1,128)S(1)}, f32[1,6272]{1,0:T(1,128)S(1)}, u32[]{:S(2)}, u32[]{:S(2)}) collective-permute-start(f32[1,6272]{1,0:T(1,128)S(1)} %get-tuple-element.22), channel_id=1, source_target_pairs={{0,64},{64,0},{1,65},{65,1},{2,66},{66,2},{3,67},{67,3},{4,68},{68... | collective-permute-start | bytes 75272 | tf_op jit(solution)/shard_map/ppermute | solution.py:433
  61.3 21.7 %all-to-all-done.1.h_ref = bf16[32,8,1664]{2,1,0:T(8,128)(2,1)S(1)} async-done(((bf16[32,8,1664]{2,1,0:T(8,128)(2,1)}), bf16[32,8,1664]{2,1,0:T(8,128)(2,1)S(1)}, u32[]{:S(2)}, u32[]{:S(2)}) %all-to-all-start.1) | async-done | bytes 852000 | tf_op jit(solution)/shard_map/all_to_all | solution.py:434
  83.0 2.7 %project.1 = f32[8,64,128]{2,1,0:T(8,128)} custom-call(s32[4]{0:T(128)S(1)} %pad_add_fusion.where_ref, bf16[32,8,1664]{2,1,0:T(8,128)(2,1)S(1)} %all-to-all-done.1.h_ref, bf16[49,64,128]{2,1,0:T(8,128)(2,1)S(1)} %get-tuple-element.13.keep_ref, bf16[50,64,128]{2,1,0:T(8,128)(2,1)S(1)} %collective-permute-done.got_ref), custom_call_target="tpu_custom_call" | custom-call | tf_op jit(solution)/shard_map/project/pallas_call | solution.py:436
  85.7 3.4 %all-to-all-start.2 = ((f32[8,64,128]{2,1,0:T(8,128)}), f32[8,64,128]{2,1,0:T(8,128)S(1)}, u32[]{:S(2)}, u32[]{:S(2)}) async-start(f32[8,64,128]{2,1,0:T(8,128)} %project.1), calls=%async_computation.2 | async-start | bytes 524288 | tf_op jit(solution)/shard_map/all_to_all | solution.py:450
  89.1 0.0 collective-permute-done.1
  89.1 1.0 fusion.1
  90.2 0.7 smooth.1
  90.8 5.1 %all-to-all-done.2.parts_ref = f32[8,64,128]{2,1,0:T(8,128)S(1)} async-done(((f32[8,64,128]{2,1,0:T(8,128)}), f32[8,64,128]{2,1,0:T(8,128)S(1)}, u32[]{:S(2)}, u32[]{:S(2)}) %all-to-all-start.2) | async-done | bytes 262176 | tf_op jit(solution)/shard_map/all_to_all | solution.py:450
  96.0 24.2 %all-gather = f32[256,128]{1,0:T(8,128)S(1)} all-gather(f32[64,128]{1,0:T(8,128)S(1)} %sum.1), channel_id=2, replica_groups=mesh['y'=8,'core'=2,'gy'=4,'w'=4,'x'=4] {'w'}, dimensions={0}, use_global_device_ids=true | all-gather | bytes 163840 | tf_op jit(solution)/shard_map/all_gather | solution.py:452
  120.2 0.9 loadings.1
  (1 shorter events, 0.0 us)
Async XLA Ops:
  4.6 4.2 %collective-permute-start = (bf16[50,64,128]{2,1,0:T(8,128)(2,1)S(1)}, bf16[50,64,128]{2,1,0:T(8,128)(2,1)S(1)}, u32[]{:S(2)}, u32[]{:S(2)}) collective-permute-start(bf16[50,64,128]{2,1,0:T(8,128)(2,1)S(1)} %get-tuple-element.15), channel_id=1, source_target_pairs={{0,64},{64,0},{1,65},{65,1},{2,66},{66,2},{3,67},{67,3},{4,68},{68... | collective-permute-start | bytes 2457608 | tf_op jit(solution)/shard_map/ppermute | solution.py:410
  6.6 44.8 %copy-start = (f32[64,12544]{1,0:T(8,128)S(1)}, f32[64,12544]{1,0:T(8,128)}, u32[]{:S(2)}) copy-start(f32[64,12544]{1,0:T(8,128)} %comps_ref.1) | copy-start | bytes 9633796
  54.1 28.9 %all-to-all-start.1 = ((bf16[32,8,1664]{2,1,0:T(8,128)(2,1)}), bf16[32,8,1664]{2,1,0:T(8,128)(2,1)S(1)}, u32[]{:S(2)}, u32[]{:S(2)}) async-start(bf16[32,8,1664]{2,1,0:T(8,128)(2,1)} %get-tuple-element.18), calls=%async_computation.1 | async-start | bytes 1703936 | tf_op jit(solution)/shard_map/all_to_all | solution.py:434
  59.3 29.8 %collective-permute-start.1 = (f32[1,6272]{1,0:T(1,128)S(1)}, f32[1,6272]{1,0:T(1,128)S(1)}, u32[]{:S(2)}, u32[]{:S(2)}) collective-permute-start(f32[1,6272]{1,0:T(1,128)S(1)} %get-tuple-element.22), channel_id=1, source_target_pairs={{0,64},{64,0},{1,65},{65,1},{2,66},{66,2},{3,67},{67,3},{4,68},{68... | collective-permute-start | bytes 75272 | tf_op jit(solution)/shard_map/ppermute | solution.py:433
  85.7 10.3 %all-to-all-start.2 = ((f32[8,64,128]{2,1,0:T(8,128)}), f32[8,64,128]{2,1,0:T(8,128)S(1)}, u32[]{:S(2)}, u32[]{:S(2)}) async-start(f32[8,64,128]{2,1,0:T(8,128)} %project.1), calls=%async_computation.2 | async-start | bytes 524288 | tf_op jit(solution)/shard_map/all_to_all | solution.py:450

commit v6 on v5

--- a/solution.py
+++ b/solution.py
@@ -292,7 +292,9 @@
         tv_den_ref[8 * i : 8 * i + 8, :] = tv_strength * den
 
 
-def project_kernel(where_ref, h_ref, keep_ref, got_ref, out_ref, wide_ref):
+def project_kernel(
+    tv_strength, where_ref, h_ref, keep_ref, got_ref, coarse_ref, edges_ref, w_ref, out_ref, tv_num_ref, tv_den_ref, wide_ref
+):
     half_blocks, tile, lane = keep_ref.shape
     chunks = h_ref.shape[0]
     comps = 2 * chunks
@@ -328,10 +330,6 @@
         for i in range(copies // 2):
             out_ref[to_core * (copies // 2) + i] = both
 
-
-def smooth_kernel(tv_strength, half_blocks, where_ref, h_ref, coarse_ref, edges_ref, w_ref, tv_num_ref, tv_den_ref):
-    lane = LANE
-    chunks = h_ref.shape[0]
     halo_row, halo_at = place_of(2 * half_blocks + 1)
     halos = []
     for n, (source, inside) in enumerate(rim_sources(where_ref, chunks)):
@@ -433,26 +431,20 @@
     h_got = lax.ppermute(h_send, "core", swap)
     h_all = lax.all_to_all(h_all, peers, 0, 0, tiled=True)
     copies = lax.axis_size(("core", "x"))
-    (both,) = call(
-        project_kernel,
+    h_pair = jnp.concatenate([h_got, h_mine, h_got], axis=1)
+    h_next = lax.dynamic_slice_in_dim(h_pair, (1 - lax.axis_index("core")) * half_bins, slab_bins, 1)
+    h_all, h_next = lax.optimization_barrier((h_all, h_next))
+    both, tv_num, tv_den = call(
+        functools.partial(project_kernel, tv_strength),
         "project",
-        [((copies, tile, 2 * comps), F32)],
-        [smem(), vmem(), vmem(), vmem()],
+        [((copies, tile, 2 * comps), F32), ((tile, comps), F32), ((tile, comps), F32)],
+        [smem()] + [vmem()] * 6,
         [pltpu.VMEM(*wide)],
-    )(here, h_all, keep, got)
-    tv_num, tv_den = call(
-        functools.partial(smooth_kernel, tv_strength, half_blocks),
-        "smooth",
-        [((tile, comps), F32)] * 2,
-        [smem()] + [vmem()] * 4,
-        cost=pl.CostEstimate(flops=80 * tile * comps, bytes_accessed=64 * tile * comps, transcendentals=8 * tile * comps),
-    )(here, h_all, coarse, edges, w)
+    )(here, h_all, keep, got, coarse, edges, w)
     both = lax.all_to_all(both, ("core", "x"), 0, 0, tiled=True)
     (both,) = call(sum_kernel, "sum", [((tile, 2 * comps), F32)], [vmem()])(both)
     both = lax.all_gather(both, "w", axis=0)
     (w_next,) = call(loadings_kernel, "loadings", [((tile, comps), F32)], [vmem()] * 4)(both, w, tv_num, tv_den)
-    h_pair = jnp.concatenate([h_got, h_mine, h_got], axis=1)
-    h_next = lax.dynamic_slice_in_dim(h_pair, (1 - lax.axis_index("core")) * half_bins, slab_bins, 1)
     return (w_next.reshape(tile_x, tile_y, comps), h_next)
 
 

time: 122 us -> 121 us (level)
  blocking collectives: 64.7 us -> 75.6 us
  waiting for transfers between devices: 28.4 us -> 22.2 us
  starting transfers between devices: 12.5 us -> 9.1 us
  Pallas kernels: 13 us -> 10.9 us
    all_to_all x0 -> x1, blocking collectives: none -> 9.38 us  [local(): both = lax.all_to_all(both, ('core', 'x'), 0, 0, tiled=True)]
    all_to_all x1 -> x0, waiting for transfers between devices: 5.13 us -> none  [local(): both = lax.all_to_all(both, ('core', 'x'), 0, 0, tiled=True)]
    all_to_all x1 -> x0, starting transfers between devices: 3.41 us -> none  [local(): both = lax.all_to_all(both, ('core', 'x'), 0, 0, tiled=True)]
    all_to_all x1, waiting for transfers between devices: 21.7 us -> 19.5 us  [local(): h_all = lax.all_to_all(h_all, peers, 0, 0, tiled=True)]
    all_gather x1, blocking collectives: 24.2 us -> 26.3 us  [local(): both = lax.all_gather(both, 'w', axis=0)]
    pallas_call x2 -> x1, Pallas kernels: 3.4 us -> 2.02 us  [local(): call(functools.partial(project_kernel, tv_strength), 'project', [((copies...]
  transfers between devices with their start and end apart: 4 -> 3, of which waited for: 3 -> 3; matrix products, arithmetic and copies ran while one was open for 1% -> 1% of each run, Pallas kernels for 3% -> 1%
where the time goes in v6:
time: 121 us; the launch traced here: 120 us
  blocking collectives  75.6 us (62%)
  waiting for transfers between devices  22.2 us (18%)
  Pallas kernels  10.9 us (9%)
  starting transfers between devices  9.1 us (8%)
  between operations  1.35 us (1%)
    all_to_all x1, blocking collectives, local(): codes = lax.all_to_all(codes, peers, 0, 0, tiled=True)  39.9 us
    all_gather x1, blocking collectives, local(): both = lax.all_gather(both, 'w', axis=0)  26.3 us
    all_to_all x1, waiting for transfers between devices, local(): h_all = lax.all_to_all(h_all, peers, 0, 0, tiled=True)  19.5 us
    all_to_all x1, blocking collectives, local(): both = lax.all_to_all(both, ('core', 'x'), 0, 0, tiled=True)  9.38 us
    all_to_all x1, starting transfers between devices, local(): h_all = lax.all_to_all(h_all, peers, 0, 0, tiled=True)  5.26 us
    pallas_call x1, Pallas kernels, local(): call(spectra_kernel, 'spectra', [((chunks, DEPTH, width), BF16), ((1, hal...  2.73 us
    pallas_call x1, Pallas kernels, local(): call(scatter_kernel, 'scatter', [((half_blocks, tile, lane), BF16), ((hal...  2.53 us
  transfers between devices with their start and end apart: 3, of which 3 were waited for; matrix products, arithmetic and copies ran while one was open for 1% of the time, Pallas kernels for 1%

profile of v6, /device:TPU:8, one launch (start us, length us, event | category | flops | bytes accessed | tf_op | source)
XLA Modules:
  0.0 120.3 jit_solution(14256410045284532785)
XLA Ops:
  1.3 0.1 pad_add_fusion.where_ref
  1.4 2.5 %scatter.1 = (bf16[49,64,128]{2,1,0:T(8,128)(2,1)S(1)}, bf16[50,64,128]{2,1,0:T(8,128)(2,1)S(1)}, f32[64,64]{1,0:T(8,128)S(1)}) custom-call(s32[4]{0:T(128)S(1)} %pad_add_fusion.where_ref, s32[1]{0:T(128)} %bitcast.10.count_ref, s32[52]{0:T(128)} %bitcast.15, f32[64,64]{1,0:T(8,128)} %bitcast.14, bf16[8,52,8,128]{3,2,1,0:T(8,128)(2,1)} %bitcast.12), custom_call_target="tpu_custom_call" | custom-call | tf_op jit(solution)/shard_map/scatter/pallas_call | solution.py:397
  3.9 1.9 %collective-permute-start = (bf16[50,64,128]{2,1,0:T(8,128)(2,1)S(1)}, bf16[50,64,128]{2,1,0:T(8,128)(2,1)S(1)}, u32[]{:S(2)}, u32[]{:S(2)}) collective-permute-start(bf16[50,64,128]{2,1,0:T(8,128)(2,1)S(1)} %get-tuple-element.18), channel_id=1, source_target_pairs={{0,64},{64,0},{1,65},{65,1},{2,66},{66,2},{3,67},{67,3},{4,68},{68... | collective-permute-start | bytes 2457608 | tf_op jit(solution)/shard_map/ppermute | solution.py:408
  5.8 0.0 copy-start
  5.8 0.7 own.1.own_ref
  6.6 1.5 %collective-permute-done.got_ref = bf16[50,64,128]{2,1,0:T(8,128)(2,1)S(1)} collective-permute-done((bf16[50,64,128]{2,1,0:T(8,128)(2,1)S(1)}, bf16[50,64,128]{2,1,0:T(8,128)(2,1)S(1)}, u32[]{:S(2)}, u32[]{:S(2)}) %collective-permute-start) | collective-permute-done | bytes 819232 | tf_op jit(solution)/shard_map/ppermute | solution.py:408
  8.1 2.0 %numer.1 = (s16[32,8,1664]{2,1,0:T(8,128)(2,1)S(1)}, f32[16,64]{1,0:T(8,128)S(1)}) custom-call(s32[4]{0:T(128)S(1)} %pad_add_fusion.where_ref, f32[13,256,128]{2,1,0:T(8,128)S(1)} %own.1.own_ref, bf16[50,64,128]{2,1,0:T(8,128)(2,1)S(1)} %collective-permute-done.got_ref, f32[64,64]{1,0:T(8,128)S(1)} %get-tuple-element.17.w_ref), custom_call_target="tpu_custom_call" | custom-call | tf_op jit(solution)/shard_map/numer/pallas_call | solution.py:416
  10.1 39.9 %all_to_all.15.codes_ref = s16[32,8,1664]{2,1,0:T(8,128)(2,1)S(1)} all-to-all(s16[32,8,1664]{2,1,0:T(8,128)(2,1)S(1)} %get-tuple-element.19), channel_id=1, replica_groups=mesh['y'=8,'core'=2,'gy'=4,'w'=4,'x'=4] {'y','gy'}, dimensions={0} | all-to-all | bytes 1703936 | tf_op jit(solution)/shard_map/all_to_all | solution.py:423
  50.0 0.0 copy-done
  50.0 2.7 %spectra.1 = (bf16[32,8,1664]{2,1,0:T(8,128)(2,1)}, f32[1,6272]{1,0:T(1,128)S(1)}, f32[1,6272]{1,0:T(1,128)S(1)}, f32[24,64]{1,0:T(8,128)S(1)}) custom-call(s32[4]{0:T(128)S(1)} %pad_add_fusion.where_ref, s16[32,8,1664]{2,1,0:T(8,128)(2,1)S(1)} %all_to_all.15.codes_ref, f32[16,64]{1,0:T(8,128)S(1)} %get-tuple-element.20.edges_ref, f32[64,12544]{1,0:T(8,128)S(1)} %copy-done, ...), custom_call_target="tpu_custom_call" | custom-call | tf_op jit(solution)/shard_map/spectra/pallas_call | solution.py:424
  52.8 5.3 %all-to-all-start.1 = ((bf16[32,8,1664]{2,1,0:T(8,128)(2,1)}), bf16[32,8,1664]{2,1,0:T(8,128)(2,1)S(1)}, u32[]{:S(2)}, u32[]{:S(2)}) async-start(bf16[32,8,1664]{2,1,0:T(8,128)(2,1)} %get-tuple-element.21), calls=%async_computation.1 | async-start | bytes 1703936 | tf_op jit(solution)/shard_map/all_to_all | solution.py:432
  58.0 1.9 %collective-permute-start.1 = (f32[1,6272]{1,0:T(1,128)S(1)}, f32[1,6272]{1,0:T(1,128)S(1)}, u32[]{:S(2)}, u32[]{:S(2)}) collective-permute-start(f32[1,6272]{1,0:T(1,128)S(1)} %get-tuple-element.22), channel_id=1, source_target_pairs={{0,64},{64,0},{1,65},{65,1},{2,66},{66,2},{3,67},{67,3},{4,68},{68... | collective-permute-start | bytes 75272 | tf_op jit(solution)/shard_map/ppermute | solution.py:431
  60.0 1.2 collective-permute-done.1
  61.1 1.0 fusion.1
  62.1 19.5 %all-to-all-done.1.h_ref = bf16[32,8,1664]{2,1,0:T(8,128)(2,1)S(1)} async-done(((bf16[32,8,1664]{2,1,0:T(8,128)(2,1)}), bf16[32,8,1664]{2,1,0:T(8,128)(2,1)S(1)}, u32[]{:S(2)}, u32[]{:S(2)}) %all-to-all-start.1) | async-done | bytes 852000 | tf_op jit(solution)/shard_map/all_to_all | solution.py:432
  81.6 2.0 %project.1 = (f32[8,64,128]{2,1,0:T(8,128)S(1)}, f32[64,64]{1,0:T(8,128)S(1)}, f32[64,64]{1,0:T(8,128)S(1)}) custom-call(s32[4]{0:T(128)S(1)} %pad_add_fusion.where_ref, bf16[32,8,1664]{2,1,0:T(8,128)(2,1)S(1)} %all-to-all-done.1.h_ref, bf16[49,64,128]{2,1,0:T(8,128)(2,1)S(1)} %get-tuple-element.16.keep_ref, ...), custom_call_target="tpu_custom_call" | custom-call | tf_op jit(solution)/shard_map/project/pallas_call | solution.py:437
  83.7 9.4 %all_to_all.16.parts_ref = f32[8,64,128]{2,1,0:T(8,128)S(1)} all-to-all(f32[8,64,128]{2,1,0:T(8,128)S(1)} %get-tuple-element.26), channel_id=1, replica_groups=mesh['y'=8,'core'=2,'gy'=4,'w'=4,'x'=4] {'core','x'}, dimensions={0} | all-to-all | bytes 524288 | tf_op jit(solution)/shard_map/all_to_all | solution.py:444
  93.1 26.3 %all-gather = f32[256,128]{1,0:T(8,128)S(1)} all-gather(f32[64,128]{1,0:T(8,128)S(1)} %sum.1), channel_id=2, replica_groups=mesh['y'=8,'core'=2,'gy'=4,'w'=4,'x'=4] {'w'}, dimensions={0}, use_global_device_ids=true | all-gather | bytes 163840 | tf_op jit(solution)/shard_map/all_gather | solution.py:446
  119.4 0.9 loadings.1
  (1 shorter events, 0.0 us)
Async XLA Ops:
  3.9 4.2 %collective-permute-start = (bf16[50,64,128]{2,1,0:T(8,128)(2,1)S(1)}, bf16[50,64,128]{2,1,0:T(8,128)(2,1)S(1)}, u32[]{:S(2)}, u32[]{:S(2)}) collective-permute-start(bf16[50,64,128]{2,1,0:T(8,128)(2,1)S(1)} %get-tuple-element.18), channel_id=1, source_target_pairs={{0,64},{64,0},{1,65},{65,1},{2,66},{66,2},{3,67},{67,3},{4,68},{68... | collective-permute-start | bytes 2457608 | tf_op jit(solution)/shard_map/ppermute | solution.py:408
  5.8 44.2 %copy-start = (f32[64,12544]{1,0:T(8,128)S(1)}, f32[64,12544]{1,0:T(8,128)}, u32[]{:S(2)}) copy-start(f32[64,12544]{1,0:T(8,128)} %comps_ref.1) | copy-start | bytes 9633796
  52.8 28.9 %all-to-all-start.1 = ((bf16[32,8,1664]{2,1,0:T(8,128)(2,1)}), bf16[32,8,1664]{2,1,0:T(8,128)(2,1)S(1)}, u32[]{:S(2)}, u32[]{:S(2)}) async-start(bf16[32,8,1664]{2,1,0:T(8,128)(2,1)} %get-tuple-element.21), calls=%async_computation.1 | async-start | bytes 1703936 | tf_op jit(solution)/shard_map/all_to_all | solution.py:432
  58.0 3.1 %collective-permute-start.1 = (f32[1,6272]{1,0:T(1,128)S(1)}, f32[1,6272]{1,0:T(1,128)S(1)}, u32[]{:S(2)}, u32[]{:S(2)}) collective-permute-start(f32[1,6272]{1,0:T(1,128)S(1)} %get-tuple-element.22), channel_id=1, source_target_pairs={{0,64},{64,0},{1,65},{65,1},{2,66},{66,2},{3,67},{67,3},{4,68},{68... | collective-permute-start | bytes 75272 | tf_op jit(solution)/shard_map/ppermute | solution.py:431

commit v7 on v6

--- a/solution.py
+++ b/solution.py
@@ -1,4 +1,5 @@
 import functools
+import math
 import jax
 import jax.numpy as jnp
 from jax import lax
@@ -51,6 +52,7 @@
 
 
 ACROSS = 13
+SPARE = 2
 DEPTH = 8
 HALO = 4
 
@@ -76,10 +78,11 @@
 
 def scatter_kernel(where_ref, count_ref, ids_hbm, w_hbm, x_hbm, keep_ref, send_ref, w_ref, ids_ref, x_ref, sems):
     copies = fetch([(x_hbm, x_ref), (ids_hbm, ids_ref), (w_hbm, w_ref)], sems)
-    tile_x, _, tile_y, lane = x_ref.shape
+    tile_x, slots, tile_y, lane = x_ref.shape
     tile = tile_x * tile_y
-    half_blocks = keep_ref.shape[0]
-    core = where_ref[2]
+    half_blocks = keep_ref.shape[0] - SPARE
+    spill = half_blocks + 1
+    core, count = where_ref[2], count_ref[0]
     keep_ref[...] = jnp.zeros_like(keep_ref)
     send_ref[...] = jnp.zeros_like(send_ref)
     for copy in copies:
@@ -91,23 +94,22 @@
     pieces = jnp.concatenate([high, mid, edges - high - mid, jnp.zeros_like(edges)], axis=0)
     send_ref[half_blocks] = jnp.concatenate([w, pieces], axis=1).astype(BF16)
 
-    def place(s, carry):
+    def place(s):
         block = ids_ref[s]
-        half = block // half_blocks
-        at = block - half * half_blocks
+        upper = block >= half_blocks
+        at = jnp.where(s < count, jnp.where(upper, block - half_blocks, block), spill)
         rows_of_slot = x_ref[:, s].astype(F32).reshape(tile, lane).astype(BF16)
-
-        @pl.when(half == core)
-        def _():
-            keep_ref[at] = rows_of_slot
-
-        @pl.when(half != core)
-        def _():
-            send_ref[at] = rows_of_slot
-
+        here = upper == (core == 1)
+        keep_ref[jnp.where(here, at, spill)] = rows_of_slot
+        send_ref[jnp.where(here, spill, at)] = rows_of_slot
+
+    def place_group(g, carry):
+        for i in range(group):
+            place(g * group + i)
         return carry
 
-    lax.fori_loop(0, count_ref[0], place, 0)
+    group = math.gcd(slots, 4)
+    lax.fori_loop(0, (count + group - 1) // group, place_group, 0)
 
 
 def put(wide_ref, q, value):
@@ -136,7 +138,7 @@
 
 
 def own_kernel(keep_ref, w_ref, own_ref):
-    numerators(w_ref[...].astype(BF16), keep_ref, keep_ref.shape[0], own_ref)
+    numerators(w_ref[...].astype(BF16), keep_ref, keep_ref.shape[0] - SPARE, own_ref)
 
 
 def rims(where_ref, w, edges):
@@ -180,7 +182,7 @@
 
 
 def numer_kernel(where_ref, own_ref, got_ref, w_ref, codes_ref, edges_ref, wide_ref):
-    half_blocks = got_ref.shape[0] - 1
+    half_blocks = got_ref.shape[0] - SPARE
     lane = LANE
     comps = w_ref.shape[1]
     chunks = codes_ref.shape[0]
@@ -295,7 +297,8 @@
 def project_kernel(
     tv_strength, where_ref, h_ref, keep_ref, got_ref, coarse_ref, edges_ref, w_ref, out_ref, tv_num_ref, tv_den_ref, wide_ref
 ):
-    half_blocks, tile, lane = keep_ref.shape
+    tile, lane = keep_ref.shape[1:]
+    half_blocks = keep_ref.shape[0] - SPARE
     chunks = h_ref.shape[0]
     comps = 2 * chunks
     copies = out_ref.shape[0]
@@ -397,7 +400,7 @@
     keep, send, w = call(
         scatter_kernel,
         "scatter",
-        [((half_blocks, tile, lane), BF16), ((half_blocks + 1, tile, lane), BF16), ((tile, comps), F32)],
+        [((half_blocks + SPARE, tile, lane), BF16)] * 2 + [((tile, comps), F32)],
         [smem(), smem(), anywhere(), anywhere(), anywhere()],
         [
             pltpu.SMEM((slot_count,), jnp.int32),

time: 121 us -> 120 us (level)
  no operation moved by 1% of the time
where the time goes in v7:
time: 120 us
  blocking collectives  76.2 us (64%)
  waiting for transfers between devices  22.3 us (19%)
  Pallas kernels  10.3 us (9%)
  starting transfers between devices  9.08 us (8%)
  between operations  1.35 us (1%)
    all_to_all x1, blocking collectives, local(): codes = lax.all_to_all(codes, peers, 0, 0, tiled=True)  40.4 us
    all_gather x1, blocking collectives, local(): both = lax.all_gather(both, 'w', axis=0)  26.5 us
    all_to_all x1, waiting for transfers between devices, local(): h_all = lax.all_to_all(h_all, peers, 0, 0, tiled=True)  19.5 us
    all_to_all x1, blocking collectives, local(): both = lax.all_to_all(both, ('core', 'x'), 0, 0, tiled=True)  9.33 us
    all_to_all x1, starting transfers between devices, local(): h_all = lax.all_to_all(h_all, peers, 0, 0, tiled=True)  5.24 us
    pallas_call x1, Pallas kernels, local(): call(spectra_kernel, 'spectra', [((chunks, DEPTH, width), BF16), ((1, hal...  2.73 us
  transfers between devices with their start and end apart: 3, of which 3 were waited for; matrix products, arithmetic and copies ran while one was open for 1% of the time, Pallas kernels for 1%

profile of v7, /device:TPU:8, one launch (start us, length us, event | category | flops | bytes accessed | tf_op | source)
XLA Modules:
  0.0 120.3 jit_solution(17384599283709346572)
XLA Ops:
  1.3 0.1 pad_add_fusion.where_ref
  1.4 2.0 %scatter.1 = (bf16[51,64,128]{2,1,0:T(8,128)(2,1)S(1)}, bf16[51,64,128]{2,1,0:T(8,128)(2,1)S(1)}, f32[64,64]{1,0:T(8,128)S(1)}) custom-call(s32[4]{0:T(128)S(1)} %pad_add_fusion.where_ref, s32[1]{0:T(128)} %bitcast.10.count_ref, s32[52]{0:T(128)} %bitcast.15, f32[64,64]{1,0:T(8,128)} %bitcast.14, bf16[8,52,8,128]{3,2,1,0:T(8,128)(2,1)} %bitcast.12), custom_call_target="tpu_custom_call" | custom-call | tf_op jit(solution)/shard_map/scatter/pallas_call | solution.py:400
  3.3 1.9 %collective-permute-start = (bf16[51,64,128]{2,1,0:T(8,128)(2,1)S(1)}, bf16[51,64,128]{2,1,0:T(8,128)(2,1)S(1)}, u32[]{:S(2)}, u32[]{:S(2)}) collective-permute-start(bf16[51,64,128]{2,1,0:T(8,128)(2,1)S(1)} %get-tuple-element.18), channel_id=1, source_target_pairs={{0,64},{64,0},{1,65},{65,1},{2,66},{66,2},{3,67},{67,3},{4,68},{68... | collective-permute-start | bytes 2506760 | tf_op jit(solution)/shard_map/ppermute | solution.py:411
  5.3 0.0 copy-start
  5.3 0.7 own.1.own_ref
  6.0 1.6 %collective-permute-done.got_ref = bf16[51,64,128]{2,1,0:T(8,128)(2,1)S(1)} collective-permute-done((bf16[51,64,128]{2,1,0:T(8,128)(2,1)S(1)}, bf16[51,64,128]{2,1,0:T(8,128)(2,1)S(1)}, u32[]{:S(2)}, u32[]{:S(2)}) %collective-permute-start) | collective-permute-done | bytes 835616 | tf_op jit(solution)/shard_map/ppermute | solution.py:411
  7.6 2.0 %numer.1 = (s16[32,8,1664]{2,1,0:T(8,128)(2,1)S(1)}, f32[16,64]{1,0:T(8,128)S(1)}) custom-call(s32[4]{0:T(128)S(1)} %pad_add_fusion.where_ref, f32[13,256,128]{2,1,0:T(8,128)S(1)} %own.1.own_ref, bf16[51,64,128]{2,1,0:T(8,128)(2,1)S(1)} %collective-permute-done.got_ref, f32[64,64]{1,0:T(8,128)S(1)} %get-tuple-element.17.w_ref), custom_call_target="tpu_custom_call" | custom-call | tf_op jit(solution)/shard_map/numer/pallas_call | solution.py:419
  9.6 40.4 %all_to_all.15.codes_ref = s16[32,8,1664]{2,1,0:T(8,128)(2,1)S(1)} all-to-all(s16[32,8,1664]{2,1,0:T(8,128)(2,1)S(1)} %get-tuple-element.19), channel_id=1, replica_groups=mesh['y'=8,'core'=2,'gy'=4,'w'=4,'x'=4] {'y','gy'}, dimensions={0} | all-to-all | bytes 1703936 | tf_op jit(solution)/shard_map/all_to_all | solution.py:426
  50.0 0.0 copy-done
  50.0 2.7 %spectra.1 = (bf16[32,8,1664]{2,1,0:T(8,128)(2,1)}, f32[1,6272]{1,0:T(1,128)S(1)}, f32[1,6272]{1,0:T(1,128)S(1)}, f32[24,64]{1,0:T(8,128)S(1)}) custom-call(s32[4]{0:T(128)S(1)} %pad_add_fusion.where_ref, s16[32,8,1664]{2,1,0:T(8,128)(2,1)S(1)} %all_to_all.15.codes_ref, f32[16,64]{1,0:T(8,128)S(1)} %get-tuple-element.20.edges_ref, f32[64,12544]{1,0:T(8,128)S(1)} %copy-done, ...), custom_call_target="tpu_custom_call" | custom-call | tf_op jit(solution)/shard_map/spectra/pallas_call | solution.py:427
  52.7 5.2 %all-to-all-start.1 = ((bf16[32,8,1664]{2,1,0:T(8,128)(2,1)}), bf16[32,8,1664]{2,1,0:T(8,128)(2,1)S(1)}, u32[]{:S(2)}, u32[]{:S(2)}) async-start(bf16[32,8,1664]{2,1,0:T(8,128)(2,1)} %get-tuple-element.21), calls=%async_computation.1 | async-start | bytes 1703936 | tf_op jit(solution)/shard_map/all_to_all | solution.py:435
  58.0 1.9 %collective-permute-start.1 = (f32[1,6272]{1,0:T(1,128)S(1)}, f32[1,6272]{1,0:T(1,128)S(1)}, u32[]{:S(2)}, u32[]{:S(2)}) collective-permute-start(f32[1,6272]{1,0:T(1,128)S(1)} %get-tuple-element.22), channel_id=1, source_target_pairs={{0,64},{64,0},{1,65},{65,1},{2,66},{66,2},{3,67},{67,3},{4,68},{68... | collective-permute-start | bytes 75272 | tf_op jit(solution)/shard_map/ppermute | solution.py:434
  59.9 1.2 collective-permute-done.1
  61.0 1.0 fusion.1
  62.1 19.5 %all-to-all-done.1.h_ref = bf16[32,8,1664]{2,1,0:T(8,128)(2,1)S(1)} async-done(((bf16[32,8,1664]{2,1,0:T(8,128)(2,1)}), bf16[32,8,1664]{2,1,0:T(8,128)(2,1)S(1)}, u32[]{:S(2)}, u32[]{:S(2)}) %all-to-all-start.1) | async-done | bytes 852000 | tf_op jit(solution)/shard_map/all_to_all | solution.py:435
  81.6 2.0 %project.1 = (f32[8,64,128]{2,1,0:T(8,128)S(1)}, f32[64,64]{1,0:T(8,128)S(1)}, f32[64,64]{1,0:T(8,128)S(1)}) custom-call(s32[4]{0:T(128)S(1)} %pad_add_fusion.where_ref, bf16[32,8,1664]{2,1,0:T(8,128)(2,1)S(1)} %all-to-all-done.1.h_ref, bf16[51,64,128]{2,1,0:T(8,128)(2,1)S(1)} %get-tuple-element.16.keep_ref, ...), custom_call_target="tpu_custom_call" | custom-call | tf_op jit(solution)/shard_map/project/pallas_call | solution.py:440
  83.6 9.3 %all_to_all.16.parts_ref = f32[8,64,128]{2,1,0:T(8,128)S(1)} all-to-all(f32[8,64,128]{2,1,0:T(8,128)S(1)} %get-tuple-element.26), channel_id=1, replica_groups=mesh['y'=8,'core'=2,'gy'=4,'w'=4,'x'=4] {'core','x'}, dimensions={0} | all-to-all | bytes 524288 | tf_op jit(solution)/shard_map/all_to_all | solution.py:447
  93.0 26.5 %all-gather = f32[256,128]{1,0:T(8,128)S(1)} all-gather(f32[64,128]{1,0:T(8,128)S(1)} %sum.1), channel_id=2, replica_groups=mesh['y'=8,'core'=2,'gy'=4,'w'=4,'x'=4] {'w'}, dimensions={0}, use_global_device_ids=true | all-gather | bytes 163840 | tf_op jit(solution)/shard_map/all_gather | solution.py:449
  119.4 0.9 loadings.1
  (1 shorter events, 0.0 us)
Async XLA Ops:
  3.3 4.2 %collective-permute-start = (bf16[51,64,128]{2,1,0:T(8,128)(2,1)S(1)}, bf16[51,64,128]{2,1,0:T(8,128)(2,1)S(1)}, u32[]{:S(2)}, u32[]{:S(2)}) collective-permute-start(bf16[51,64,128]{2,1,0:T(8,128)(2,1)S(1)} %get-tuple-element.18), channel_id=1, source_target_pairs={{0,64},{64,0},{1,65},{65,1},{2,66},{66,2},{3,67},{67,3},{4,68},{68... | collective-permute-start | bytes 2506760 | tf_op jit(solution)/shard_map/ppermute | solution.py:411
  5.3 44.7 %copy-start = (f32[64,12544]{1,0:T(8,128)S(1)}, f32[64,12544]{1,0:T(8,128)}, u32[]{:S(2)}) copy-start(f32[64,12544]{1,0:T(8,128)} %comps_ref.1) | copy-start | bytes 9633796
  52.7 28.9 %all-to-all-start.1 = ((bf16[32,8,1664]{2,1,0:T(8,128)(2,1)}), bf16[32,8,1664]{2,1,0:T(8,128)(2,1)S(1)}, u32[]{:S(2)}, u32[]{:S(2)}) async-start(bf16[32,8,1664]{2,1,0:T(8,128)(2,1)} %get-tuple-element.21), calls=%async_computation.1 | async-start | bytes 1703936 | tf_op jit(solution)/shard_map/all_to_all | solution.py:435
  58.0 3.1 %collective-permute-start.1 = (f32[1,6272]{1,0:T(1,128)S(1)}, f32[1,6272]{1,0:T(1,128)S(1)}, u32[]{:S(2)}, u32[]{:S(2)}) collective-permute-start(f32[1,6272]{1,0:T(1,128)S(1)} %get-tuple-element.22), channel_id=1, source_target_pairs={{0,64},{64,0},{1,65},{65,1},{2,66},{66,2},{3,67},{67,3},{4,68},{68... | collective-permute-start | bytes 75272 | tf_op jit(solution)/shard_map/ppermute | solution.py:434

commit v8 on v7

--- a/solution.py
+++ b/solution.py
@@ -322,12 +322,25 @@
         partner = jnp.concatenate([got_ref[i] for i in group], axis=1)
         total = total + nt(jnp.concatenate([own, partner, h], axis=0), h)
     name = component_of(iota((comps, lane), 0))
-    to_low = jnp.where(iota((comps, lane), 1) == name, 1.0, 0.0)
-    to_high = jnp.where(iota((comps, lane), 1) == name + comps, 1.0, 0.0)
-    exact = dict(preferred_element_type=F32, precision=lax.Precision.HIGHEST)
-    spec = lax.dot_general(to_low, total[2 * tile :], (((0,), (0,)), ((), ())), **exact)[:comps]
-    spec = jnp.dot(spec, to_high, **exact)
-    cross = jnp.dot(total[: 2 * tile], to_low, **exact)
+    to_low = jnp.where(iota((comps, lane), 1) == name, 1.0, 0.0).astype(BF16)
+
+    def pieces(value):
+        high = value.astype(BF16)
+        rest = value - high.astype(F32)
+        mid = rest.astype(BF16)
+        return [high, mid, (rest - mid.astype(F32)).astype(BF16)]
+
+    rows = total.shape[0]
+    moved = jnp.dot(jnp.concatenate(pieces(total), axis=0), to_low, preferred_element_type=F32)
+    moved = moved[:rows] + moved[rows : 2 * rows] + moved[2 * rows :]
+    cross = moved[: 2 * tile]
+    spec = lax.dot_general(
+        to_low,
+        jnp.concatenate(pieces(moved[2 * tile :]), axis=1),
+        (((0,), (0,)), ((), ())),
+        preferred_element_type=F32,
+    )[:comps]
+    spec = pltpu.roll(spec[:, :lane] + spec[:, lane : 2 * lane] + spec[:, 2 * lane :], comps, 1)
     for to_core in range(2):
         both = spec + jnp.where(core == to_core, cross[:tile], cross[tile:])
         for i in range(copies // 2):

time: 120 us -> 120 us (level)
  no operation moved by 1% of the time
where the time goes in v8:
time: 120 us
  blocking collectives  75.5 us (63%)
  waiting for transfers between devices  22.2 us (18%)
  Pallas kernels  10.5 us (9%)
  starting transfers between devices  9.1 us (8%)
  between operations  1.35 us (1%)
    all_to_all x1, blocking collectives, local(): codes = lax.all_to_all(codes, peers, 0, 0, tiled=True)  40.2 us
    all_gather x1, blocking collectives, local(): both = lax.all_gather(both, 'w', axis=0)  26.1 us
    all_to_all x1, waiting for transfers between devices, local(): h_all = lax.all_to_all(h_all, peers, 0, 0, tiled=True)  19.5 us
    all_to_all x1, blocking collectives, local(): both = lax.all_to_all(both, ('core', 'x'), 0, 0, tiled=True)  9.33 us
    all_to_all x1, starting transfers between devices, local(): h_all = lax.all_to_all(h_all, peers, 0, 0, tiled=True)  5.26 us
    pallas_call x1, Pallas kernels, local(): call(spectra_kernel, 'spectra', [((chunks, DEPTH, width), BF16), ((1, hal...  2.73 us
  transfers between devices with their start and end apart: 3, of which 3 were waited for; matrix products, arithmetic and copies ran while one was open for 1% of the time, Pallas kernels for 1%

profile of v8, /device:TPU:8, one launch (start us, length us, event | category | flops | bytes accessed | tf_op | source)
XLA Modules:
  0.0 119.8 jit_solution(3929246570785835816)
XLA Ops:
  1.3 0.1 pad_add_fusion.where_ref
  1.4 2.3 %scatter.1 = (bf16[51,64,128]{2,1,0:T(8,128)(2,1)S(1)}, bf16[51,64,128]{2,1,0:T(8,128)(2,1)S(1)}, f32[64,64]{1,0:T(8,128)S(1)}) custom-call(s32[4]{0:T(128)S(1)} %pad_add_fusion.where_ref, s32[1]{0:T(128)} %bitcast.10.count_ref, s32[52]{0:T(128)} %bitcast.15, f32[64,64]{1,0:T(8,128)} %bitcast.14, bf16[8,52,8,128]{3,2,1,0:T(8,128)(2,1)} %bitcast.12), custom_call_target="tpu_custom_call" | custom-call | tf_op jit(solution)/shard_map/scatter/pallas_call | solution.py:413
  3.7 1.9 %collective-permute-start = (bf16[51,64,128]{2,1,0:T(8,128)(2,1)S(1)}, bf16[51,64,128]{2,1,0:T(8,128)(2,1)S(1)}, u32[]{:S(2)}, u32[]{:S(2)}) collective-permute-start(bf16[51,64,128]{2,1,0:T(8,128)(2,1)S(1)} %get-tuple-element.18), channel_id=1, source_target_pairs={{0,64},{64,0},{1,65},{65,1},{2,66},{66,2},{3,67},{67,3},{4,68},{68... | collective-permute-start | bytes 2506760 | tf_op jit(solution)/shard_map/ppermute | solution.py:424
  5.6 0.0 copy-start
  5.6 0.7 own.1.own_ref
  6.3 1.6 %collective-permute-done.got_ref = bf16[51,64,128]{2,1,0:T(8,128)(2,1)S(1)} collective-permute-done((bf16[51,64,128]{2,1,0:T(8,128)(2,1)S(1)}, bf16[51,64,128]{2,1,0:T(8,128)(2,1)S(1)}, u32[]{:S(2)}, u32[]{:S(2)}) %collective-permute-start) | collective-permute-done | bytes 835616 | tf_op jit(solution)/shard_map/ppermute | solution.py:424
  7.9 2.0 %numer.1 = (s16[32,8,1664]{2,1,0:T(8,128)(2,1)S(1)}, f32[16,64]{1,0:T(8,128)S(1)}) custom-call(s32[4]{0:T(128)S(1)} %pad_add_fusion.where_ref, f32[13,256,128]{2,1,0:T(8,128)S(1)} %own.1.own_ref, bf16[51,64,128]{2,1,0:T(8,128)(2,1)S(1)} %collective-permute-done.got_ref, f32[64,64]{1,0:T(8,128)S(1)} %get-tuple-element.17.w_ref), custom_call_target="tpu_custom_call" | custom-call | tf_op jit(solution)/shard_map/numer/pallas_call | solution.py:432
  9.9 40.2 %all_to_all.15.codes_ref = s16[32,8,1664]{2,1,0:T(8,128)(2,1)S(1)} all-to-all(s16[32,8,1664]{2,1,0:T(8,128)(2,1)S(1)} %get-tuple-element.19), channel_id=1, replica_groups=mesh['y'=8,'core'=2,'gy'=4,'w'=4,'x'=4] {'y','gy'}, dimensions={0} | all-to-all | bytes 1703936 | tf_op jit(solution)/shard_map/all_to_all | solution.py:439
  50.1 0.0 copy-done
  50.1 2.7 %spectra.1 = (bf16[32,8,1664]{2,1,0:T(8,128)(2,1)}, f32[1,6272]{1,0:T(1,128)S(1)}, f32[1,6272]{1,0:T(1,128)S(1)}, f32[24,64]{1,0:T(8,128)S(1)}) custom-call(s32[4]{0:T(128)S(1)} %pad_add_fusion.where_ref, s16[32,8,1664]{2,1,0:T(8,128)(2,1)S(1)} %all_to_all.15.codes_ref, f32[16,64]{1,0:T(8,128)S(1)} %get-tuple-element.20.edges_ref, f32[64,12544]{1,0:T(8,128)S(1)} %copy-done, ...), custom_call_target="tpu_custom_call" | custom-call | tf_op jit(solution)/shard_map/spectra/pallas_call | solution.py:440
  52.8 5.3 %all-to-all-start.1 = ((bf16[32,8,1664]{2,1,0:T(8,128)(2,1)}), bf16[32,8,1664]{2,1,0:T(8,128)(2,1)S(1)}, u32[]{:S(2)}, u32[]{:S(2)}) async-start(bf16[32,8,1664]{2,1,0:T(8,128)(2,1)} %get-tuple-element.21), calls=%async_computation.1 | async-start | bytes 1703936 | tf_op jit(solution)/shard_map/all_to_all | solution.py:448
  58.1 1.9 %collective-permute-start.1 = (f32[1,6272]{1,0:T(1,128)S(1)}, f32[1,6272]{1,0:T(1,128)S(1)}, u32[]{:S(2)}, u32[]{:S(2)}) collective-permute-start(f32[1,6272]{1,0:T(1,128)S(1)} %get-tuple-element.22), channel_id=1, source_target_pairs={{0,64},{64,0},{1,65},{65,1},{2,66},{66,2},{3,67},{67,3},{4,68},{68... | collective-permute-start | bytes 75272 | tf_op jit(solution)/shard_map/ppermute | solution.py:447
  60.0 1.2 collective-permute-done.1
  61.1 1.0 fusion.1
  62.2 19.5 %all-to-all-done.1.h_ref = bf16[32,8,1664]{2,1,0:T(8,128)(2,1)S(1)} async-done(((bf16[32,8,1664]{2,1,0:T(8,128)(2,1)}), bf16[32,8,1664]{2,1,0:T(8,128)(2,1)S(1)}, u32[]{:S(2)}, u32[]{:S(2)}) %all-to-all-start.1) | async-done | bytes 852000 | tf_op jit(solution)/shard_map/all_to_all | solution.py:448
  81.7 1.9 %project.1 = (f32[8,64,128]{2,1,0:T(8,128)S(1)}, f32[64,64]{1,0:T(8,128)S(1)}, f32[64,64]{1,0:T(8,128)S(1)}) custom-call(s32[4]{0:T(128)S(1)} %pad_add_fusion.where_ref, bf16[32,8,1664]{2,1,0:T(8,128)(2,1)S(1)} %all-to-all-done.1.h_ref, bf16[51,64,128]{2,1,0:T(8,128)(2,1)S(1)} %get-tuple-element.16.keep_ref, ...), custom_call_target="tpu_custom_call" | custom-call | tf_op jit(solution)/shard_map/project/pallas_call | solution.py:453
  83.5 9.3 %all_to_all.16.parts_ref = f32[8,64,128]{2,1,0:T(8,128)S(1)} all-to-all(f32[8,64,128]{2,1,0:T(8,128)S(1)} %get-tuple-element.26), channel_id=1, replica_groups=mesh['y'=8,'core'=2,'gy'=4,'w'=4,'x'=4] {'core','x'}, dimensions={0} | all-to-all | bytes 524288 | tf_op jit(solution)/shard_map/all_to_all | solution.py:460
  92.9 26.1 %all-gather = f32[256,128]{1,0:T(8,128)S(1)} all-gather(f32[64,128]{1,0:T(8,128)S(1)} %sum.1), channel_id=2, replica_groups=mesh['y'=8,'core'=2,'gy'=4,'w'=4,'x'=4] {'w'}, dimensions={0}, use_global_device_ids=true | all-gather | bytes 163840 | tf_op jit(solution)/shard_map/all_gather | solution.py:462
  118.9 0.9 loadings.1
  (1 shorter events, 0.0 us)
Async XLA Ops:
  3.7 4.2 %collective-permute-start = (bf16[51,64,128]{2,1,0:T(8,128)(2,1)S(1)}, bf16[51,64,128]{2,1,0:T(8,128)(2,1)S(1)}, u32[]{:S(2)}, u32[]{:S(2)}) collective-permute-start(bf16[51,64,128]{2,1,0:T(8,128)(2,1)S(1)} %get-tuple-element.18), channel_id=1, source_target_pairs={{0,64},{64,0},{1,65},{65,1},{2,66},{66,2},{3,67},{67,3},{4,68},{68... | collective-permute-start | bytes 2506760 | tf_op jit(solution)/shard_map/ppermute | solution.py:424
  5.6 44.5 %copy-start = (f32[64,12544]{1,0:T(8,128)S(1)}, f32[64,12544]{1,0:T(8,128)}, u32[]{:S(2)}) copy-start(f32[64,12544]{1,0:T(8,128)} %comps_ref.1) | copy-start | bytes 9633796
  52.8 28.9 %all-to-all-start.1 = ((bf16[32,8,1664]{2,1,0:T(8,128)(2,1)}), bf16[32,8,1664]{2,1,0:T(8,128)(2,1)S(1)}, u32[]{:S(2)}, u32[]{:S(2)}) async-start(bf16[32,8,1664]{2,1,0:T(8,128)(2,1)} %get-tuple-element.21), calls=%async_computation.1 | async-start | bytes 1703936 | tf_op jit(solution)/shard_map/all_to_all | solution.py:448
  58.1 3.1 %collective-permute-start.1 = (f32[1,6272]{1,0:T(1,128)S(1)}, f32[1,6272]{1,0:T(1,128)S(1)}, u32[]{:S(2)}, u32[]{:S(2)}) collective-permute-start(f32[1,6272]{1,0:T(1,128)S(1)} %get-tuple-element.22), channel_id=1, source_target_pairs={{0,64},{64,0},{1,65},{65,1},{2,66},{66,2},{3,67},{67,3},{4,68},{68... | collective-permute-start | bytes 75272 | tf_op jit(solution)/shard_map/ppermute | solution.py:447
